TPU v7x, 32 devices: a whole 2x2x4 slice. The times are simulated.
32 devices in a mesh: rep: 8 (over z, y), ep: 4 (over x, core).
Axes of the slice: x: 2, y: 2, z: 4, core: 2. Of those that a mesh axis runs over, the one named last changes fastest.
Arguments:
- tokens: bfloat16 [32768, 1024], P(('rep', 'ep')), may hold values from -6 to 6
- cotangent: bfloat16 [32768, 1024], P(('rep', 'ep')), may hold values from -6 to 6
- gain_attn: float32 [1024], replicated, may hold values from 0.5 to 1.5
- w_qkv: bfloat16 [1024, 3072], replicated, may hold values from -0.1875 to 0.1875
- w_out: bfloat16 [1024, 1024], replicated, may hold values from -0.75 to 0.75
- rel_table: float32 [32, 16], replicated, may hold values from -3 to 3
- gain_moe: float32 [1024], replicated, may hold values from 0.5 to 1.5
- w_router: bfloat16 [1024, 4], replicated, may hold values from -0.125 to 0.125
- w_gate: bfloat16 [4, 1024, 2816], P('ep'), may hold values from -0.1875 to 0.1875
- w_up: bfloat16 [4, 1024, 2816], P('ep'), may hold values from -0.1875 to 0.1875
- w_down: bfloat16 [4, 2816, 1024], P('ep'), may hold values from -0.109375 to 0.109375
- expert_ids: int32 [32768, 2], P(('rep', 'ep')), may hold values from 0 to 3, all different within a row
- priority: int32 [32, 2048], P(('rep', 'ep')), may hold values from 0 to 2047, each once within a row
- span_starts: int32 [32, 2], P(('rep', 'ep')), may hold values from 0 to 768, as said below
Outputs:
- block_out: bfloat16 [32768, 1024], P(('rep', 'ep'))
- grad_tokens: float32 [32768, 1024], P(('rep', 'ep'))
- grad_gain_attn: float32 [1024], replicated
- grad_w_qkv: float32 [1024, 3072], replicated
- grad_w_out: float32 [1024, 1024], replicated
- grad_rel_table: float32 [32, 16], replicated
- grad_gain_moe: float32 [1024], replicated
- grad_w_router: float32 [1024, 4], replicated
- grad_w_gate: float32 [4, 1024, 2816], P('ep', 'rep')
- grad_w_up: float32 [4, 1024, 2816], P('ep', 'rep')
- grad_w_down: float32 [4, 2816, 1024], P('ep', 'rep')
Inputs may be any that keep to these rules, and one draw needn't show every extreme that they name: `expert_ids`: each token names two different experts. `priority`: each row is a permutation of the 2048 pairs of one device. `span_starts`: the spans of a sequence rise, are disjoint and lie inside the sequence.
All inputs are finite; a program needn't handle non-finite values.
Results may differ from a plain program's by a relative error of at most 0.015.
Values may be sent and summed in bfloat16 or wider, within the bound.
A program may use at most 640 MiB of HBM per device.

v0:
```python
import jax
import jax.numpy as jnp
import numpy as np
from jax import lax
from jax.sharding import PartitionSpec as P

D = 1024
H = 16
HD = 64
BUCKETS = 32
MAXDIST = 128
SEQ = 1024
PIC = 256
QBLOCK = 512


EPSILON = 1e-06
NEGATIVE = -1e30


def bucket_index(length):
    offsets = np.arange(-(length - 1), length)
    half_count = BUCKETS // 2
    near_count = half_count // 2
    upper_part = (offsets > 0).astype(np.int64) * half_count
    distance = np.abs(offsets)
    ratio = np.log(np.maximum(distance, 1) / near_count) / np.log(MAXDIST / near_count)
    distant_bucket = np.minimum(
        near_count + np.floor(ratio * (half_count - near_count)).astype(np.int64), half_count - 1
    )
    return upper_part + np.where(distance < near_count, distance, distant_bucket)


def block_buckets(offset):
    bucket_all = bucket_index(SEQ)
    places = np.arange(SEQ)[None, :] - (offset + np.arange(QBLOCK))[:, None] + SEQ - 1
    return bucket_all[places].astype(np.int32)


def rms_forward(values, gain):
    scale_rows = lax.rsqrt(jnp.mean(values * values, axis=-1, keepdims=True) + EPSILON)
    return (values * scale_rows * gain, scale_rows)


def rms_backward(values, scale_rows, gain, upstream):
    scaled_grad = upstream * gain
    gain_grad = jnp.sum(upstream * values * scale_rows, axis=0)
    inner_mean = jnp.mean(scaled_grad * values, axis=-1, keepdims=True)
    return (scale_rows * scaled_grad - values * scale_rows**3 * inner_mean, gain_grad)


def permitted_mask(starts, first_row, rows, length):
    query_pos = first_row + jnp.arange(rows, dtype=jnp.int32)
    key_pos = jnp.arange(length, dtype=jnp.int32)
    causal = key_pos[None, :] <= query_pos[:, None]
    query_in = (query_pos[None, :] >= starts[:, None]) & (
        query_pos[None, :] < starts[:, None] + PIC
    )
    key_in = (key_pos[None, :] >= starts[:, None]) & (key_pos[None, :] < starts[:, None] + PIC)
    return causal | jnp.any(query_in[:, :, None] & key_in[:, None, :], axis=0)


def block_parts(block, queries, keys_all, every_value_rows, rel_heads, span_starts):
    first_row = block * QBLOCK
    sequence = first_row // SEQ
    offset = first_row - sequence * SEQ
    key_first = sequence * SEQ
    bucket_block = jnp.asarray(block_buckets(offset))
    block_bias_tile = jnp.take(rel_heads, bucket_block, axis=1)
    allowed = permitted_mask(span_starts[sequence], offset, QBLOCK, SEQ)
    return (
        first_row,
        key_first,
        bucket_block,
        queries[:, first_row : first_row + QBLOCK],
        keys_all,
        every_value_rows,
        block_bias_tile,
        allowed,
    )


def masked_scores(query_block, key_block, block_bias_tile, allowed):
    raw_scores = jnp.einsum(
        "hqd,hkd->hqk", query_block, key_block, preferred_element_type=jnp.float32
    )
    return jnp.where(allowed[None], raw_scores * HD ** (-0.5) + block_bias_tile, NEGATIVE)


def geglu(gate_pre, up_pre):
    return jax.nn.gelu(gate_pre, approximate=True) * up_pre


def expert_sums(received, gate_low, up_low, hidden, grad_recv):
    local_experts = received.shape[1]
    model_width = received.shape[3]
    hidden_width = hidden.shape[3]
    replicas = lax.axis_size("rep")
    joined_grads = jnp.concatenate([gate_low, up_low], axis=3)
    columns = received
    inner_sum = lax.psum_scatter(
        jnp.einsum("secd,secg->deg", columns, joined_grads, preferred_element_type=jnp.float32)
        .reshape(model_width // replicas * lax.axis_size("rep"), -1)
        .astype(jnp.bfloat16),
        "rep",
        scatter_dimension=0,
        tiled=True,
    ).astype(jnp.float32)
    columns = hidden
    outer_sum = lax.psum_scatter(
        jnp.einsum("secf,secd->fed", columns, grad_recv, preferred_element_type=jnp.float32)
        .reshape(hidden_width // replicas * lax.axis_size("rep"), -1)
        .astype(jnp.bfloat16),
        "rep",
        scatter_dimension=0,
        tiled=True,
    ).astype(jnp.float32)
    inner_sum = inner_sum.reshape(inner_sum.shape[0], local_experts, 2 * hidden_width)
    grad_w_gate = jnp.transpose(inner_sum[:, :, :hidden_width], (1, 0, 2))
    grad_w_up = jnp.transpose(inner_sum[:, :, hidden_width:], (1, 0, 2))
    grad_w_down = jnp.transpose(
        outer_sum.reshape(outer_sum.shape[0], local_experts, model_width), (1, 0, 2)
    )
    return (grad_w_gate, grad_w_up, grad_w_down)


def per_device(
    tokens,
    cotangent,
    gain_attn,
    w_qkv,
    w_out,
    rel_table,
    gain_moe,
    w_router,
    w_gate,
    w_up,
    w_down,
    expert_ids,
    priority,
    span_starts,
):
    tok_count = tokens.shape[0]
    experts = w_router.shape[1]
    local_experts = w_gate.shape[0]
    groups = lax.axis_size("ep")
    capacity = 5 * tok_count // (2 * experts)
    pair_count = 2 * tok_count
    score_scale = HD ** (-0.5)
    block_count = tok_count // QBLOCK
    rel_heads = jnp.transpose(rel_table)
    token_float = tokens.astype(jnp.float32)
    normed, scale_attn = rms_forward(token_float, gain_attn)
    normed_low = normed.astype(jnp.bfloat16)
    qkv = jnp.dot(normed_low, w_qkv, preferred_element_type=jnp.float32).astype(jnp.bfloat16)
    heads_major = jnp.transpose(qkv.reshape(tok_count, 3, H, HD), (1, 2, 0, 3))
    queries = heads_major[0]
    keys_all = heads_major[1]
    every_value_rows = heads_major[2]
    attended_list = []
    maxima_list = []
    totals_list = []
    for block in range(block_count):
        parts = block_parts(block, queries, keys_all, every_value_rows, rel_heads, span_starts)
        scores = masked_scores(parts[3], parts[4], parts[6], parts[7])
        maxima = jnp.max(scores, axis=-1, keepdims=True)
        expo = jnp.exp(scores - maxima)
        totals = jnp.sum(expo, axis=-1, keepdims=True)
        probs = (expo / totals).astype(jnp.bfloat16)
        attended_list.append(
            jnp.einsum("hqk,hkd->hqd", probs, parts[5], preferred_element_type=jnp.float32)
        )
        maxima_list.append(maxima)
        totals_list.append(totals)
    attended_heads = jnp.concatenate(attended_list, axis=1).astype(jnp.bfloat16)
    attended_low = jnp.transpose(attended_heads, (1, 0, 2)).reshape(tok_count, D)
    mixed = token_float + jnp.dot(attended_low, w_out, preferred_element_type=jnp.float32)
    routed, scale_moe = rms_forward(mixed, gain_moe)
    routed_low = routed.astype(jnp.bfloat16)
    logits = jnp.dot(routed_low, w_router, preferred_element_type=jnp.float32)
    choose = expert_ids[:, :, None] == jnp.arange(experts, dtype=jnp.int32)[None, None, :]
    chosen = jnp.sum(jnp.where(choose, logits[:, None, :], 0.0), axis=-1)
    gates = jax.nn.softmax(chosen, axis=-1)
    flat_ids = expert_ids.reshape(-1)
    ranks = priority.reshape(-1)
    onehot = choose.reshape(pair_count, experts)
    earlier = (ranks[:, None] < ranks[None, :]).astype(jnp.bfloat16)
    counts = jnp.einsum(
        "ap,ae->pe", earlier, onehot.astype(jnp.bfloat16), preferred_element_type=jnp.float32
    )
    slots = jnp.sum(jnp.where(onehot, counts, 0.0), axis=-1).astype(jnp.int32)
    target = jnp.where(slots < capacity, flat_ids * capacity + slots, experts * capacity)
    owner = jnp.full((experts * capacity,), pair_count, jnp.int32)
    owner = owner.at[target].set(jnp.arange(pair_count, dtype=jnp.int32), mode="drop")
    owner_token = owner // 2
    send_rows = jnp.take(routed_low, owner_token, axis=0, mode="fill", fill_value=0)
    send_rows = send_rows.reshape(groups, local_experts, capacity, D)
    piece = lax.all_to_all(send_rows, "ep", split_axis=0, concat_axis=0, tiled=True)
    gate_pre = jnp.einsum("secd,edf->secf", piece, w_gate, preferred_element_type=jnp.float32)
    up_pre = jnp.einsum("secd,edf->secf", piece, w_up, preferred_element_type=jnp.float32)
    hidden = geglu(gate_pre, up_pre).astype(jnp.bfloat16)
    result = jnp.einsum(
        "secf,efd->secd", hidden, w_down, preferred_element_type=jnp.float32
    ).astype(jnp.bfloat16)
    expert_results = (result, piece, gate_pre, up_pre, hidden)
    received = expert_results[1]
    returned = lax.all_to_all(
        expert_results[0], "ep", split_axis=0, concat_axis=0, tiled=True
    ).reshape(experts * capacity, D)
    pair_rows = jnp.take(returned, target, axis=0, mode="fill", fill_value=0).astype(jnp.float32)
    pair_rows = pair_rows.reshape(tok_count, 2, D)
    block_out = (mixed + jnp.sum(gates[:, :, None] * pair_rows, axis=1)).astype(jnp.bfloat16)
    grad_out = cotangent.astype(jnp.float32)
    grad_gates = jnp.sum(pair_rows * grad_out[:, None, :], axis=-1)
    gate_slots = jnp.take(gates.reshape(-1), owner, mode="fill", fill_value=0.0)
    grad_send = (
        jnp.take(grad_out, owner_token, axis=0, mode="fill", fill_value=0.0) * gate_slots[:, None]
    )
    grad_send = grad_send.astype(jnp.bfloat16).reshape(groups, local_experts, capacity, D)
    grad_recv = lax.all_to_all(grad_send, "ep", split_axis=0, concat_axis=0, tiled=True)
    grad_hidden = jnp.einsum(
        "secd,efd->secf", grad_recv, w_down, preferred_element_type=jnp.float32
    )
    gate_pre = expert_results[2]
    up_pre = expert_results[3]
    hidden = expert_results[4]
    unused, geglu_pull = jax.vjp(geglu, gate_pre, up_pre)
    gradient_gate_logits, grad_up_pre = geglu_pull(grad_hidden)
    gate_low = gradient_gate_logits.astype(jnp.bfloat16)
    up_low = grad_up_pre.astype(jnp.bfloat16)
    grad_rows = (
        jnp.einsum("secf,edf->secd", gate_low, w_gate, preferred_element_type=jnp.float32)
        + jnp.einsum("secf,edf->secd", up_low, w_up, preferred_element_type=jnp.float32)
    ).astype(jnp.bfloat16)
    grad_home = lax.all_to_all(grad_rows, "ep", split_axis=0, concat_axis=0, tiled=True).reshape(
        experts * capacity, D
    )
    grad_pairs = jnp.take(grad_home, target, axis=0, mode="fill", fill_value=0).astype(jnp.float32)
    grad_pairs = grad_pairs.reshape(tok_count, 2, D)
    grad_chosen = gates * (grad_gates - jnp.sum(gates * grad_gates, axis=-1, keepdims=True))
    grad_logits = jnp.sum(jnp.where(choose, grad_chosen[:, :, None], 0.0), axis=1).astype(
        jnp.bfloat16
    )
    grad_w_router = jnp.einsum(
        "td,te->de", routed_low, grad_logits, preferred_element_type=jnp.float32
    )
    grad_routed = jnp.sum(grad_pairs, axis=1) + jnp.einsum(
        "te,de->td", grad_logits, w_router, preferred_element_type=jnp.float32
    )
    grad_norm_moe, grad_gain_moe = rms_backward(mixed, scale_moe, gain_moe, grad_routed)
    grad_mixed = grad_out + grad_norm_moe
    grad_branch = grad_mixed.astype(jnp.bfloat16)
    grad_w_out = jnp.einsum(
        "td,te->de", attended_low, grad_branch, preferred_element_type=jnp.float32
    )
    grad_attended = jnp.einsum("te,de->td", grad_branch, w_out, preferred_element_type=jnp.float32)
    grad_attended = jnp.transpose(
        grad_attended.astype(jnp.bfloat16).reshape(tok_count, H, HD), (1, 0, 2)
    )
    grad_query_list = []
    grad_keys = jnp.zeros((H, tok_count, HD), jnp.float32)
    grad_values = jnp.zeros((H, tok_count, HD), jnp.float32)
    grad_rel_table = jnp.zeros((BUCKETS, H), jnp.float32)
    bucket_ids = jnp.arange(BUCKETS, dtype=jnp.int32)
    for block in range(block_count):
        parts = block_parts(block, queries, keys_all, every_value_rows, rel_heads, span_starts)
        first_row, key_first, bucket_block = (parts[0], parts[1], parts[2])
        scores = masked_scores(parts[3], parts[4], parts[6], parts[7])
        probs = jnp.exp(scores - maxima_list[block]) / totals_list[block]
        grad_block = grad_attended[:, first_row : first_row + QBLOCK]
        grad_probs = jnp.einsum(
            "hqd,hkd->hqk", grad_block, parts[5], preferred_element_type=jnp.float32
        )
        inner_sum = jnp.sum(probs * grad_probs, axis=-1, keepdims=True)
        gradient_score_matrix = (probs * (grad_probs - inner_sum)).astype(jnp.bfloat16)
        grad_query_list.append(
            jnp.einsum(
                "hqk,hkd->hqd", gradient_score_matrix, parts[4], preferred_element_type=jnp.float32
            )
            * score_scale
        )
        grad_keys = grad_keys.at[:, key_first : key_first + SEQ].add(
            jnp.einsum(
                "hqk,hqd->hkd", gradient_score_matrix, parts[3], preferred_element_type=jnp.float32
            )
            * score_scale
        )
        grad_values = grad_values.at[:, key_first : key_first + SEQ].add(
            jnp.einsum(
                "hqk,hqd->hkd",
                probs.astype(jnp.bfloat16),
                grad_block,
                preferred_element_type=jnp.float32,
            )
        )
        bucket_lookup_grid = (bucket_ids[:, None, None] == bucket_block[None]).astype(jnp.bfloat16)
        grad_rel_table = grad_rel_table + jnp.einsum(
            "clm,plm->pc",
            gradient_score_matrix,
            bucket_lookup_grid,
            preferred_element_type=jnp.float32,
        )
    grad_heads = jnp.stack(
        [jnp.concatenate(grad_query_list, axis=1), grad_keys, grad_values], axis=0
    ).astype(jnp.bfloat16)
    grad_qkv = jnp.transpose(grad_heads, (2, 0, 1, 3)).reshape(tok_count, 3 * D)
    grad_w_qkv = jnp.einsum("td,tf->df", normed_low, grad_qkv, preferred_element_type=jnp.float32)
    grad_normed = jnp.einsum("tf,df->td", grad_qkv, w_qkv, preferred_element_type=jnp.float32)
    grad_norm_attn, grad_gain_attn = rms_backward(token_float, scale_attn, gain_attn, grad_normed)
    grad_tokens = grad_mixed + grad_norm_attn
    grad_w_gate, grad_w_up, grad_w_down = expert_sums(received, gate_low, up_low, hidden, grad_recv)
    summed = lax.psum(
        (grad_w_qkv, grad_w_out, grad_rel_table, grad_w_router, grad_gain_attn, grad_gain_moe),
        ("rep", "ep"),
    )
    return (
        block_out,
        grad_tokens,
        summed[4],
        summed[0],
        summed[1],
        summed[2],
        summed[5],
        summed[3],
        grad_w_gate,
        grad_w_up,
        grad_w_down,
    )


def solution(mesh):
    placed = (
        P(("rep", "ep"), None),
        P(("rep", "ep"), None),
        P(),
        P(),
        P(),
        P(),
        P(),
        P(),
        P("ep", None, None),
        P("ep", None, None),
        P("ep", None, None),
        P(("rep", "ep"), None),
        P(("rep", "ep"), None),
        P(("rep", "ep"), None),
    )
    return jax.shard_map(
        per_device,
        mesh=mesh,
        in_specs=placed,
        out_specs=(
            P(("rep", "ep"), None),
            P(("rep", "ep"), None),
            P(),
            P(),
            P(),
            P(),
            P(),
            P(),
            P("ep", "rep", None),
            P("ep", "rep", None),
            P("ep", "rep", None),
        ),
        check_vma=False,
    )
```

profile of v0, /device:TPU:0, one launch (start us, length us, event | category | flops | bytes accessed | tf_op | source)
XLA Modules:
  0.0 5367.8 jit_solution(6524713804246528465)
XLA Ops:
  47.0 1897.5 %gather_fusion.3 = f32[524288,16]{1,0:T(8,128)} fusion(f32[16,32]{0,1:T(8,128)S(1)} %bitcast.294, s32[524288]{0:T(1024)} %broadcast_clamp_fusion.1), kind=kCustom, calls=%fused_computation.clone | custom fusion | bytes 69206016 | tf_op jit(solution)/shard_map/jit(_take)/gather | solution.py:69
  1944.5 143.1 %copy.145 = f32[512,1024,16]{1,0,2:T(8,128)} copy(f32[512,1024,16]{2,1,0:T(8,128)} %bitcast.7) | data formatting | bytes 67108864 | tf_op jit(solution)/shard_map/jit(_take)/gather | solution.py:69
  2090.4 26.5 fusion.165
  2139.5 1897.5 %gather_fusion.4 = f32[524288,16]{1,0:T(8,128)} fusion(f32[16,32]{0,1:T(8,128)S(1)} %bitcast.295, s32[524288]{0:T(1024)} %broadcast_clamp_fusion), kind=kCustom, calls=%fused_computation.2.clone | custom fusion | bytes 69206016 | tf_op jit(solution)/shard_map/jit(_take)/gather | solution.py:69
  4037.0 143.1 %copy.146 = f32[512,1024,16]{1,0,2:T(8,128)} copy(f32[512,1024,16]{2,1,0:T(8,128)} %bitcast.10) | data formatting | bytes 67108864 | tf_op jit(solution)/shard_map/jit(_take)/gather | solution.py:69
  4180.1 26.3 fusion.162
  4270.1 63.9 %all_to_all.20 = bf16[4,1,640,1024]{3,2,1,0:T(8,128)(2,1)S(1)} all-to-all(bf16[4,1,640,1024]{3,2,1,0:T(8,128)(2,1)S(1)} %broadcast_select_fusion), channel_id=1, replica_groups=mesh['rep'=8,'ep'=4] {'ep'}, dimensions={0} | all-to-all | bytes 10485760 | tf_op jit(solution)/shard_map/all_to_all | solution.py:198
  4334.0 23.1 fusion.47
  4533.6 55.9 %all-to-all-done.2 = bf16[4,1,640,1024]{3,2,1,0:T(8,128)(2,1)} async-done(((bf16[4,1,640,1024]{3,2,1,0:T(8,128)(2,1)}), bf16[4,1,640,1024]{3,2,1,0:T(8,128)(2,1)}, u32[]{:S(2)}, u32[]{:S(2)}) %all-to-all-start.2) | async-done | bytes 5242912 | tf_op jit(solution)/shard_map/all_to_all | solution.py:220
  4589.6 22.5 fusion.58
  4620.5 42.6 fusion.14
  4663.1 21.4 fusion.27
  4684.5 23.4 fusion.52
  4713.0 38.9 fusion.31
  4867.4 22.5 multiply_reduce_fusion
  4890.0 29.0 multiply_convert_fusion
  4928.5 22.6 multiply_reduce_fusion.1
  4951.1 27.7 multiply_convert_fusion.1
  4989.8 20.0 fusion.33
  5009.8 22.8 fusion.79
  5092.7 24.2 fusion.96
  5116.9 26.5 fusion.102
  5143.4 41.6 all-reduce
  5198.5 148.3 %all-reduce.4.cloned.1.call-done = (f32[1024,3072]{1,0:T(8,128)}, f32[1024,1024]{1,0:T(8,128)}) async-done(((f32[1024,3072]{1,0:T(8,128)}, f32[1024,1024]{1,0:T(8,128)}), (f32[1024,3072]{1,0:T(8,128)}, f32[1024,1024]{1,0:T(8,128)})) %all-reduce.4.cloned.1.call-update) | async-done | bytes 16777232 | tf_op jit(solution)/shard_map/psum | solution.py:312
  (270 shorter events, 540.0 us)
Async XLA Ops:
  8.0 4219.7 %copy-start = (bf16[1024,1024]{1,0:T(8,128)(2,1)S(1)}, bf16[1024,1024]{1,0:T(8,128)(2,1)}, u32[]{:S(2)}) copy-start(bf16[1024,1024]{1,0:T(8,128)(2,1)} %param.42) | copy-start | bytes 6291460
  8.0 35.0 copy-start.51
  43.8 1900.7 %copy-start.1 = (f32[32,16]{1,0:T(8,128)}, f32[32,16]{1,0:T(8,128)S(1)}, u32[]{:S(2)}) copy-start(f32[32,16]{1,0:T(8,128)S(1)} %copy.110) | copy-start | bytes 6148
  1944.5 143.1 %copy-start.57 = (pred[2,1024]{1,0:T(4,128)(4,1)S(1)}, pred[2,1024]{1,0:T(4,128)(4,1)}, u32[]{:S(2)}) copy-start(pred[2,1024]{1,0:T(4,128)(4,1)} %compare_and_fusion) | copy-start | bytes 6148
  1944.5 143.1 %copy-start.59 = (pred[2,512]{1,0:T(4,128)(4,1)S(1)}, pred[2,512]{1,0:T(4,128)(4,1)}, u32[]{:S(2)}) copy-start(pred[2,512]{1,0:T(4,128)(4,1)} %get-tuple-element.165) | copy-start | bytes 3076
  1944.5 143.1 %copy-start.60 = (pred[2,512]{1,0:T(4,128)(4,1)S(1)}, pred[2,512]{1,0:T(4,128)(4,1)}, u32[]{:S(2)}) copy-start(pred[2,512]{1,0:T(4,128)(4,1)} %get-tuple-element.166) | copy-start | bytes 3076
  1944.5 144.6 %copy-start.52 = (s32[512]{0:T(512)S(1)}, s32[512]{0:T(512)}, u32[]{:S(2)}) copy-start(s32[512]{0:T(512)} %copy-done.51) | copy-start | bytes 6148
  2090.4 26.5 copy-start.16
  4037.0 143.1 %copy-start.17 = (pred[512,1024]{1,0:T(8,128)(4,1)S(1)}, pred[512,1024]{1,0:T(8,128)(4,1)}, u32[]{:S(2)}) copy-start(pred[512,1024]{1,0:T(8,128)(4,1)} %get-tuple-element.180) | copy-start | bytes 1572868
  4240.6 25.9 copy-start.35
  4270.1 87.0 %slice-start.4 = ((s8[5767168]{0:T(1024)(128)(4,1)}), s8[4194304]{0:T(1024)(128)(4,1)S(1)}, s32[]{:S(2)}) async-start(s8[5767168]{0:T(1024)(128)(4,1)} %bitcast.321), calls=%async_computation.13 | async-start | bytes 8388608
  4334.0 66.8 %slice-start.2 = ((s8[5767168]{0:T(1024)(128)(4,1)}), s8[4194304]{0:T(1024)(128)(4,1)S(1)}, s32[]{:S(2)}) async-start(s8[5767168]{0:T(1024)(128)(4,1)} %bitcast.319), calls=%async_computation.11 | async-start | bytes 8388608
  4357.1 43.8 slice-start.3
  4418.5 64.7 %all-to-all-start.1 = ((bf16[4,1,640,1024]{3,2,1,0:T(8,128)(2,1)}), bf16[4,1,640,1024]{3,2,1,0:T(8,128)(2,1)}, u32[]{:S(2)}, u32[]{:S(2)}) async-start(bf16[4,1,640,1024]{3,2,1,0:T(8,128)(2,1)} %convert_bitcast_fusion), calls=%async_computation.1 | async-start | bytes 10485760 | tf_op jit(solution)/shard_map/all_to_all | solution.py:207
  4465.7 31.6 copy-start.49
  4465.7 31.6 copy-start.31
  4525.0 64.5 %all-to-all-start.2 = ((bf16[4,1,640,1024]{3,2,1,0:T(8,128)(2,1)}), bf16[4,1,640,1024]{3,2,1,0:T(8,128)(2,1)}, u32[]{:S(2)}, u32[]{:S(2)}) async-start(bf16[4,1,640,1024]{3,2,1,0:T(8,128)(2,1)} %multiply_convert_fusion.2), calls=%async_computation.2 | async-start | bytes 10485760 | tf_op jit(solution)/shard_map/all_to_all | solution.py:220
  4530.1 654.9 %reduce-scatter.9.cloned.1.call-start = ((), (), s32[]{:S(2)}) async-start(), calls=%async_computation.7 | async-start | bytes 6488064
  4707.9 64.5 %all-to-all-start.3 = ((bf16[4,1,640,1024]{3,2,1,0:T(8,128)(2,1)}), bf16[4,1,640,1024]{3,2,1,0:T(8,128)(2,1)}, u32[]{:S(2)}, u32[]{:S(2)}) async-start(bf16[4,1,640,1024]{3,2,1,0:T(8,128)(2,1)} %fusion.52), calls=%async_computation.3 | async-start | bytes 10485760 | tf_op jit(solution)/shard_map/all_to_all | solution.py:235
  4712.9 477.7 %reduce-scatter.7.cloned.1.call-start = ((), (), s32[]{:S(2)}) async-start(), calls=%async_computation.6 | async-start | bytes 12976128
  4766.7 580.1 %all-reduce.4.cloned.1.call-start = ((), (), s32[]{:S(2)}) async-start(), calls=%async_computation.8 | async-start | bytes 33554432 | tf_op jit(solution)/shard_map/psum | solution.py:312
  5092.7 24.2 copy-start.66
  5116.9 26.5 copy-start.41
  5116.9 26.5 copy-start.58
  (57 other events, 511.8 us)
Sparse Core Ops, SparseCore 0:
  4620.6 110.3 reduce-scatter.8
  4766.8 194.2 reduce-scatter.6
Sparse Core Ops, SparseCore 1:
  5068.5 278.2 all-reduce.3
where the time goes:
time: 5460 us; the launch traced here: 5370 us
  local copies, waits for them, and re-layouts  4310 us (79%)
  matrix products  534 us (10%)
  waiting for transfers between devices  227 us (4%)
  other arithmetic  161 us (3%)
  blocking collectives  105 us (2%)
    gather x4, local copies, waits for them, and re-layouts, block_parts(): block_bias_tile = jnp.take(rel_heads, bucket_block, axis=1)  4080 us
    psum x1, waiting for transfers between devices, per_device(): lax.psum((grad_w_qkv, grad_w_out, grad_rel_table, grad_w_router, grad_gai...  148 us
  transfers between devices with their start and end apart: 6, of which 4 were waited for; matrix products, arithmetic and copies ran while one was open for 11% of the time, Pallas kernels for 0%

commit v1 on v0

--- a/solution.py
+++ b/solution.py
@@ -3,6 +3,8 @@
 import numpy as np
 from jax import lax
 from jax.sharding import PartitionSpec as P
+from jax.experimental import pallas as pl
+from jax.experimental.pallas import tpu as pltpu
 
 D = 1024
 H = 16
@@ -11,15 +13,16 @@
 MAXDIST = 128
 SEQ = 1024
 PIC = 256
-QBLOCK = 512
-
-
 EPSILON = 1e-06
 NEGATIVE = -1e30
-
-
-def bucket_index(length):
-    offsets = np.arange(-(length - 1), length)
+LOG2E = 1.4426950408889634
+QB = 256
+KB = 128
+WIDE = 768
+VMEM_LIMIT = 56 * 1024 * 1024
+
+
+def bucket_of(offsets):
     half_count = BUCKETS // 2
     near_count = half_count // 2
     upper_part = (offsets > 0).astype(np.int64) * half_count
@@ -31,10 +34,265 @@
     return upper_part + np.where(distance < near_count, distance, distant_bucket)
 
 
-def block_buckets(offset):
-    bucket_all = bucket_index(SEQ)
-    places = np.arange(SEQ)[None, :] - (offset + np.arange(QBLOCK))[:, None] + SEQ - 1
-    return bucket_all[places].astype(np.int32)
+def wide_onehot():
+    places = np.arange(WIDE)
+    offsets = np.where(places < 640, 256 - places, 1024 - places)
+    return (bucket_of(offsets)[:, None] == np.arange(BUCKETS)[None, :]).astype(np.float32)
+
+
+def dot_nt(a, b):
+    return lax.dot_general(a, b, (((1,), (1,)), ((), ())), preferred_element_type=jnp.float32)
+
+
+def dot_nn(a, b):
+    return lax.dot_general(a, b, (((1,), (0,)), ((), ())), preferred_element_type=jnp.float32)
+
+
+def key_count(i):
+    return min((i + 2) * QB, SEQ)
+
+
+def fill_mask(span_ref, mask_s):
+    for i in range(SEQ // QB):
+        for d in range(4):
+            if 2 * i + d >= SEQ // KB:
+                continue
+            k = (2 * i + d) * KB + lax.broadcasted_iota(jnp.int32, (KB, QB), 0)
+            q = i * QB + lax.broadcasted_iota(jnp.int32, (KB, QB), 1)
+            ok = k <= q
+            for s in range(2):
+                start = span_ref[0, s]
+                ok = ok | ((k >= start) & (k < start + PIC) & (q >= start) & (q < start + PIC))
+            mask_s[4 * i + d] = jnp.where(ok, 0.0, NEGATIVE)
+
+
+def spread_bias(diag_ref, h, bias_s):
+    row = jnp.broadcast_to(diag_ref[0, h : h + 1, :], (KB, WIDE))
+    bias_s[h] = pltpu.roll(row, 0, 1, stride=1, stride_axis=0)
+
+
+def shifted(s, i, kt, h, bias_s, mask_s, low, high, row):
+    d = kt - 2 * i
+    if d <= -2:
+        return s + (low if row is None else low + row)
+    if d >= 3:
+        s = s + (high if row is None else high + row)
+    else:
+        s = s + bias_s[h, :, (2 - d) * 128 : (2 - d) * 128 + 256]
+        if row is not None:
+            s = s + row
+    if d >= 0:
+        s = s + mask_s[4 * i + d]
+    return s
+
+
+def diagonal_sums(x):
+    rows = x.shape[0]
+    while rows > 8:
+        rows //= 2
+        x = x[:rows] + pltpu.roll(x[rows:], WIDE - rows, 1)
+    total = x[0:1]
+    for r in range(1, rows):
+        total = total + pltpu.roll(x[r : r + 1], WIDE - r, 1)
+    return total
+
+
+def half_lanes(x, h):
+    lane = lax.broadcasted_iota(jnp.int32, x.shape, 1)
+    return jnp.where((lane < HD) if h == 0 else (lane >= HD), x, jnp.zeros_like(x))
+
+
+def attn_fwd_kernel(span_ref, q_ref, k_ref, v_ref, diag_ref, out_ref, lse_ref, mask_s, bias_s, vt_s, s_s, p_s):
+    @pl.when(pl.program_id(0) == 0)
+    def _():
+        fill_mask(span_ref, mask_s)
+
+    vt = jnp.transpose(v_ref[...])
+    for h in range(2):
+        spread_bias(diag_ref, h, bias_s)
+        vt_s[h, :HD] = vt[h * HD : (h + 1) * HD]
+        vt_s[h, HD:] = jnp.ones((16, SEQ), jnp.bfloat16)
+    scale = LOG2E * HD ** (-0.5)
+    for i in range(SEQ // QB):
+        nk = key_count(i)
+        outs = []
+        for h in range(2):
+            low = diag_ref[0, h : h + 1, 600:601]
+            high = diag_ref[0, h : h + 1, 0:1]
+            qs = half_lanes(q_ref[i * QB : (i + 1) * QB, :], h)
+            s_s[h, :nk] = dot_nt(k_ref[:nk, :], qs)
+            top = None
+            for kt in range(nk // KB):
+                s = shifted(s_s[h, kt * KB : (kt + 1) * KB] * scale, i, kt, h, bias_s, mask_s, low, high, None)
+                s_s[h, kt * KB : (kt + 1) * KB] = s
+                t = jnp.max(s.reshape(KB // 8, 8, QB), axis=0)
+                top = t if top is None else jnp.maximum(top, t)
+            m = jnp.max(top, axis=0, keepdims=True)
+            for kt in range(nk // KB):
+                p_s[h, kt * KB : (kt + 1) * KB] = jnp.exp2(s_s[h, kt * KB : (kt + 1) * KB] - m).astype(jnp.bfloat16)
+            ot = dot_nn(vt_s[h, :, :nk], p_s[h, :nk])
+            total = ot[HD : HD + 1]
+            outs.append(ot[:HD] / total)
+            lse_ref[0, h : h + 1, i * QB : (i + 1) * QB] = m + jnp.log2(total)
+        out_ref[i * QB : (i + 1) * QB, :] = jnp.transpose(jnp.concatenate(outs, axis=0)).astype(jnp.bfloat16)
+
+
+def attn_fwd(spans, qkv, diag):
+    col = lambda off: pl.BlockSpec((SEQ, 128), lambda g: (0, g + off))
+    return pl.pallas_call(
+        attn_fwd_kernel,
+        grid=(H // 2,),
+        in_specs=[
+            pl.BlockSpec(memory_space=pltpu.SMEM),
+            col(0),
+            col(8),
+            col(16),
+            pl.BlockSpec((1, 2, WIDE), lambda g: (g, 0, 0)),
+        ],
+        out_specs=[col(0), pl.BlockSpec((1, 2, SEQ), lambda g: (g, 0, 0))],
+        out_shape=[
+            jax.ShapeDtypeStruct((SEQ, D), jnp.bfloat16),
+            jax.ShapeDtypeStruct((H // 2, 2, SEQ), jnp.float32),
+        ],
+        scratch_shapes=[
+            pltpu.VMEM((16, KB, QB), jnp.float32),
+            pltpu.VMEM((2, KB, WIDE), jnp.float32),
+            pltpu.VMEM((2, HD + 16, SEQ), jnp.bfloat16),
+            pltpu.VMEM((2, SEQ, QB), jnp.float32),
+            pltpu.VMEM((2, SEQ, QB), jnp.bfloat16),
+        ],
+        compiler_params=pltpu.CompilerParams(vmem_limit_bytes=VMEM_LIMIT),
+        cost_estimate=pl.CostEstimate(flops=2 * 2 * 16 * 1024 * 1024 * 128, bytes_accessed=10 << 20, transcendentals=16 << 20),
+        name="attn_fwd",
+    )(spans, qkv, qkv, qkv, diag)
+
+
+def attn_bwd_kernel(
+    span_ref, q_ref, k_ref, v_ref, g_ref, o_ref, lse_ref, diag_ref,
+    out_ref, drel_ref, far_ref,
+    mask_s, bias_s, acc_s, kt_s, s_s, dp_s, p_s, ds_s, dk_s, dv_s, delta_s,
+):
+    part = pl.program_id(1)
+
+    @pl.when((pl.program_id(0) == 0) & (part == 0))
+    def _():
+        fill_mask(span_ref, mask_s)
+
+    @pl.when(part == 1)
+    def _():
+        out_ref[...] = (dk_s[...] * HD ** (-0.5)).astype(jnp.bfloat16)
+
+    @pl.when(part == 2)
+    def _():
+        out_ref[...] = dv_s[...].astype(jnp.bfloat16)
+
+    @pl.when(part == 0)
+    def _():
+        kt_s[...] = jnp.transpose(k_ref[...])
+        prod = jnp.transpose(g_ref[...].astype(jnp.float32) * o_ref[...].astype(jnp.float32))
+        for h in range(2):
+            spread_bias(diag_ref, h, bias_s)
+            delta_s[h : h + 1] = jnp.sum(prod[h * HD : (h + 1) * HD], axis=0, keepdims=True)
+        acc_s[...] = jnp.zeros_like(acc_s)
+        far_ref[...] = jnp.zeros_like(far_ref)
+        scale = LOG2E * HD ** (-0.5)
+        for i in reversed(range(SEQ // QB)):
+            nk = key_count(i)
+            rows = slice(i * QB, (i + 1) * QB)
+            dqs = []
+            for h in range(2):
+                low = diag_ref[0, h : h + 1, 600:601]
+                high = diag_ref[0, h : h + 1, 0:1]
+                qs = half_lanes(q_ref[rows, :], h)
+                gs = half_lanes(g_ref[rows, :], h)
+                s_s[h, :nk] = dot_nt(k_ref[:nk, :], qs)
+                dp_s[h, :nk] = dot_nt(v_ref[:nk, :], gs)
+                nlse = -lse_ref[0, h : h + 1, rows]
+                delta = delta_s[h : h + 1, rows]
+                for kt in range(nk // KB):
+                    tile = slice(kt * KB, (kt + 1) * KB)
+                    d = kt - 2 * i
+                    p = jnp.exp2(shifted(s_s[h, tile] * scale, i, kt, h, bias_s, mask_s, low, high, nlse))
+                    ds = p * (dp_s[h, tile] - delta)
+                    p_s[tile, h * QB : (h + 1) * QB] = p.astype(jnp.bfloat16)
+                    ds_s[tile, h * QB : (h + 1) * QB] = ds.astype(jnp.bfloat16)
+                    if -1 <= d <= 2:
+                        cols = slice((2 - d) * 128, (2 - d) * 128 + 256)
+                        acc_s[h, :, cols] += ds
+                    else:
+                        far_ref[0, h, 0 if d < 0 else 1] += jnp.sum(ds.reshape(KB // 8, 8, QB), axis=0)
+                dqs.append(dot_nn(kt_s[h * HD : (h + 1) * HD, :nk], ds_s[:nk, h * QB : (h + 1) * QB]))
+            out_ref[rows, :] = (jnp.transpose(jnp.concatenate(dqs, axis=0)) * HD ** (-0.5)).astype(jnp.bfloat16)
+            gg = jnp.concatenate([half_lanes(g_ref[rows, :], h) for h in range(2)], axis=0)
+            qq = jnp.concatenate([half_lanes(q_ref[rows, :], h) for h in range(2)], axis=0)
+            dv = dot_nn(p_s[:nk, :], gg)
+            dk = dot_nn(ds_s[:nk, :], qq)
+            if i == SEQ // QB - 1:
+                dv_s[...] = dv
+                dk_s[...] = dk
+            else:
+                dv_s[:nk] += dv
+                dk_s[:nk] += dk
+        for h in range(2):
+            drel_ref[0, h : h + 1, :] = diagonal_sums(acc_s[h])
+
+
+def attn_bwd(spans, qkv, grad_att, att, lse, diag):
+    col = lambda off: pl.BlockSpec((SEQ, 128), lambda g, p: (0, g + off))
+    one = lambda *dims: pl.BlockSpec((1, *dims), lambda g, p: (g,) + (0,) * len(dims))
+    return pl.pallas_call(
+        attn_bwd_kernel,
+        grid=(H // 2, 3),
+        in_specs=[
+            pl.BlockSpec(memory_space=pltpu.SMEM),
+            col(0),
+            col(8),
+            col(16),
+            col(0),
+            col(0),
+            one(2, SEQ),
+            one(2, WIDE),
+        ],
+        out_specs=[
+            pl.BlockSpec((SEQ, 128), lambda g, p: (0, p * 8 + g)),
+            one(2, WIDE),
+            one(2, 2, 8, QB),
+        ],
+        out_shape=[
+            jax.ShapeDtypeStruct((SEQ, 3 * D), jnp.bfloat16),
+            jax.ShapeDtypeStruct((H // 2, 2, WIDE), jnp.float32),
+            jax.ShapeDtypeStruct((H // 2, 2, 2, 8, QB), jnp.float32),
+        ],
+        scratch_shapes=[
+            pltpu.VMEM((16, KB, QB), jnp.float32),
+            pltpu.VMEM((2, KB, WIDE), jnp.float32),
+            pltpu.VMEM((2, KB, WIDE), jnp.float32),
+            pltpu.VMEM((128, SEQ), jnp.bfloat16),
+            pltpu.VMEM((2, SEQ, QB), jnp.float32),
+            pltpu.VMEM((2, SEQ, QB), jnp.float32),
+            pltpu.VMEM((SEQ, 2 * QB), jnp.bfloat16),
+            pltpu.VMEM((SEQ, 2 * QB), jnp.bfloat16),
+            pltpu.VMEM((SEQ, 128), jnp.float32),
+            pltpu.VMEM((SEQ, 128), jnp.float32),
+            pltpu.VMEM((2, SEQ), jnp.float32),
+        ],
+        compiler_params=pltpu.CompilerParams(vmem_limit_bytes=VMEM_LIMIT),
+        cost_estimate=pl.CostEstimate(flops=5 * 2 * 16 * 1024 * 1024 * 128, bytes_accessed=16 << 20, transcendentals=16 << 20),
+        name="attn_bwd",
+    )(spans, qkv, qkv, qkv, grad_att, att, lse, diag)
+
+
+def wide_diag(rel_table):
+    return jnp.einsum(
+        "mb,bh->hm", jnp.asarray(wide_onehot()), rel_table * LOG2E, precision=lax.Precision.HIGHEST
+    ).reshape(H // 2, 2, WIDE)
+
+
+def rel_grad(drel, far):
+    sums = drel.reshape(H, WIDE)
+    far = jnp.sum(far.reshape(H, 2, 8 * QB), axis=-1)
+    sums = sums.at[:, 600].add(far[:, 0]).at[:, 0].add(far[:, 1])
+    return jnp.einsum("mb,hm->bh", jnp.asarray(wide_onehot()), sums, precision=lax.Precision.HIGHEST)
 
 
 def rms_forward(values, gain):
@@ -47,44 +305,6 @@
     gain_grad = jnp.sum(upstream * values * scale_rows, axis=0)
     inner_mean = jnp.mean(scaled_grad * values, axis=-1, keepdims=True)
     return (scale_rows * scaled_grad - values * scale_rows**3 * inner_mean, gain_grad)
-
-
-def permitted_mask(starts, first_row, rows, length):
-    query_pos = first_row + jnp.arange(rows, dtype=jnp.int32)
-    key_pos = jnp.arange(length, dtype=jnp.int32)
-    causal = key_pos[None, :] <= query_pos[:, None]
-    query_in = (query_pos[None, :] >= starts[:, None]) & (
-        query_pos[None, :] < starts[:, None] + PIC
-    )
-    key_in = (key_pos[None, :] >= starts[:, None]) & (key_pos[None, :] < starts[:, None] + PIC)
-    return causal | jnp.any(query_in[:, :, None] & key_in[:, None, :], axis=0)
-
-
-def block_parts(block, queries, keys_all, every_value_rows, rel_heads, span_starts):
-    first_row = block * QBLOCK
-    sequence = first_row // SEQ
-    offset = first_row - sequence * SEQ
-    key_first = sequence * SEQ
-    bucket_block = jnp.asarray(block_buckets(offset))
-    block_bias_tile = jnp.take(rel_heads, bucket_block, axis=1)
-    allowed = permitted_mask(span_starts[sequence], offset, QBLOCK, SEQ)
-    return (
-        first_row,
-        key_first,
-        bucket_block,
-        queries[:, first_row : first_row + QBLOCK],
-        keys_all,
-        every_value_rows,
-        block_bias_tile,
-        allowed,
-    )
-
-
-def masked_scores(query_block, key_block, block_bias_tile, allowed):
-    raw_scores = jnp.einsum(
-        "hqd,hkd->hqk", query_block, key_block, preferred_element_type=jnp.float32
-    )
-    return jnp.where(allowed[None], raw_scores * HD ** (-0.5) + block_bias_tile, NEGATIVE)
 
 
 def geglu(gate_pre, up_pre):
@@ -146,34 +366,12 @@
     groups = lax.axis_size("ep")
     capacity = 5 * tok_count // (2 * experts)
     pair_count = 2 * tok_count
-    score_scale = HD ** (-0.5)
-    block_count = tok_count // QBLOCK
-    rel_heads = jnp.transpose(rel_table)
+    diag = wide_diag(rel_table)
     token_float = tokens.astype(jnp.float32)
     normed, scale_attn = rms_forward(token_float, gain_attn)
     normed_low = normed.astype(jnp.bfloat16)
     qkv = jnp.dot(normed_low, w_qkv, preferred_element_type=jnp.float32).astype(jnp.bfloat16)
-    heads_major = jnp.transpose(qkv.reshape(tok_count, 3, H, HD), (1, 2, 0, 3))
-    queries = heads_major[0]
-    keys_all = heads_major[1]
-    every_value_rows = heads_major[2]
-    attended_list = []
-    maxima_list = []
-    totals_list = []
-    for block in range(block_count):
-        parts = block_parts(block, queries, keys_all, every_value_rows, rel_heads, span_starts)
-        scores = masked_scores(parts[3], parts[4], parts[6], parts[7])
-        maxima = jnp.max(scores, axis=-1, keepdims=True)
-        expo = jnp.exp(scores - maxima)
-        totals = jnp.sum(expo, axis=-1, keepdims=True)
-        probs = (expo / totals).astype(jnp.bfloat16)
-        attended_list.append(
-            jnp.einsum("hqk,hkd->hqd", probs, parts[5], preferred_element_type=jnp.float32)
-        )
-        maxima_list.append(maxima)
-        totals_list.append(totals)
-    attended_heads = jnp.concatenate(attended_list, axis=1).astype(jnp.bfloat16)
-    attended_low = jnp.transpose(attended_heads, (1, 0, 2)).reshape(tok_count, D)
+    attended_low, lse = attn_fwd(span_starts, qkv, diag)
     mixed = token_float + jnp.dot(attended_low, w_out, preferred_element_type=jnp.float32)
     routed, scale_moe = rms_forward(mixed, gain_moe)
     routed_low = routed.astype(jnp.bfloat16)
@@ -254,65 +452,20 @@
         "td,te->de", attended_low, grad_branch, preferred_element_type=jnp.float32
     )
     grad_attended = jnp.einsum("te,de->td", grad_branch, w_out, preferred_element_type=jnp.float32)
-    grad_attended = jnp.transpose(
-        grad_attended.astype(jnp.bfloat16).reshape(tok_count, H, HD), (1, 0, 2)
-    )
-    grad_query_list = []
-    grad_keys = jnp.zeros((H, tok_count, HD), jnp.float32)
-    grad_values = jnp.zeros((H, tok_count, HD), jnp.float32)
-    grad_rel_table = jnp.zeros((BUCKETS, H), jnp.float32)
-    bucket_ids = jnp.arange(BUCKETS, dtype=jnp.int32)
-    for block in range(block_count):
-        parts = block_parts(block, queries, keys_all, every_value_rows, rel_heads, span_starts)
-        first_row, key_first, bucket_block = (parts[0], parts[1], parts[2])
-        scores = masked_scores(parts[3], parts[4], parts[6], parts[7])
-        probs = jnp.exp(scores - maxima_list[block]) / totals_list[block]
-        grad_block = grad_attended[:, first_row : first_row + QBLOCK]
-        grad_probs = jnp.einsum(
-            "hqd,hkd->hqk", grad_block, parts[5], preferred_element_type=jnp.float32
-        )
-        inner_sum = jnp.sum(probs * grad_probs, axis=-1, keepdims=True)
-        gradient_score_matrix = (probs * (grad_probs - inner_sum)).astype(jnp.bfloat16)
-        grad_query_list.append(
-            jnp.einsum(
-                "hqk,hkd->hqd", gradient_score_matrix, parts[4], preferred_element_type=jnp.float32
-            )
-            * score_scale
-        )
-        grad_keys = grad_keys.at[:, key_first : key_first + SEQ].add(
-            jnp.einsum(
-                "hqk,hqd->hkd", gradient_score_matrix, parts[3], preferred_element_type=jnp.float32
-            )
-            * score_scale
-        )
-        grad_values = grad_values.at[:, key_first : key_first + SEQ].add(
-            jnp.einsum(
-                "hqk,hqd->hkd",
-                probs.astype(jnp.bfloat16),
-                grad_block,
-                preferred_element_type=jnp.float32,
-            )
-        )
-        bucket_lookup_grid = (bucket_ids[:, None, None] == bucket_block[None]).astype(jnp.bfloat16)
-        grad_rel_table = grad_rel_table + jnp.einsum(
-            "clm,plm->pc",
-            gradient_score_matrix,
-            bucket_lookup_grid,
-            preferred_element_type=jnp.float32,
-        )
-    grad_heads = jnp.stack(
-        [jnp.concatenate(grad_query_list, axis=1), grad_keys, grad_values], axis=0
-    ).astype(jnp.bfloat16)
-    grad_qkv = jnp.transpose(grad_heads, (2, 0, 1, 3)).reshape(tok_count, 3 * D)
+    grad_qkv, drel, far = attn_bwd(
+        span_starts, qkv, grad_attended.astype(jnp.bfloat16), attended_low, lse, diag
+    )
+    grad_rel_table = rel_grad(drel, far)
     grad_w_qkv = jnp.einsum("td,tf->df", normed_low, grad_qkv, preferred_element_type=jnp.float32)
     grad_normed = jnp.einsum("tf,df->td", grad_qkv, w_qkv, preferred_element_type=jnp.float32)
     grad_norm_attn, grad_gain_attn = rms_backward(token_float, scale_attn, gain_attn, grad_normed)
     grad_tokens = grad_mixed + grad_norm_attn
     grad_w_gate, grad_w_up, grad_w_down = expert_sums(received, gate_low, up_low, hidden, grad_recv)
-    summed = lax.psum(
-        (grad_w_qkv, grad_w_out, grad_rel_table, grad_w_router, grad_gain_attn, grad_gain_moe),
-        ("rep", "ep"),
-    )
+    everyone = ("rep", "ep")
+    sum_w_out = lax.psum(grad_w_out.astype(jnp.bfloat16), everyone).astype(jnp.float32)
+    sum_w_qkv = lax.psum(grad_w_qkv.astype(jnp.bfloat16), everyone).astype(jnp.float32)
+    small = lax.psum((grad_rel_table, grad_w_router, grad_gain_attn, grad_gain_moe), everyone)
+    summed = (sum_w_qkv, sum_w_out) + tuple(small)
     return (
         block_out,
         grad_tokens,

time: 5460 us -> 1180 us (0.22); the launches traced: 5370 us -> 1170 us
  local copies, waits for them, and re-layouts: 4310 us -> 202 us
  matrix products: 534 us -> 272 us
  Pallas kernels: 0 us -> 102 us
  waiting for transfers between devices: 227 us -> 296 us
  blocking collectives: 105 us -> 170 us
  other arithmetic: 161 us -> 101 us
    gather x4 -> x0, local copies, waits for them, and re-layouts: 4080 us -> none  [block_parts(): block_bias_tile = jnp.take(rel_heads, bucket_block, axis=1)]
    dot_general x12 -> x2, matrix products: 215 us -> 2.18 us  [the longest x1 1.42 us: wide_diag(): jnp.einsum('mb,bh->hm', jnp.asarray(wide_onehot()), rel_table * LOG2E, pr...]
    pallas_call x0 -> x2, Pallas kernels: none -> 102 us  [the longest x1 61.9 us: attn_bwd(): pl.pallas_call(attn_bwd_kernel, grid=(H // 2, 3), in_specs=[pl.BlockSpec(...]
    unnamed x5, waiting for transfers between devices: 0.05 us -> 68.2 us
    all_to_all x0 -> x1, blocking collectives: none -> 63.4 us  [per_device(): lax.all_to_all(grad_send, 'ep', split_axis=0, concat_axis=0, tiled=True)]
    all_to_all x1 -> x0, waiting for transfers between devices: 55.9 us -> none  [per_device(): lax.all_to_all(grad_send, 'ep', split_axis=0, concat_axis=0, tiled=True)]
  transfers between devices with their start and end apart: 6 -> 5, of which waited for: 4 -> 4; matrix products, arithmetic and copies ran while one was open for 11% -> 15% of each run, Pallas kernels for 0% -> 0%
where the time goes in v1:
time: 1180 us; the launch traced here: 1170 us
  waiting for transfers between devices  296 us (25%)
  matrix products  272 us (23%)
  local copies, waits for them, and re-layouts  202 us (17%)
  blocking collectives  170 us (14%)
  Pallas kernels  102 us (9%)
  other arithmetic  101 us (9%)
  between operations  16.4 us (1%)
    psum x1, waiting for transfers between devices, per_device(): lax.psum(grad_w_qkv.astype(jnp.bfloat16), everyone).astype(jnp.float32)  151 us
    unnamed x5, waiting for transfers between devices  68.2 us
    all_to_all x1, blocking collectives, per_device(): lax.all_to_all(send_rows, 'ep', split_axis=0, concat_axis=0, tiled=True)  63.9 us
    all_to_all x1, blocking collectives, per_device(): lax.all_to_all(grad_send, 'ep', split_axis=0, concat_axis=0, tiled=True)  63.4 us
    pallas_call x1, Pallas kernels, attn_bwd(): pl.pallas_call(attn_bwd_kernel, grid=(H // 2, 3), in_specs=[pl.BlockSpec(...  61.9 us
    unnamed x108, local copies, waits for them, and re-layouts  60.9 us
    all_to_all x1, waiting for transfers between devices, per_device(): lax.all_to_all(grad_rows, 'ep', split_axis=0, concat_axis=0, tiled=True)  59.4 us
    dot_general x1, matrix products, per_device(): jnp.einsum('secd,efd->secf', grad_recv, w_down, preferred_element_type=jn...  42.5 us
  transfers between devices with their start and end apart: 5, of which 4 were waited for; matrix products, arithmetic and copies ran while one was open for 15% of the time, Pallas kernels for 0%

profile of v1, /device:TPU:0, one launch (start us, length us, event | category | flops | bytes accessed | tf_op | source)
XLA Modules:
  0.0 1169.6 jit_solution(15440393737902099946)
XLA Ops:
  44.0 39.9 %attn_fwd.1 = (bf16[1024,1024]{1,0:T(8,128)(2,1)}, f32[8,2,1024]{2,1,0:T(2,128)}) custom-call(s32[1,2]{1,0:T(1,128)} %span_ref.3, bf16[1024,3072]{1,0:T(8,128)(2,1)} %convolution_convert_fusion.1.q_ref.k_ref.v_ref, bf16[1024,3072]{1,0:T(8,128)(2,1)} %convolution_convert_fusion.1.q_ref.k_ref.v_ref, ...), custom_call_target="tpu_custom_call" | custom-call | flops 8589934592 | bytes 10485760 | tf_op jit(solution)/shard_map/attn_fwd/pallas_call | solution.py:142
  95.9 13.9 %gather_fusion = bf16[2560,1024]{1,0:T(8,128)(2,1)} fusion(bf16[1024,1024]{1,0:T(8,128)(2,1)} %copy.99, s32[3072]{0:T(1024)S(1)} %pad_clamp_fusion.1), kind=kCustom, calls=%fused_computation.2 | custom fusion | bytes 10496000 | tf_op jit(solution)/shard_map/jit(_take)/gather | solution.py:394
  113.4 63.9 %all_to_all.20 = bf16[4,1,640,1024]{3,2,1,0:T(8,128)(2,1)S(1)} all-to-all(bf16[4,1,640,1024]{3,2,1,0:T(8,128)(2,1)S(1)} %broadcast_select_fusion), channel_id=1, replica_groups=mesh['rep'=8,'ep'=4] {'ep'}, dimensions={0} | all-to-all | bytes 10485760 | tf_op jit(solution)/shard_map/all_to_all | solution.py:396
  177.3 23.1 %fusion.29 = f32[4,640,2816]{2,1,0:T(8,128)} fusion(bf16[1,1024,2816]{2,1,0:T(8,128)(2,1)} %param.31, bf16[4,1,640,1024]{3,2,1,0:T(8,128)(2,1)S(1)} %all_to_all.20), kind=kOutput, calls=%fused_computation.55 | convolution fusion | flops 14763950080 | bytes 39845888 | tf_op jit(solution)/shard_map/secd,edf->secf/dot_general | solution.py:398
  200.4 18.7 %fusion.32 = f32[4,640,2816]{2,1,0:T(8,128)} fusion(bf16[1,1024,2816]{2,1,0:T(8,128)(2,1)S(1)} %bitcast.192, bf16[4,1,640,1024]{3,2,1,0:T(8,128)(2,1)S(1)} %all_to_all.20), kind=kOutput, calls=%fused_computation.58 | convolution fusion | flops 14763950080 | bytes 39845888 | tf_op jit(solution)/shard_map/secd,edf->secf/dot_general | solution.py:397
  219.1 20.0 %fusion.16 = bf16[4,640,2816]{2,1,0:T(8,128)(2,1)S(1)} fusion(f32[4,640,2816]{2,1,0:T(8,128)} %fusion.29, f32[4,640,2816]{2,1,0:T(8,128)} %fusion.32), kind=kLoop, calls=%fused_computation.31 | loop fusion | flops 72089600 | bytes 72089600 | tf_op jit(solution)/shard_map/reshape.73
  244.1 17.4 %convert_bitcast_fusion = bf16[4,1,640,1024]{3,2,1,0:T(8,128)(2,1)} fusion(bf16[4,640,2816]{2,1,0:T(8,128)(2,1)S(1)} %fusion.16, bf16[1,2816,1024]{2,1,0:T(8,128)(2,1)S(1)} %bitcast.190), kind=kOutput, calls=%fused_computation.68 | convolution fusion | flops 14766571520 | bytes 25427968 | tf_op jit(solution)/shard_map/secf,efd->secd/dot_general | solution.py:400
  274.9 14.2 %gather_fusion.1 = f32[2560,1024]{1,0:T(8,128)} fusion(f32[1024,1024]{1,0:T(8,128)} %copy.104, s32[3072]{0:T(1024)S(1)} %pad_clamp_fusion.1), kind=kCustom, calls=%fused_computation.3 | custom fusion | bytes 20981760 | tf_op jit(solution)/shard_map/jit(_take)/gather | solution.py:415
  309.0 17.3 %all-to-all-done.1 = bf16[4,1,640,1024]{3,2,1,0:T(8,128)(2,1)} async-done(((bf16[4,1,640,1024]{3,2,1,0:T(8,128)(2,1)}), bf16[4,1,640,1024]{3,2,1,0:T(8,128)(2,1)}, u32[]{:S(2)}, u32[]{:S(2)}) %all-to-all-start.1) | async-done | bytes 5242912 | tf_op jit(solution)/shard_map/all_to_all | solution.py:405
  326.3 14.1 %gather_fusion.3 = bf16[2048,1024]{1,0:T(8,128)(2,1)} fusion(bf16[2560,1024]{1,0:T(8,128)(2,1)} %bitcast.25, s32[2048]{0:T(1024)S(1)} %broadcast_clamp_fusion), kind=kCustom, calls=%fused_computation.clone | custom fusion | bytes 8396800 | tf_op jit(solution)/shard_map/jit(_take)/gather | solution.py:408
  365.7 63.4 %all_to_all.21 = bf16[4,1,640,1024]{3,2,1,0:T(8,128)(2,1)} all-to-all(bf16[4,1,640,1024]{3,2,1,0:T(8,128)(2,1)S(1)} %multiply_convert_fusion), channel_id=1, replica_groups=mesh['rep'=8,'ep'=4] {'ep'}, dimensions={0} | all-to-all | bytes 10485760 | tf_op jit(solution)/shard_map/all_to_all | solution.py:418
  429.1 42.5 %fusion.6 = (bf16[4,1,640,2816]{3,2,0,1:T(8,128)(2,1)}, bf16[4,1,640,2816]{3,2,0,1:T(8,128)(2,1)}) fusion(f32[4,640,2816]{2,1,0:T(8,128)} %fusion.32, f32[4,640,2816]{2,1,0:T(8,128)} %fusion.29, bf16[1,2816,1024]{2,1,0:T(8,128)(2,1)} %param.32, bf16[4,1,640,1024]{3,2,1,0:T(8,128)(2,1)} %all_to_all.21), kind=kOutput, calls=%fused_computation.14 | convolution fusion | flops 14936965120 | bytes 97517568 | tf_op jit(solution)/shard_map/secd,efd->secf/dot_general | solution.py:419
  471.6 20.9 %fusion.17 = f32[4,640,1024]{2,1,0:T(8,128)} fusion(bf16[4,1,640,2816]{3,2,0,1:T(8,128)(2,1)} %get-tuple-element.105, bf16[1,1024,2816]{2,1,0:T(8,128)(2,1)} %param.31), kind=kOutput, calls=%fused_computation.32 | convolution fusion | flops 14763950080 | bytes 30670848 | tf_op jit(solution)/shard_map/secf,edf->secd/dot_general | solution.py:431
  492.6 23.2 %fusion.34 = bf16[4,1,640,1024]{3,2,1,0:T(8,128)(2,1)} fusion(f32[4,640,1024]{2,1,0:T(8,128)} %fusion.17, bf16[1,1024,2816]{2,1,0:T(8,128)(2,1)} %param.30, bf16[4,1,640,2816]{3,2,0,1:T(8,128)(2,1)} %get-tuple-element.104), kind=kOutput, calls=%fused_computation.62 | convolution fusion | flops 14769192960 | bytes 35913728 | tf_op jit(solution)/shard_map/secf,edf->secd/dot_general | solution.py:430
  521.1 59.4 %all-to-all-done.3 = bf16[4,1,640,1024]{3,2,1,0:T(8,128)(2,1)} async-done(((bf16[4,1,640,1024]{3,2,1,0:T(8,128)(2,1)}), bf16[4,1,640,1024]{3,2,1,0:T(8,128)(2,1)}, u32[]{:S(2)}, u32[]{:S(2)}) %all-to-all-start.3) | async-done | bytes 5242912 | tf_op jit(solution)/shard_map/all_to_all | solution.py:433
  580.4 14.4 %gather_fusion.4 = bf16[2048,1024]{1,0:T(8,128)(2,1)} fusion(bf16[2560,1024]{1,0:T(8,128)(2,1)} %bitcast.42, s32[2048]{0:T(1024)S(1)} %broadcast_clamp_fusion), kind=kCustom, calls=%fused_computation.1.clone | custom fusion | bytes 8396800 | tf_op jit(solution)/shard_map/jit(_take)/gather | solution.py:436
  650.4 13.8 %multiply_reduce_fusion.1 = f32[1024,1024]{1,0:T(8,128)} fusion(f32[1024,2,1024]{2,1,0:T(2,128)} %reshape.398, f32[1024,2]{1,0:T(8,128)S(1)} %copy-done.11), kind=kLoop, calls=%fused_computation.47 | loop fusion | flops 3145728 | bytes 12591104 | tf_op jit(solution)/shard_map/reduce_sum | solution.py:410
  685.0 61.9 %attn_bwd.1 = (bf16[1024,3072]{1,0:T(8,128)(2,1)}, f32[8,2,768]{2,1,0:T(2,128)}, f32[8,2,2,8,256]{4,3,2,1,0:T(8,128)}) custom-call(s32[1,2]{1,0:T(1,128)} %span_ref.3, bf16[1024,3072]{1,0:T(8,128)(2,1)} %convolution_convert_fusion.1.q_ref.k_ref.v_ref, bf16[1024,3072]{1,0:T(8,128)(2,1)} %convolution_convert_fusion.1.q_ref.k_ref.v_ref, ...), custom_call_target="tpu_custom_call" | custom-call | flops 21474836480 | bytes 16777216 | tf_op jit(solution)/shard_map/attn_bwd/pallas_call | solution.py:243
  759.1 22.4 %fusion.40 = bf16[2816,1024]{0,1:T(8,128)(2,1)} fusion(bf16[4,640,2816]{2,1,0:T(8,128)(2,1)} %copy-done.7, bf16[4,1,640,1024]{3,2,1,0:T(8,128)(2,1)} %all_to_all.21), kind=kOutput, calls=%fused_computation.70 | convolution fusion | flops 14766833664 | bytes 25427968 | tf_op jit(solution)/shard_map/secf,secd->fed/dot_general | solution.py:331
  790.0 38.9 %fusion.21 = bf16[1024,5632]{0,1:T(8,128)(2,1)} fusion(bf16[4,1,640,2816]{3,2,0,1:T(8,128)(2,1)} %get-tuple-element.105, bf16[4,1,640,2816]{3,2,0,1:T(8,128)(2,1)} %get-tuple-element.104, bf16[4,1,640,1024]{3,2,1,0:T(8,128)(2,1)} %copy-done.9), kind=kOutput, calls=%fused_computation.39 | convolution fusion | flops 29591339008 | bytes 45613056 | tf_op jit(solution)/shard_map/secd,secg->deg/dot_general | solution.py:322
  828.9 16.1 %copy.130 = bf16[1024,5632]{1,0:T(8,128)(2,1)} copy(bf16[1024,5632]{0,1:T(8,128)(2,1)} %fusion.21) | data formatting | bytes 23068672
  876.0 42.3 %all-reduce = (f32[1024]{0:T(1024)}, f32[32,16]{0,1:T(8,128)}, f32[1024]{0:T(1024)}, f32[1024,4]{0,1:T(4,128)}) all-reduce(f32[1024]{0:T(1024)S(1)} %get-tuple-element.92, f32[32,16]{0,1:T(8,128)S(1)} %fusion.86, f32[1024]{0:T(1024)S(1)} %copy-done.39, f32[1024,4]{0,1:T(4,128)S(1)} %fusion.87), channel_id=1, replica_groups=mesh['rep'=8,'ep'=4] {'rep','ep'}, use_global_device_ids=true, to_apply=%region_15.17 | all-reduce | flops 6656 | bytes 53248 | tf_op jit(solution)/shard_map/psum | solution.py:467
  918.3 151.3 %all-reduce.4.cloned.1.call-done = (bf16[1024,3072]{1,0:T(8,128)(2,1)}, bf16[1024,1024]{1,0:T(8,128)(2,1)}) async-done(((bf16[1024,3072]{1,0:T(8,128)(2,1)}, bf16[1024,1024]{1,0:T(8,128)(2,1)}), (bf16[1024,3072]{1,0:T(8,128)(2,1)}, bf16[1024,1024]{1,0:T(8,128)(2,1)})) %all-reduce.4.cloned.1.call-update) | async-done | bytes 8388624 | tf_op jit(solution)/shard_map/psum | solution.py:466
  1086.1 68.1 %reduce-scatter.7.cloned.1.call-done = bf16[128,5632]{1,0:T(8,128)(2,1)} async-done(((bf16[1024,5632]{1,0:T(8,128)(2,1)}), bf16[128,5632]{1,0:T(8,128)(2,1)}) %reduce-scatter.7.cloned.1.call-update) | async-done | bytes 1441808
  (195 shorter events, 272.1 us)
Async XLA Ops:
  8.0 76.0 %copy-start = (bf16[1024,1024]{1,0:T(8,128)(2,1)S(1)}, bf16[1024,1024]{1,0:T(8,128)(2,1)}, u32[]{:S(2)}) copy-start(bf16[1024,1024]{1,0:T(8,128)(2,1)} %param.26) | copy-start | bytes 6291460
  12.7 18.7 %copy-start.20 = (s32[2048]{0:T(1024)}, s32[2048]{0:T(1024)S(1)}, u32[]{:S(2)}) copy-start(s32[2048]{0:T(1024)S(1)} %eq.25) | copy-start | bytes 24580
  12.7 19.3 %copy-start.40 = (f32[1024]{0:T(1024)S(1)}, f32[1024]{0:T(1024)}, u32[]{:S(2)}) copy-start(f32[1024]{0:T(1024)} %param.24) | copy-start | bytes 12292
  25.3 18.7 %copy-start.14 = (s32[2560]{0:T(1024)}, s32[2560]{0:T(1024)S(1)}, u32[]{:S(2)}) copy-start(s32[2560]{0:T(1024)S(1)} %scatter_custom_fusion) | copy-start | bytes 30724
  25.4 84.5 %copy-start.31 = (pred[4,640]{1,0:T(4,128)(4,1)}, pred[4,640]{1,0:T(4,128)(4,1)S(1)}, u32[]{:S(2)}) copy-start(pred[4,640]{1,0:T(4,128)(4,1)S(1)} %broadcast_in_dim.98) | copy-start | bytes 7684
  44.0 40.0 %copy-start.2 = (bf16[1024,1024]{0,1:T(8,128)(2,1)S(1)}, bf16[1024,1024]{0,1:T(8,128)(2,1)}, u32[]{:S(2)}) copy-start(bf16[1024,1024]{0,1:T(8,128)(2,1)} %copy.95) | copy-start | bytes 6291460
  113.4 87.0 %slice-start.2 = ((s8[5767168]{0:T(1024)(128)(4,1)}), s8[4194304]{0:T(1024)(128)(4,1)S(1)}, s32[]{:S(2)}) async-start(s8[5767168]{0:T(1024)(128)(4,1)} %bitcast.191), calls=%async_computation.11 | async-start | bytes 8388608
  177.3 23.1 %copy-start.9 = (bf16[4,1,640,1024]{3,2,1,0:T(8,128)(2,1)}, bf16[4,1,640,1024]{3,2,1,0:T(8,128)(2,1)S(1)}, u32[]{:S(2)}) copy-start(bf16[4,1,640,1024]{3,2,1,0:T(8,128)(2,1)S(1)} %all_to_all.20) | copy-start | bytes 15728644
  177.3 23.1 %slice-start.3 = ((s8[5767168]{0:T(1024)(128)(4,1)}), s8[1572864]{0:T(1024)(128)(4,1)S(1)}, s32[]{:S(2)}) async-start(s8[5767168]{0:T(1024)(128)(4,1)} %bitcast.191), calls=%async_computation.12 | async-start | bytes 3145728
  177.3 66.9 %slice-start = ((s8[5767168]{0:T(1024)(128)(4,1)}), s8[4194304]{0:T(1024)(128)(4,1)S(1)}, s32[]{:S(2)}) async-start(s8[5767168]{0:T(1024)(128)(4,1)} %bitcast.189), calls=%async_computation.9 | async-start | bytes 8388608
  200.4 43.8 %slice-start.1 = ((s8[5767168]{0:T(1024)(128)(4,1)}), s8[1572864]{0:T(1024)(128)(4,1)S(1)}, s32[]{:S(2)}) async-start(s8[5767168]{0:T(1024)(128)(4,1)} %bitcast.189), calls=%async_computation.10 | async-start | bytes 3145728
  261.5 64.8 %all-to-all-start.1 = ((bf16[4,1,640,1024]{3,2,1,0:T(8,128)(2,1)}), bf16[4,1,640,1024]{3,2,1,0:T(8,128)(2,1)}, u32[]{:S(2)}, u32[]{:S(2)}) async-start(bf16[4,1,640,1024]{3,2,1,0:T(8,128)(2,1)} %convert_bitcast_fusion), calls=%async_computation.1 | async-start | bytes 10485760 | tf_op jit(solution)/shard_map/all_to_all | solution.py:405
  309.0 31.4 %copy-start.33 = (pred[2048]{0:T(1024)(128)(4,1)}, pred[2048]{0:T(1024)(128)(4,1)S(1)}, u32[]{:S(2)}) copy-start(pred[2048]{0:T(1024)(128)(4,1)S(1)} %compare_and_fusion.1) | copy-start | bytes 6148
  346.8 13.9 %copy-start.10 = (f32[1024,2]{1,0:T(8,128)}, f32[1024,2]{1,0:T(8,128)S(1)}, u32[]{:S(2)}) copy-start(f32[1024,2]{1,0:T(8,128)S(1)} %copy.96) | copy-start | bytes 24580
  347.1 13.7 %copy-start.32 = (pred[4,640]{1,0:T(4,128)(4,1)S(1)}, pred[4,640]{1,0:T(4,128)(4,1)}, u32[]{:S(2)}) copy-start(pred[4,640]{1,0:T(4,128)(4,1)} %copy-done.31) | copy-start | bytes 7684
  515.8 64.7 %all-to-all-start.3 = ((bf16[4,1,640,1024]{3,2,1,0:T(8,128)(2,1)}), bf16[4,1,640,1024]{3,2,1,0:T(8,128)(2,1)}, u32[]{:S(2)}, u32[]{:S(2)}) async-start(bf16[4,1,640,1024]{3,2,1,0:T(8,128)(2,1)} %fusion.34), calls=%async_computation.3 | async-start | bytes 10485760 | tf_op jit(solution)/shard_map/all_to_all | solution.py:433
  521.0 548.6 %all-reduce.4.cloned.1.call-start = ((), (), s32[]{:S(2)}) async-start(), calls=%async_computation.8 | async-start | bytes 16777216 | tf_op jit(solution)/shard_map/psum | solution.py:466
  521.1 111.4 %copy-start.18 = (bf16[1024,4]{0,1:T(4,128)(2,1)}, bf16[1024,4]{0,1:T(4,128)(2,1)S(1)}, u32[]{:S(2)}) copy-start(bf16[1024,4]{0,1:T(4,128)(2,1)S(1)} %select_reduce_fusion) | copy-start | bytes 24580
  580.4 14.4 %copy-start.34 = (pred[2048]{0:T(1024)(128)(4,1)S(1)}, pred[2048]{0:T(1024)(128)(4,1)}, u32[]{:S(2)}) copy-start(pred[2048]{0:T(1024)(128)(4,1)} %copy-done.33) | copy-start | bytes 6148
  684.9 62.0 %copy-start.3 = (bf16[1024,1024]{0,1:T(8,128)(2,1)S(1)}, bf16[1024,1024]{0,1:T(8,128)(2,1)}, u32[]{:S(2)}) copy-start(bf16[1024,1024]{0,1:T(8,128)(2,1)} %copy.95) | copy-start | bytes 6291460
  684.9 62.0 %copy-start.37 = (f32[1024]{0:T(1024)S(1)}, f32[1024]{0:T(1024)}, u32[]{:S(2)}) copy-start(f32[1024]{0:T(1024)} %copy-done.36) | copy-start | bytes 12292
  684.9 62.0 %copy-start.41 = (f32[1024]{0:T(1024)S(1)}, f32[1024]{0:T(1024)}, u32[]{:S(2)}) copy-start(f32[1024]{0:T(1024)} %param.24) | copy-start | bytes 12292
  759.1 321.2 %reduce-scatter.9.cloned.1.call-start = ((), (), s32[]{:S(2)}) async-start(), calls=%async_computation.7 | async-start | bytes 6488064
  790.0 364.2 %reduce-scatter.7.cloned.1.call-start = ((), (), s32[]{:S(2)}) async-start(), calls=%async_computation.6 | async-start | bytes 12976128
  (28 other events, 208.6 us)
Sparse Core Ops, SparseCore 0:
  759.2 310.3 all-reduce.3
Sparse Core Ops, SparseCore 1:
  790.1 135.8 reduce-scatter.8
  929.4 224.7 reduce-scatter.6

commit v2 on v1

--- a/solution.py
+++ b/solution.py
@@ -1,3 +1,4 @@
+from functools import partial
 import jax
 import jax.numpy as jnp
 import numpy as np
@@ -20,6 +21,7 @@
 KB = 128
 WIDE = 768
 VMEM_LIMIT = 56 * 1024 * 1024
+LIGHT = pl.CostEstimate(flops=1000, bytes_accessed=1000, transcendentals=0)
 
 
 def bucket_of(offsets):
@@ -162,7 +164,7 @@
             pltpu.VMEM((2, SEQ, QB), jnp.bfloat16),
         ],
         compiler_params=pltpu.CompilerParams(vmem_limit_bytes=VMEM_LIMIT),
-        cost_estimate=pl.CostEstimate(flops=2 * 2 * 16 * 1024 * 1024 * 128, bytes_accessed=10 << 20, transcendentals=16 << 20),
+        cost_estimate=LIGHT,
         name="attn_fwd",
     )(spans, qkv, qkv, qkv, diag)
 
@@ -237,12 +239,15 @@
             drel_ref[0, h : h + 1, :] = diagonal_sums(acc_s[h])
 
 
-def attn_bwd(spans, qkv, grad_att, att, lse, diag):
-    col = lambda off: pl.BlockSpec((SEQ, 128), lambda g, p: (0, g + off))
-    one = lambda *dims: pl.BlockSpec((1, *dims), lambda g, p: (g,) + (0,) * len(dims))
+def attn_bwd(spans, qkv, grad_att, att, lse, diag, half):
+    pairs = H // 4
+    base = half * pairs
+    col = lambda off: pl.BlockSpec((SEQ, 128), lambda g, p: (0, base + g + off))
+    one = lambda *dims: pl.BlockSpec((1, *dims), lambda g, p: (base + g,) + (0,) * len(dims))
+    new = lambda *dims: pl.BlockSpec((1, *dims), lambda g, p: (g,) + (0,) * len(dims))
     return pl.pallas_call(
         attn_bwd_kernel,
-        grid=(H // 2, 3),
+        grid=(pairs, 3),
         in_specs=[
             pl.BlockSpec(memory_space=pltpu.SMEM),
             col(0),
@@ -254,14 +259,14 @@
             one(2, WIDE),
         ],
         out_specs=[
-            pl.BlockSpec((SEQ, 128), lambda g, p: (0, p * 8 + g)),
-            one(2, WIDE),
-            one(2, 2, 8, QB),
+            pl.BlockSpec((SEQ, 128), lambda g, p: (0, p * pairs + g)),
+            new(2, WIDE),
+            new(2, 2, 8, QB),
         ],
         out_shape=[
-            jax.ShapeDtypeStruct((SEQ, 3 * D), jnp.bfloat16),
-            jax.ShapeDtypeStruct((H // 2, 2, WIDE), jnp.float32),
-            jax.ShapeDtypeStruct((H // 2, 2, 2, 8, QB), jnp.float32),
+            jax.ShapeDtypeStruct((SEQ, 3 * D // 2), jnp.bfloat16),
+            jax.ShapeDtypeStruct((pairs, 2, WIDE), jnp.float32),
+            jax.ShapeDtypeStruct((pairs, 2, 2, 8, QB), jnp.float32),
         ],
         scratch_shapes=[
             pltpu.VMEM((16, KB, QB), jnp.float32),
@@ -277,8 +282,8 @@
             pltpu.VMEM((2, SEQ), jnp.float32),
         ],
         compiler_params=pltpu.CompilerParams(vmem_limit_bytes=VMEM_LIMIT),
-        cost_estimate=pl.CostEstimate(flops=5 * 2 * 16 * 1024 * 1024 * 128, bytes_accessed=16 << 20, transcendentals=16 << 20),
-        name="attn_bwd",
+        cost_estimate=LIGHT,
+        name=f"attn_bwd_{half}",
     )(spans, qkv, qkv, qkv, grad_att, att, lse, diag)
 
 
@@ -295,6 +300,319 @@
     return jnp.einsum("mb,hm->bh", jnp.asarray(wide_onehot()), sums, precision=lax.Precision.HIGHEST)
 
 
+FT = 256
+
+
+def dot_tn(a, b):
+    return lax.dot_general(a, b, (((0,), (0,)), ((), ())), preferred_element_type=jnp.float32)
+
+
+VMEM_MOST = 58 * 1024 * 1024
+PARTS = 2
+
+
+def slot_onehot(meta_ref, n, rows):
+    slot = meta_ref[n, 0:1]
+    return lax.broadcasted_iota(jnp.int32, (rows, slot.shape[1]), 0) == slot
+
+
+def expert_fwd_kernel(meta_ref, wr_ref, tok_a, tok_b, cot_a, cot_b, gate_ref, up_ref, down_ref, *rest):
+    x_ref, gc_ref, hid_ref, slope_ref, act_ref, p_a, p_b, gg_ref, hot_s, turned_s, hid_s, gate_s = rest[-12:]
+    step = pl.program_id(0)
+    wide = hid_s.shape[1] // FT
+    deep = D // FT
+    rows = x_ref.shape[0] // 2
+    count = tok_a.shape[0]
+    pair = [(0, tok_a, cot_a, slice(0, rows)), (1, tok_b, cot_b, slice(rows, 2 * rows))]
+    chunk = 2 * rows // PARTS
+
+    @pl.when(step == 0)
+    def _():
+        for n, tok_ref, cot_ref, here in pair:
+            logits = dot_nt(wr_ref[...], tok_ref[...])
+            other, own = meta_ref[n, 1:2], meta_ref[n, 2:3]
+            names = lax.broadcasted_iota(jnp.int32, logits.shape, 0)
+            mine = jnp.sum(jnp.where(names == own, logits, 0.0), axis=0, keepdims=True)
+            theirs = jnp.sum(jnp.where(names == other, logits, 0.0), axis=0, keepdims=True)
+            gate = 1.0 / (1.0 + jnp.exp(theirs - mine))
+            hot = slot_onehot(meta_ref, n, rows)
+            gates = jnp.sum(jnp.where(hot, gate, 0.0), axis=1, keepdims=True)
+            lane = lax.broadcasted_iota(jnp.int32, (rows, 128), 1)
+            gate_s[here] = jnp.where(lane < 64, gates, 0.0)
+            hot = jnp.where(hot, 1.0, 0.0).astype(jnp.bfloat16)
+            hot_s[n] = hot
+            turned_s[n] = jnp.transpose(hot)
+            x_ref[here] = dot_nn(hot_s[n], tok_ref[...]).astype(jnp.bfloat16)
+
+    @pl.when(step < wide)
+    def _():
+        cols = pl.ds(pl.multiple_of(step * FT, FT), FT)
+        root = (2.0 / np.pi) ** 0.5
+        for c in range(PARTS):
+            here = slice(c * chunk, (c + 1) * chunk)
+            g = dot_nn(x_ref[here], gate_ref[0])
+            u = dot_nn(x_ref[here], up_ref[0])
+            square = g * g
+            t = jnp.tanh(g * (root + (root * 0.044715) * square))
+            half = 0.5 + 0.5 * t
+            act = g * half
+            slope = half + (act * (1.0 - t)) * (root + (3.0 * root * 0.044715) * square)
+            slope_ref[here] = (u * slope).astype(jnp.bfloat16)
+            act_ref[here] = act.astype(jnp.bfloat16)
+            hidden = (act * u).astype(jnp.bfloat16)
+            hid_s[here, cols] = hidden
+            hid_ref[here] = hidden
+
+    for n in range(deep):
+
+        @pl.when(step == wide + n)
+        def _():
+            cols = slice(n * FT, (n + 1) * FT)
+            outs = dot_nn(hid_s[...], down_ref[0])
+            for s, tok_ref, cot_ref, here in pair:
+                gates = gate_s[here, 0:1]
+                out = outs[here].astype(jnp.bfloat16).astype(jnp.float32)
+                cot = dot_nn(hot_s[s], cot_ref[...])
+                lane = lax.broadcasted_iota(jnp.int32, (rows, 128), 1)
+                gate_s[here] += jnp.where(lane < 64, 0.0, jnp.sum(out * cot, axis=1, keepdims=True))
+                gc_ref[here, cols] = (gates * cot).astype(jnp.bfloat16)
+                p_ref = (p_a, p_b)[s]
+                p_ref[...] = dot_nn(turned_s[s], (gates * out).astype(jnp.bfloat16)).astype(jnp.bfloat16)
+
+    @pl.when(step == wide + deep - 1)
+    def _():
+        for s, tok_ref, cot_ref, here in pair:
+            gg = jnp.where(slot_onehot(meta_ref, s, rows), gate_s[here, 64:65], 0.0)
+            gg = jnp.sum(gg, axis=0, keepdims=True)
+            own = meta_ref[s, 2:3]
+            gg_ref[s] = jnp.where(lax.broadcasted_iota(jnp.int32, (8, count), 0) == own, gg, 0.0)
+
+
+def expert_bwd_kernel(meta_ref, gc_ref, slope_ref, act_ref, down_ref, gate_ref, up_ref, dg_ref, du_ref, dp_a, dp_b, turned_s, dg_s, du_s):
+    step = pl.program_id(0)
+    wide = dg_s.shape[1] // FT
+    rows = gc_ref.shape[0] // 2
+
+    @pl.when(step == 0)
+    def _():
+        for n in range(2):
+            hot = jnp.where(slot_onehot(meta_ref, n, rows), 1.0, 0.0).astype(jnp.bfloat16)
+            turned_s[n] = jnp.transpose(hot)
+
+    @pl.when(step < wide)
+    def _():
+        cols = pl.ds(pl.multiple_of(step * FT, FT), FT)
+        dh = dot_nt(gc_ref[...], down_ref[0])
+        dg = (dh * slope_ref[...].astype(jnp.float32)).astype(jnp.bfloat16)
+        du = (dh * act_ref[...].astype(jnp.float32)).astype(jnp.bfloat16)
+        dg_s[:, cols] = dg
+        du_s[:, cols] = du
+        dg_ref[...] = dg
+        du_ref[...] = du
+
+    @pl.when(step >= wide)
+    def _():
+        dx = (dot_nt(dg_s[...], gate_ref[0]) + dot_nt(du_s[...], up_ref[0])).astype(jnp.bfloat16)
+        for s in range(2):
+            dp_ref = (dp_a, dp_b)[s]
+            dp_ref[...] = dot_nn(turned_s[s], dx[s * rows : (s + 1) * rows]).astype(jnp.bfloat16)
+
+
+def low_shape(*shape):
+    return jax.ShapeDtypeStruct(shape, jnp.bfloat16)
+
+
+def expert_fwd(place, chips, rows, meta, router_rows, toks, cots, w_gate, w_up, w_down, buffers):
+    count = toks[0].shape[0]
+    width = w_gate.shape[2]
+    wide = width // FT
+    deep = D // FT
+    once = pl.Buffered(1)
+    whole = lambda *shape: pl.BlockSpec(shape, lambda j: (0,) * len(shape), pipeline_mode=once)
+    mine = pl.BlockSpec((2 * rows, D), lambda j: (place, 0), pipeline_mode=once)
+    one = lambda j: jnp.minimum(j, wide - 1)
+    two = lambda j: jnp.maximum(j - wide, 0)
+    strip = pl.BlockSpec((2 * rows, FT), lambda j: (place, one(j)))
+    total = 2 * chips * rows
+    buffers = () if buffers is None else tuple(buffers)
+    return pl.pallas_call(
+        expert_fwd_kernel,
+        grid=(wide + deep,),
+        in_specs=[whole(2, 8, count), whole(8, D)]
+        + [whole(count, D)] * 2
+        + [pl.BlockSpec((count, FT), lambda j: (0, two(j)))] * 2
+        + [pl.BlockSpec((1, D, FT), lambda j: (0, 0, one(j)))] * 2
+        + [pl.BlockSpec((1, width, FT), lambda j: (0, 0, two(j)))]
+        + [pl.BlockSpec(memory_space=pl.ANY)] * len(buffers),
+        out_specs=[
+            mine,
+            mine,
+            strip,
+            strip,
+            strip,
+            pl.BlockSpec((count, FT), lambda j: (0, two(j))),
+            pl.BlockSpec((count, FT), lambda j: (0, two(j))),
+            whole(2, 8, count),
+        ],
+        out_shape=[low_shape(total, D)] * 2
+        + [low_shape(total, width)] * 3
+        + [low_shape(count, D)] * 2
+        + [jax.ShapeDtypeStruct((2, 8, count), jnp.float32)],
+        scratch_shapes=[
+            pltpu.VMEM((2, rows, count), jnp.bfloat16),
+            pltpu.VMEM((2, count, rows), jnp.bfloat16),
+            pltpu.VMEM((2 * rows, width), jnp.bfloat16),
+            pltpu.VMEM((2 * rows, 128), jnp.float32),
+        ],
+        input_output_aliases={9 + n: n for n in range(len(buffers))},
+        compiler_params=pltpu.CompilerParams(vmem_limit_bytes=VMEM_MOST),
+        cost_estimate=LIGHT,
+        name=f"expert_fwd_{place}",
+    )(meta, router_rows, *toks, *cots, w_gate, w_up, w_down, *buffers)
+
+
+def expert_bwd(place, rows, meta, gc, slope, act, w_gate, w_up, w_down):
+    count = meta.shape[2]
+    total, width = slope.shape
+    wide = width // FT
+    deep = D // FT
+    once = pl.Buffered(1)
+    one = lambda j: jnp.minimum(j, wide - 1)
+    two = lambda j: jnp.maximum(j - wide, 0)
+    strip = pl.BlockSpec((2 * rows, FT), lambda j: (place, one(j)))
+    return pl.pallas_call(
+        expert_bwd_kernel,
+        grid=(wide + deep,),
+        in_specs=[
+            pl.BlockSpec((2, 8, count), lambda j: (0, 0, 0), pipeline_mode=once),
+            pl.BlockSpec((2 * rows, D), lambda j: (place, 0), pipeline_mode=once),
+            strip,
+            strip,
+            pl.BlockSpec((1, FT, D), lambda j: (0, one(j), 0)),
+            pl.BlockSpec((1, FT, width), lambda j: (0, two(j), 0)),
+            pl.BlockSpec((1, FT, width), lambda j: (0, two(j), 0)),
+        ],
+        out_specs=[strip] * 2 + [pl.BlockSpec((count, FT), lambda j: (0, two(j)))] * 2,
+        out_shape=[low_shape(total, width)] * 2 + [low_shape(count, D)] * 2,
+        scratch_shapes=[
+            pltpu.VMEM((2, count, rows), jnp.bfloat16),
+            pltpu.VMEM((2 * rows, width), jnp.bfloat16),
+            pltpu.VMEM((2 * rows, width), jnp.bfloat16),
+        ],
+        input_output_aliases={2: 0, 3: 1},
+        compiler_params=pltpu.CompilerParams(vmem_limit_bytes=VMEM_MOST),
+        cost_estimate=LIGHT,
+        name=f"expert_bwd_{place}",
+    )(meta, gc, slope, act, w_down, w_gate, w_up)
+
+
+def grad_down_kernel(left_ref, right_ref, out_ref, turned_s):
+    @pl.when(pl.program_id(0) == 0)
+    def _():
+        turned_s[...] = jnp.transpose(left_ref[...])
+
+    tile = dot_nn(turned_s[...], right_ref[...])
+    out_ref[...] = jnp.transpose(tile).astype(jnp.bfloat16)
+
+
+def grad_in_kernel(left_ref, gate_ref, up_ref, out_gate_ref, out_up_ref, turned_s):
+    @pl.when(pl.program_id(0) == 0)
+    def _():
+        turned_s[...] = jnp.transpose(left_ref[...])
+
+    out_gate_ref[...] = dot_nn(turned_s[...], gate_ref[...]).astype(jnp.bfloat16)
+    out_up_ref[...] = dot_nn(turned_s[...], up_ref[...]).astype(jnp.bfloat16)
+
+
+def grad_down(gc, hidden):
+    total, width = hidden.shape
+    return pl.pallas_call(
+        grad_down_kernel,
+        grid=(width // FT,),
+        in_specs=[pl.BlockSpec((total, D), lambda j: (0, 0)), pl.BlockSpec((total, FT), lambda j: (0, j))],
+        out_specs=pl.BlockSpec((FT, D), lambda j: (j, 0)),
+        out_shape=jax.ShapeDtypeStruct((width, D), jnp.bfloat16),
+        scratch_shapes=[pltpu.VMEM((D, total), jnp.bfloat16)],
+        compiler_params=pltpu.CompilerParams(vmem_limit_bytes=VMEM_LIMIT),
+        cost_estimate=LIGHT,
+        name="grad_down",
+    )(gc, hidden)
+
+
+def grad_in(rows, dgate, dup):
+    total, width = dgate.shape
+    strip = pl.BlockSpec((total, FT), lambda j: (0, j))
+    out = pl.BlockSpec((D, FT), lambda j: (0, j))
+    return pl.pallas_call(
+        grad_in_kernel,
+        grid=(width // FT,),
+        in_specs=[pl.BlockSpec((total, D), lambda j: (0, 0)), strip, strip],
+        out_specs=[out, out],
+        out_shape=[jax.ShapeDtypeStruct((D, width), jnp.bfloat16)] * 2,
+        scratch_shapes=[pltpu.VMEM((D, total), jnp.bfloat16)],
+        compiler_params=pltpu.CompilerParams(vmem_limit_bytes=VMEM_LIMIT),
+        cost_estimate=LIGHT,
+        name="grad_in",
+    )(rows, dgate, dup)
+
+
+def grad_half_kernel(left_ref, right_ref, out_ref, turned_s):
+    @pl.when(pl.program_id(0) == 0)
+    def _():
+        turned_s[...] = jnp.transpose(left_ref[...])
+
+    out_ref[...] = dot_nn(turned_s[...], right_ref[...]).astype(jnp.bfloat16)
+
+
+def grad_rows(left, right, name):
+    count, width = right.shape
+    return pl.pallas_call(
+        grad_half_kernel,
+        grid=(width // 512,),
+        in_specs=[pl.BlockSpec((count, D), lambda j: (0, 0)), pl.BlockSpec((count, 512), lambda j: (0, j))],
+        out_specs=pl.BlockSpec((D, 512), lambda j: (0, j)),
+        out_shape=jax.ShapeDtypeStruct((D, width), jnp.bfloat16),
+        scratch_shapes=[pltpu.VMEM((D, count), jnp.bfloat16)],
+        compiler_params=pltpu.CompilerParams(vmem_limit_bytes=VMEM_LIMIT),
+        cost_estimate=LIGHT,
+        name=name,
+    )(left, right)
+
+
+def grad_normed_kernel(first_ref, second_ref, w_ref, out_ref):
+    step = pl.program_id(0)
+
+    @pl.when(step == 0)
+    def _():
+        out_ref[...] = jnp.zeros_like(out_ref)
+
+    @pl.when(step % 2 == 0)
+    def _():
+        out_ref[...] += dot_nt(first_ref[...], w_ref[...])
+
+    @pl.when(step % 2 == 1)
+    def _():
+        out_ref[...] += dot_nt(second_ref[...], w_ref[...])
+
+
+def grad_normed_of(first, second, w_qkv):
+    count = first.shape[0]
+    part = pl.BlockSpec((count, D // 2), lambda j: (0, j // 2))
+    return pl.pallas_call(
+        grad_normed_kernel,
+        grid=(6,),
+        in_specs=[part, part, pl.BlockSpec((D, D // 2), lambda j: (0, j))],
+        out_specs=pl.BlockSpec((count, D), lambda j: (0, 0)),
+        out_shape=jax.ShapeDtypeStruct((count, D), jnp.float32),
+        compiler_params=pltpu.CompilerParams(vmem_limit_bytes=VMEM_LIMIT),
+        cost_estimate=LIGHT,
+        name="grad_normed",
+    )(first, second, w_qkv)
+
+
+OUTER = 4
+
+
 def rms_forward(values, gain):
     scale_rows = lax.rsqrt(jnp.mean(values * values, axis=-1, keepdims=True) + EPSILON)
     return (values * scale_rows * gain, scale_rows)
@@ -307,41 +625,97 @@
     return (scale_rows * scaled_grad - values * scale_rows**3 * inner_mean, gain_grad)
 
 
-def geglu(gate_pre, up_pre):
-    return jax.nn.gelu(gate_pre, approximate=True) * up_pre
-
-
-def expert_sums(received, gate_low, up_low, hidden, grad_recv):
-    local_experts = received.shape[1]
-    model_width = received.shape[3]
-    hidden_width = hidden.shape[3]
+def tie(*arrays):
+    return lax.optimization_barrier(arrays)
+
+
+def to_sibling(x):
+    groups = lax.axis_size("ep")
+    return lax.ppermute(x, "ep", [(e, e ^ 1) for e in range(groups)])
+
+
+def from_chip(x, away, cross=0):
+    groups = lax.axis_size("ep")
+    return lax.ppermute(x, "ep", [(e, ((e - 2 * away) % groups) ^ cross) for e in range(groups)])
+
+
+def core_pairs(step):
+    return [(e, e ^ 1) for e in range(lax.axis_size("ep"))]
+
+
+def chip_pairs(step):
+    groups = lax.axis_size("ep")
+    return [(e, (e + 2 * step) % groups) for e in range(groups)]
+
+
+def inner_pairs(step):
     replicas = lax.axis_size("rep")
-    joined_grads = jnp.concatenate([gate_low, up_low], axis=3)
-    columns = received
-    inner_sum = lax.psum_scatter(
-        jnp.einsum("secd,secg->deg", columns, joined_grads, preferred_element_type=jnp.float32)
-        .reshape(model_width // replicas * lax.axis_size("rep"), -1)
-        .astype(jnp.bfloat16),
-        "rep",
-        scatter_dimension=0,
-        tiled=True,
-    ).astype(jnp.float32)
-    columns = hidden
-    outer_sum = lax.psum_scatter(
-        jnp.einsum("secf,secd->fed", columns, grad_recv, preferred_element_type=jnp.float32)
-        .reshape(hidden_width // replicas * lax.axis_size("rep"), -1)
-        .astype(jnp.bfloat16),
-        "rep",
-        scatter_dimension=0,
-        tiled=True,
-    ).astype(jnp.float32)
-    inner_sum = inner_sum.reshape(inner_sum.shape[0], local_experts, 2 * hidden_width)
-    grad_w_gate = jnp.transpose(inner_sum[:, :, :hidden_width], (1, 0, 2))
-    grad_w_up = jnp.transpose(inner_sum[:, :, hidden_width:], (1, 0, 2))
-    grad_w_down = jnp.transpose(
-        outer_sum.reshape(outer_sum.shape[0], local_experts, model_width), (1, 0, 2)
+    inner = replicas // OUTER
+    return [(r, r - r % inner + (r + step) % inner) for r in range(replicas)]
+
+
+def outer_pairs(step):
+    replicas = lax.axis_size("rep")
+    return [(r, (r + step * (replicas // OUTER)) % replicas) for r in range(replicas)]
+
+
+def levels():
+    ep, rep = lax.axis_index("ep"), lax.axis_index("rep")
+    inner = lax.axis_size("rep") // OUTER
+    return (
+        ("ep", 2, ep % 2, core_pairs),
+        ("ep", lax.axis_size("ep") // 2, ep // 2, chip_pairs),
+        ("rep", inner, rep % inner, inner_pairs),
+        ("rep", OUTER, rep // inner, outer_pairs),
     )
-    return (grad_w_gate, grad_w_up, grad_w_down)
+
+
+def swapped(x, level):
+    axis, size, place, pairs = level
+    out = [lax.dynamic_index_in_dim(x, place, 0, keepdims=False)]
+    for step in range(1, size):
+        sent = lax.dynamic_index_in_dim(x, (place + step) % size, 0, keepdims=False)
+        out.append(lax.ppermute(sent, axis, pairs(step)))
+    return out
+
+
+def total(arrays):
+    return sum([x.astype(jnp.float32) for x in arrays[1:]], arrays[0].astype(jnp.float32))
+
+
+def low_total(arrays):
+    return total(arrays).astype(arrays[0].dtype)
+
+
+def collected(x, level):
+    axis, size, place, pairs = level
+    if size == 2:
+        other = lax.ppermute(x, axis, pairs(1))
+        return jnp.concatenate([jnp.where(place == 0, x, other), jnp.where(place == 0, other, x)])
+    out = lax.dynamic_update_index_in_dim(jnp.zeros((size, *x.shape), x.dtype), x, place, 0)
+    for step in range(1, size):
+        other = lax.ppermute(x, axis, pairs(step))
+        out = lax.dynamic_update_index_in_dim(out, other, (place - step) % size, 0)
+    return out.reshape(-1, *x.shape[1:])
+
+
+def rows_swapped(x, level):
+    return swapped(x.reshape(level[1], -1, x.shape[1]), level)
+
+
+def near_swapped(x):
+    replicas = lax.axis_size("rep")
+    blocks = x.reshape(OUTER, replicas // OUTER, x.shape[0] // replicas, x.shape[1])
+    return swapped(jnp.swapaxes(blocks, 0, 1), levels()[2])
+
+
+def slot_table(expert_ids, priority, experts, capacity):
+    ranks = priority.reshape(-1, 2)
+    names = jnp.arange(experts, dtype=jnp.int32)[:, None]
+    first, second = expert_ids[:, 0][None, :] == names, expert_ids[:, 1][None, :] == names
+    rank = jnp.where(first, ranks[:, 0][None, :], jnp.where(second, ranks[:, 1][None, :], 1 << 20))
+    slot = jnp.sum((rank[:, :, None] < rank[:, None, :]).astype(jnp.int32), axis=1)
+    return jnp.where((first | second) & (slot < capacity), slot, -1)
 
 
 def per_device(
@@ -362,16 +736,34 @@
 ):
     tok_count = tokens.shape[0]
     experts = w_router.shape[1]
-    local_experts = w_gate.shape[0]
     groups = lax.axis_size("ep")
+    chips = groups // 2
     capacity = 5 * tok_count // (2 * experts)
-    pair_count = 2 * tok_count
+    own = lax.axis_index("ep")
+
+    slots = slot_table(expert_ids, priority, experts, capacity)
+    ids = jnp.transpose(expert_ids)
+    table = jnp.concatenate([slots, ids], axis=0)
+    info = [(table, to_sibling(table))] + [(from_chip(table, n), from_chip(table, n, 1)) for n in range(1, chips)]
+    cot_sib = to_sibling(cotangent)
+    cot_far = [from_chip(cotangent, n) for n in range(1, chips)]
+    metas = []
+    for pair in info:
+        rows = []
+        for table in pair:
+            slot = lax.dynamic_slice_in_dim(table, own, 1, axis=0)
+            one, two = table[experts : experts + 1], table[experts + 1 :]
+            other = jnp.where(one == own, two, one)
+            rows.append(jnp.concatenate([slot, other, jnp.full((6, tok_count), 1, jnp.int32) * own], axis=0))
+        metas.append(jnp.stack(rows))
+
     diag = wide_diag(rel_table)
     token_float = tokens.astype(jnp.float32)
     normed, scale_attn = rms_forward(token_float, gain_attn)
     normed_low = normed.astype(jnp.bfloat16)
     qkv = jnp.dot(normed_low, w_qkv, preferred_element_type=jnp.float32).astype(jnp.bfloat16)
     attended_low, lse = attn_fwd(span_starts, qkv, diag)
+    attended_low, cot_sib, cot_far, metas = tie(attended_low, cot_sib, cot_far, metas)
     mixed = token_float + jnp.dot(attended_low, w_out, preferred_element_type=jnp.float32)
     routed, scale_moe = rms_forward(mixed, gain_moe)
     routed_low = routed.astype(jnp.bfloat16)
@@ -379,105 +771,147 @@
     choose = expert_ids[:, :, None] == jnp.arange(experts, dtype=jnp.int32)[None, None, :]
     chosen = jnp.sum(jnp.where(choose, logits[:, None, :], 0.0), axis=-1)
     gates = jax.nn.softmax(chosen, axis=-1)
-    flat_ids = expert_ids.reshape(-1)
-    ranks = priority.reshape(-1)
-    onehot = choose.reshape(pair_count, experts)
-    earlier = (ranks[:, None] < ranks[None, :]).astype(jnp.bfloat16)
-    counts = jnp.einsum(
-        "ap,ae->pe", earlier, onehot.astype(jnp.bfloat16), preferred_element_type=jnp.float32
-    )
-    slots = jnp.sum(jnp.where(onehot, counts, 0.0), axis=-1).astype(jnp.int32)
-    target = jnp.where(slots < capacity, flat_ids * capacity + slots, experts * capacity)
-    owner = jnp.full((experts * capacity,), pair_count, jnp.int32)
-    owner = owner.at[target].set(jnp.arange(pair_count, dtype=jnp.int32), mode="drop")
-    owner_token = owner // 2
-    send_rows = jnp.take(routed_low, owner_token, axis=0, mode="fill", fill_value=0)
-    send_rows = send_rows.reshape(groups, local_experts, capacity, D)
-    piece = lax.all_to_all(send_rows, "ep", split_axis=0, concat_axis=0, tiled=True)
-    gate_pre = jnp.einsum("secd,edf->secf", piece, w_gate, preferred_element_type=jnp.float32)
-    up_pre = jnp.einsum("secd,edf->secf", piece, w_up, preferred_element_type=jnp.float32)
-    hidden = geglu(gate_pre, up_pre).astype(jnp.bfloat16)
-    result = jnp.einsum(
-        "secf,efd->secd", hidden, w_down, preferred_element_type=jnp.float32
-    ).astype(jnp.bfloat16)
-    expert_results = (result, piece, gate_pre, up_pre, hidden)
-    received = expert_results[1]
-    returned = lax.all_to_all(
-        expert_results[0], "ep", split_axis=0, concat_axis=0, tiled=True
-    ).reshape(experts * capacity, D)
-    pair_rows = jnp.take(returned, target, axis=0, mode="fill", fill_value=0).astype(jnp.float32)
-    pair_rows = pair_rows.reshape(tok_count, 2, D)
-    block_out = (mixed + jnp.sum(gates[:, :, None] * pair_rows, axis=1)).astype(jnp.bfloat16)
+
+    router_rows = jnp.zeros((8, D), jnp.bfloat16).at[:experts].set(jnp.transpose(w_router))
+    weights = (w_gate, w_up, w_down)
+    core, chip, inner, outer = levels()
+
+    tok_far = [from_chip(routed_low, n) for n in range(1, chips)]
+    cots = [(cotangent, cot_sib)] + [(far, to_sibling(far)) for far in cot_far]
+    pair = (routed_low, to_sibling(routed_low))
+    made = expert_fwd(0, chips, capacity, metas[0], router_rows, pair, cots[0], *weights, None)
+    made, tok_far, cots = tie(made, tok_far, cots)
+    toks = [(far, to_sibling(far)) for far in tok_far]
+    outs, dots = [made[5:7]], [(made[7][0], made[7][1])]
+    buffers = made[:5]
+    for away in range(1, chips):
+        made = expert_fwd(
+            away, chips, capacity, metas[away], router_rows, toks[away - 1], cots[away], *weights, buffers
+        )
+        buffers = made[:5]
+        outs.append(made[5:7])
+        dots.append((made[7][0], made[7][1]))
+    rows_in, rows_out, hidden, slope, act = buffers
+
+    met = [[to_sibling(other) for mine, other in part] for part in (dots, outs)]
+    down_low = grad_down(rows_out, hidden)
+    down_low, slope, met, dots, outs = tie(down_low, slope, met, dots, outs)
+    dots, outs = [
+        [total([mine[n][0], got[n]]) for n in range(chips)] for mine, got in zip((dots, outs), met)
+    ]
+    outs_low = [x.astype(jnp.bfloat16) for x in outs[1:]]
+    slope, outs_low, down_low = tie(slope, outs_low, down_low)
+    far_outs = [from_chip(x, chips - 1 - n) for n, x in enumerate(outs_low)]
+    far_dots = [from_chip(x, chips - 1 - n) for n, x in enumerate(dots[1:])]
+    down_near = near_swapped(down_low)
+    grads = [None] * chips
+    for away in reversed(range(1, chips)):
+        slope, act, *grads[away] = expert_bwd(away, capacity, metas[away], rows_out, slope, act, *weights)
+    slope, far_outs, far_dots = tie(slope, far_outs, far_dots)
+    far_grads = []
+    for away in range(1, chips):
+        far_grads += [from_chip(grads[away][0], chips - away), from_chip(grads[away][1], chips - away, 1)]
+    slope, act, *here = expert_bwd(0, capacity, metas[0], rows_out, slope, act, *weights)
+    slope, down_near = tie(slope, down_near)
+    down_near = low_total(down_near)
+    slope, down_near = tie(slope, down_near)
+    near_grads = to_sibling(here[1])
+    down_far = swapped(down_near, outer)
+    gate_low, up_low = grad_in(rows_in, slope, act)
+    gate_low, up_low, far_grads, near_grads = tie(gate_low, up_low, far_grads, near_grads)
+    grad_pairs = total([here[0], near_grads] + far_grads)
+    grad_gates_all = total([dots[0]] + far_dots)
+    block_out = (mixed + total([outs[0]] + far_outs)).astype(jnp.bfloat16)
+    gate_near = near_swapped(gate_low)
+
     grad_out = cotangent.astype(jnp.float32)
-    grad_gates = jnp.sum(pair_rows * grad_out[:, None, :], axis=-1)
-    gate_slots = jnp.take(gates.reshape(-1), owner, mode="fill", fill_value=0.0)
-    grad_send = (
-        jnp.take(grad_out, owner_token, axis=0, mode="fill", fill_value=0.0) * gate_slots[:, None]
-    )
-    grad_send = grad_send.astype(jnp.bfloat16).reshape(groups, local_experts, capacity, D)
-    grad_recv = lax.all_to_all(grad_send, "ep", split_axis=0, concat_axis=0, tiled=True)
-    grad_hidden = jnp.einsum(
-        "secd,efd->secf", grad_recv, w_down, preferred_element_type=jnp.float32
-    )
-    gate_pre = expert_results[2]
-    up_pre = expert_results[3]
-    hidden = expert_results[4]
-    unused, geglu_pull = jax.vjp(geglu, gate_pre, up_pre)
-    gradient_gate_logits, grad_up_pre = geglu_pull(grad_hidden)
-    gate_low = gradient_gate_logits.astype(jnp.bfloat16)
-    up_low = grad_up_pre.astype(jnp.bfloat16)
-    grad_rows = (
-        jnp.einsum("secf,edf->secd", gate_low, w_gate, preferred_element_type=jnp.float32)
-        + jnp.einsum("secf,edf->secd", up_low, w_up, preferred_element_type=jnp.float32)
-    ).astype(jnp.bfloat16)
-    grad_home = lax.all_to_all(grad_rows, "ep", split_axis=0, concat_axis=0, tiled=True).reshape(
-        experts * capacity, D
-    )
-    grad_pairs = jnp.take(grad_home, target, axis=0, mode="fill", fill_value=0).astype(jnp.float32)
-    grad_pairs = grad_pairs.reshape(tok_count, 2, D)
+    by_token = jnp.transpose(grad_gates_all[:experts])
+    grad_gates = jnp.sum(jnp.where(choose, by_token[:, None, :], 0.0), axis=-1)
     grad_chosen = gates * (grad_gates - jnp.sum(gates * grad_gates, axis=-1, keepdims=True))
-    grad_logits = jnp.sum(jnp.where(choose, grad_chosen[:, :, None], 0.0), axis=1).astype(
-        jnp.bfloat16
-    )
-    grad_w_router = jnp.einsum(
-        "td,te->de", routed_low, grad_logits, preferred_element_type=jnp.float32
-    )
-    grad_routed = jnp.sum(grad_pairs, axis=1) + jnp.einsum(
+    grad_logits = jnp.sum(jnp.where(choose, grad_chosen[:, :, None], 0.0), axis=1).astype(jnp.bfloat16)
+    grad_w_router = jnp.einsum("td,te->de", routed_low, grad_logits, preferred_element_type=jnp.float32)
+    grad_routed = grad_pairs + jnp.einsum(
         "te,de->td", grad_logits, w_router, preferred_element_type=jnp.float32
     )
     grad_norm_moe, grad_gain_moe = rms_backward(mixed, scale_moe, gain_moe, grad_routed)
     grad_mixed = grad_out + grad_norm_moe
     grad_branch = grad_mixed.astype(jnp.bfloat16)
-    grad_w_out = jnp.einsum(
-        "td,te->de", attended_low, grad_branch, preferred_element_type=jnp.float32
+    grad_attended = jnp.einsum(
+        "te,de->td", grad_branch, w_out, preferred_element_type=jnp.float32
+    ).astype(jnp.bfloat16)
+
+    grad_attended, grad_branch, block_out = tie(grad_attended, grad_branch, block_out)
+    first = attn_bwd(span_starts, qkv, grad_attended, attended_low, lse, diag, 0)
+    half_first = grad_rows(normed_low, first[0], "grad_qkv_0")
+    grad_w_out = grad_rows(attended_low, grad_branch, "grad_out")
+    half_first, grad_w_out, grad_attended, gate_near, down_far = tie(
+        half_first, grad_w_out, grad_attended, gate_near, down_far
     )
-    grad_attended = jnp.einsum("te,de->td", grad_branch, w_out, preferred_element_type=jnp.float32)
-    grad_qkv, drel, far = attn_bwd(
-        span_starts, qkv, grad_attended.astype(jnp.bfloat16), attended_low, lse, diag
-    )
-    grad_rel_table = rel_grad(drel, far)
-    grad_w_qkv = jnp.einsum("td,tf->df", normed_low, grad_qkv, preferred_element_type=jnp.float32)
-    grad_normed = jnp.einsum("tf,df->td", grad_qkv, w_qkv, preferred_element_type=jnp.float32)
+    gate_near = low_total(gate_near)
+    sum_down = total(down_far)
+    gate_near, grad_attended, sum_down = tie(gate_near, grad_attended, sum_down)
+    gate_far = swapped(gate_near, outer)
+    up_near = near_swapped(up_low)
+    early = [rows_swapped(x, core) for x in (half_first, grad_w_out)]
+    second = attn_bwd(span_starts, qkv, grad_attended, attended_low, lse, diag, 1)
+    second, early = tie(second, early)
+    early = tie(*[low_total(x) for x in early])
+    early = [rows_swapped(x, chip) for x in early]
+    half_second = grad_rows(normed_low, second[0], "grad_qkv_1")
+    grad_normed = grad_normed_of(first[0], second[0], w_qkv)
+    half_second, grad_normed, early, gate_far, up_near = tie(half_second, grad_normed, early, gate_far, up_near)
+    up_near = low_total(up_near)
+    early = [low_total(x) for x in early]
     grad_norm_attn, grad_gain_attn = rms_backward(token_float, scale_attn, gain_attn, grad_normed)
     grad_tokens = grad_mixed + grad_norm_attn
-    grad_w_gate, grad_w_up, grad_w_down = expert_sums(received, gate_low, up_low, hidden, grad_recv)
-    everyone = ("rep", "ep")
-    sum_w_out = lax.psum(grad_w_out.astype(jnp.bfloat16), everyone).astype(jnp.float32)
-    sum_w_qkv = lax.psum(grad_w_qkv.astype(jnp.bfloat16), everyone).astype(jnp.float32)
-    small = lax.psum((grad_rel_table, grad_w_router, grad_gain_attn, grad_gain_moe), everyone)
-    summed = (sum_w_qkv, sum_w_out) + tuple(small)
+    grad_rel_table = rel_grad(jnp.concatenate([first[1], second[1]]), jnp.concatenate([first[2], second[2]]))
+    small = jnp.concatenate(
+        [
+            jnp.transpose(grad_w_router),
+            jnp.pad(grad_rel_table.reshape(1, -1), ((0, 0), (0, D - BUCKETS * H))),
+            grad_gain_attn[None],
+            grad_gain_moe[None],
+        ]
+    )
+    small = jnp.pad(jnp.transpose(small), ((0, 0), (0, 128 - small.shape[0])))
+    up_near, half_second, small, early, grad_tokens = tie(up_near, half_second, small, early, grad_tokens)
+    up_far = swapped(up_near, outer)
+    late = tie(*[rows_swapped(x, core) for x in (half_second, small)])
+    late = [low_total(x) for x in late]
+    late = tie(*[rows_swapped(x, inner) for x in late])
+    late, early = tie([low_total(x) for x in late], early)
+    late, early = tie([rows_swapped(x, chip) for x in late], [rows_swapped(x, inner) for x in early])
+    both = tie(*[low_total(x) for x in (*early, *late)])
+    both, up_far = tie([rows_swapped(x, outer) for x in both], up_far)
+    both = tie(*[low_total(x) for x in both])
+    both = tie(*[collected(x, outer) for x in both])
+    both = tie(*[collected(x, level) for x, level in zip(both, (inner, inner, chip, chip))])
+    both = tie(*[collected(x, level) for x, level in zip(both, (chip, chip, inner, inner))])
+    both = tie(*[collected(x, core) for x in both])
+    sum_first, sum_w_out, sum_second, small = [x.astype(jnp.float32) for x in both]
+    sum_gate, sum_up = total(gate_far), total(up_far)
+    sum_w_qkv = jnp.concatenate(
+        [x[:, n * D // 2 : (n + 1) * D // 2] for n in range(3) for x in (sum_first, sum_second)], axis=1
+    )
+    small = jnp.transpose(small)
+    small = (
+        small[experts, : BUCKETS * H].reshape(BUCKETS, H),
+        jnp.transpose(small[:experts]),
+        small[experts + 1],
+        small[experts + 2],
+    )
     return (
         block_out,
         grad_tokens,
-        summed[4],
-        summed[0],
-        summed[1],
-        summed[2],
-        summed[5],
-        summed[3],
-        grad_w_gate,
-        grad_w_up,
-        grad_w_down,
+        small[2],
+        sum_w_qkv,
+        sum_w_out,
+        small[0],
+        small[3],
+        small[1],
+        sum_gate[None],
+        sum_up[None],
+        sum_down[None],
     )
 
 

time: 1180 us -> 833 us (0.71)
  Pallas kernels: 102 us -> 430 us
  matrix products: 272 us -> 26.2 us
  blocking collectives: 170 us -> 0 us
  waiting for transfers between devices: 296 us -> 132 us
  local copies, waits for them, and re-layouts: 202 us -> 49.1 us
  starting transfers between devices: 10.7 us -> 118 us
  other arithmetic: 101 us -> 65.7 us
  between operations: 16.4 us -> 2.49 us
    pallas_call x1 -> x12, Pallas kernels: 61.9 us -> 390 us  [the longest x2 136 us: expert_fwd(): pl.pallas_call(expert_fwd_kernel, grid=(wide + deep,), in_specs=[whole(2,...]
    dot_general x12 -> x0, matrix products: 238 us -> none  [the longest x1 42.5 us: per_device(): jnp.einsum('secd,efd->secf', grad_recv, w_down, preferred_element_type=jn...]
    psum x1 -> x0, waiting for transfers between devices: 151 us -> none  [per_device(): lax.psum(grad_w_qkv.astype(jnp.bfloat16), everyone).astype(jnp.float32)]
    ppermute x0 -> x78, waiting for transfers between devices: none -> 132 us  [the longest x36 80.8 us: swapped(): out.append(lax.ppermute(sent, axis, pairs(step)))]
    all_to_all x2 -> x0, blocking collectives: 127 us -> none  [the longest x1 63.9 us: per_device(): lax.all_to_all(send_rows, 'ep', split_axis=0, concat_axis=0, tiled=True)]
    ppermute x0 -> x78, starting transfers between devices: none -> 118 us  [the longest x36 79.6 us: swapped(): out.append(lax.ppermute(sent, axis, pairs(step)))]
    all_to_all x2 -> x0, waiting for transfers between devices: 76.7 us -> none  [the longest x1 59.4 us: per_device(): lax.all_to_all(grad_rows, 'ep', split_axis=0, concat_axis=0, tiled=True)]
    gather x5 -> x0, local copies, waits for them, and re-layouts: 70.2 us -> none  [the longest x1 14.4 us: per_device(): jnp.take(grad_home, target, axis=0, mode='fill', fill_value=0)]
  transfers between devices with their start and end apart: 5 -> 78, of which waited for: 4 -> 26; matrix products, arithmetic and copies ran while one was open for 15% -> 10% of each run, Pallas kernels for 0% -> 52%
where the time goes in v2:
time: 833 us; the launch traced here: 824 us
  Pallas kernels  430 us (52%)
  waiting for transfers between devices  132 us (16%)
  starting transfers between devices  118 us (14%)
  other arithmetic  65.7 us (8%)
  local copies, waits for them, and re-layouts  49.1 us (6%)
  matrix products  26.2 us (3%)
    pallas_call x2, Pallas kernels, expert_fwd(): pl.pallas_call(expert_fwd_kernel, grid=(wide + deep,), in_specs=[whole(2,...  136 us
    pallas_call x2, Pallas kernels, expert_bwd(): pl.pallas_call(expert_bwd_kernel, grid=(wide + deep,), in_specs=[pl.Block...  93.3 us
    ppermute x36, waiting for transfers between devices, swapped(): out.append(lax.ppermute(sent, axis, pairs(step)))  80.8 us
    ppermute x36, starting transfers between devices, swapped(): out.append(lax.ppermute(sent, axis, pairs(step)))  79.6 us
    pallas_call x2, Pallas kernels, attn_bwd(): pl.pallas_call(attn_bwd_kernel, grid=(pairs, 3), in_specs=[pl.BlockSpec(m...  64.6 us
    pallas_call x1, Pallas kernels, attn_fwd(): pl.pallas_call(attn_fwd_kernel, grid=(H // 2,), in_specs=[pl.BlockSpec(me...  40 us
    pallas_call x1, Pallas kernels, grad_in(): pl.pallas_call(grad_in_kernel, grid=(width // FT,), in_specs=[pl.BlockSpe...  38.1 us
    ppermute x12, waiting for transfers between devices, collected(): other = lax.ppermute(x, axis, pairs(1))  31.3 us
  transfers between devices with their start and end apart: 78, of which 26 were waited for; matrix products, arithmetic and copies ran while one was open for 10% of the time, Pallas kernels for 52%

profile of v2, /device:TPU:0, one launch (start us, length us, event | category | flops | bytes accessed | tf_op | source)
XLA Modules:
  0.0 823.7 jit_solution(6783052285593155386)
XLA Ops:
  16.2 12.1 %convolution_convert_fusion.q_ref.k_ref.v_ref = bf16[1024,3072]{1,0:T(8,128)(2,1)} fusion(bf16[1024,1024]{1,0:T(8,128)(2,1)S(1)} %fusion.2.left_ref, bf16[1024,3072]{1,0:T(8,128)(2,1)} %w_ref.1), kind=kOutput, calls=%fused_computation.10 | convolution fusion | flops 6445596672 | bytes 14680064 | tf_op jit(solution)/shard_map/dot_general | solution.py:764
  29.4 40.0 %attn_fwd.1 = (bf16[1024,1024]{1,0:T(8,128)(2,1)}, f32[8,2,1024]{2,1,0:T(2,128)}) custom-call(s32[1,2]{1,0:T(1,128)} %span_ref.5, bf16[1024,3072]{1,0:T(8,128)(2,1)} %convolution_convert_fusion.q_ref.k_ref.v_ref, bf16[1024,3072]{1,0:T(8,128)(2,1)} %convolution_convert_fusion.q_ref.k_ref.v_ref, bf16[1024,3072]{1,0:T(8,128)(2,1)} %convolution_convert_fusion.q_ref.k_ref.v_ref, ...), custom_call_target="tpu_custom_call" | custom-call | flops 1000 | bytes 1000 | tf_op jit(solution)/shard_map/attn_fwd/pallas_call | solution.py:144
  80.8 62.1 %expert_fwd_0.1 = (bf16[2560,1024]{1,0:T(8,128)(2,1)}, bf16[2560,1024]{1,0:T(8,128)(2,1)}, bf16[2560,2816]{1,0:T(8,128)(2,1)}, bf16[2560,2816]{1,0:T(8,128)(2,1)...) custom-call(s32[2,8,1024]{2,1,0:T(8,128)} %get-tuple-element.231.met, ...), custom_call_target="tpu_custom_call" | custom-call | flops 1000 | bytes 1000 | tf_op jit(solution)/shard_map/expert_fwd_0/pallas_call | solution.py:438
  148.3 73.9 %expert_fwd_1.1 = (bf16[2560,1024]{1,0:T(8,128)(2,1)}, bf16[2560,1024]{1,0:T(8,128)(2,1)}, bf16[2560,2816]{1,0:T(8,128)(2,1)}, bf16[2560,2816]{1,0:T(8,128)(2,1)...) custom-call(s32[2,8,1024]{2,1,0:T(8,128)} %get-tuple-element.232.met, ...), custom_call_target="tpu_custom_call", output_to_operand_aliasing={{0}: (9, {}), {1}: (10, {}), {2}: (11, {}), {3}: (12, {}), ... | custom-call | flops 1000 | bytes 1000 | tf_op jit(solution)/shard_map/expert_fwd_1/pallas_call | solution.py:438
  223.7 22.9 %grad_down.1 = bf16[2816,1024]{1,0:T(8,128)(2,1)} custom-call(bf16[2560,1024]{1,0:T(8,128)(2,1)} %get-tuple-element.251.left_ref.gc_ref, bf16[2560,2816]{1,0:T(8,128)(2,1)} %get-tuple-element.252.right_ref), custom_call_target="tpu_custom_call" | custom-call | flops 1000 | bytes 1000 | tf_op jit(solution)/shard_map/grad_down/pallas_call | solution.py:529
  264.2 46.6 %expert_bwd_1.1 = (bf16[2560,2816]{1,0:T(8,128)(2,1)}, bf16[2560,2816]{1,0:T(8,128)(2,1)}, bf16[1024,1024]{1,0:T(8,128)(2,1)}, bf16[1024,1024]{1,0:T(8,128)(2,1)}) custom-call(s32[2,8,1024]{2,1,0:T(8,128)} %get-tuple-element.232.meta_ref, bf16[2560,1024]{1,0:T(8,128)(2,1)} %get-tuple-element.251.left_ref.gc_ref, ...), custom_call_target="tpu_custom_call", output_to_operand_aliasing={{0}: (2, {}), {1}: (3, {})} | custom-call | flops 1000 | bytes 1000 | tf_op jit(solution)/shard_map/expert_bwd_1/pallas_call | solution.py:483
  311.6 46.8 %expert_bwd_0.1 = (bf16[2560,2816]{1,0:T(8,128)(2,1)}, bf16[2560,2816]{1,0:T(8,128)(2,1)}, bf16[1024,1024]{1,0:T(8,128)(2,1)}, bf16[1024,1024]{1,0:T(8,128)(2,1)}) custom-call(s32[2,8,1024]{2,1,0:T(8,128)} %get-tuple-element.231.meta_ref, bf16[2560,1024]{1,0:T(8,128)(2,1)} %get-tuple-element.251.left_ref.gc_ref, ...), custom_call_target="tpu_custom_call", output_to_operand_aliasing={{0}: (2, {}), {1}: (3, {})} | custom-call | flops 1000 | bytes 1000 | tf_op jit(solution)/shard_map/expert_bwd_0/pallas_call | solution.py:483
  371.8 38.1 %grad_in.1 = (bf16[1024,2816]{1,0:T(8,128)(2,1)}, bf16[1024,2816]{1,0:T(8,128)(2,1)}) custom-call(bf16[2560,1024]{1,0:T(8,128)(2,1)} %get-tuple-element.273.left_ref, bf16[2560,2816]{1,0:T(8,128)(2,1)} %get-tuple-element.279.gate_ref, bf16[2560,2816]{1,0:T(8,128)(2,1)} %get-tuple-element.280.up_ref), custom_call_target="tpu_custom_call" | custom-call | flops 1000 | bytes 1000 | tf_op jit(solution)/shard_map/grad_in/pallas_call | solution.py:546
  419.3 7.6 multiply_reduce_fusion
  433.4 6.2 grad_out.1
  439.6 32.4 %attn_bwd_0.1 = (bf16[1024,1536]{1,0:T(8,128)(2,1)}, f32[4,2,768]{2,1,0:T(2,128)}, f32[4,2,2,8,256]{4,3,2,1,0:T(8,128)}) custom-call(s32[1,2]{1,0:T(1,128)} %span_ref.5, bf16[1024,3072]{1,0:T(8,128)(2,1)} %convolution_convert_fusion.q_ref.k_ref.v_ref, bf16[1024,3072]{1,0:T(8,128)(2,1)} %convolution_convert_fusion.q_ref.k_ref.v_ref, ...), custom_call_target="tpu_custom_call" | custom-call | flops 1000 | bytes 1000 | tf_op jit(solution)/shard_map/attn_bwd_0/pallas_call | solution.py:248
  472.0 7.7 grad_qkv_0.1
  492.4 32.2 %attn_bwd_1.1 = (bf16[1024,1536]{1,0:T(8,128)(2,1)}, f32[4,2,768]{2,1,0:T(2,128)}, f32[4,2,2,8,256]{4,3,2,1,0:T(8,128)}) custom-call(s32[1,2]{1,0:T(1,128)} %span_ref.5, bf16[1024,3072]{1,0:T(8,128)(2,1)} %convolution_convert_fusion.q_ref.k_ref.v_ref, bf16[1024,3072]{1,0:T(8,128)(2,1)} %convolution_convert_fusion.q_ref.k_ref.v_ref, ...), custom_call_target="tpu_custom_call" | custom-call | flops 1000 | bytes 1000 | tf_op jit(solution)/shard_map/attn_bwd_1/pallas_call | solution.py:248
  535.9 10.6 %collective-permute-done.30 = bf16[4,128,2816]{2,1,0:T(8,128)(2,1)} collective-permute-done((bf16[4,128,2816]{2,1,0:T(8,128)(2,1)}, bf16[4,128,2816]{2,1,0:T(8,128)(2,1)}, u32[]{:S(2)}, u32[]{:S(2)}) %collective-permute-start.30) | collective-permute-done | bytes 2883616 | tf_op jit(solution)/shard_map/ppermute | solution.py:678
  547.6 13.3 %grad_normed.1 = f32[1024,1024]{1,0:T(8,128)} custom-call(bf16[1024,1536]{1,0:T(8,128)(2,1)} %get-tuple-element.298.right_ref.first_ref, bf16[1024,1536]{1,0:T(8,128)(2,1)} %get-tuple-element.315.right_ref.second_ref, bf16[1024,3072]{1,0:T(8,128)(2,1)} %w_ref.1), custom_call_target="tpu_custom_call" | custom-call | flops 1000 | bytes 1000 | tf_op jit(solution)/shard_map/grad_normed/pallas_call | solution.py:601
  560.9 7.8 grad_qkv_1.1
  570.6 7.2 collective-permute-done.28
  604.6 19.8 %collective-permute-done.34 = f32[256,128]{1,0:T(8,128)S(1)} collective-permute-done((f32[256,128]{1,0:T(8,128)S(1)}, f32[256,128]{1,0:T(8,128)S(1)}, u32[]{:S(2)}, u32[]{:S(2)}) %collective-permute-start.34) | collective-permute-done | bytes 131104 | tf_op jit(solution)/shard_map/ppermute | solution.py:678
  630.6 15.4 %collective-permute-start.51 = (bf16[128,2816]{1,0:T(8,128)(2,1)S(1)}, bf16[128,2816]{1,0:T(8,128)(2,1)S(1)}, u32[]{:S(2)}, u32[]{:S(2)}) collective-permute-start(bf16[128,2816]{1,0:T(8,128)(2,1)S(1)} %get-tuple-element.487), channel_id=1, source_target_pairs={{0,8},{4,12},{8,16},{12,20},{16,24},{20,28},{24,0},{28,4},{1,9},{5... | collective-permute-start | bytes 2162696 | tf_op jit(solution)/shard_map/ppermute | solution.py:678
  651.3 6.4 collective-permute-start.48
  662.7 28.7 %collective-permute-done.52 = bf16[128,2816]{1,0:T(8,128)(2,1)S(1)} collective-permute-done((bf16[128,2816]{1,0:T(8,128)(2,1)S(1)}, bf16[128,2816]{1,0:T(8,128)(2,1)S(1)}, u32[]{:S(2)}, u32[]{:S(2)}) %collective-permute-start.52) | collective-permute-done | bytes 720928 | tf_op jit(solution)/shard_map/ppermute | solution.py:678
  691.4 17.2 %collective-permute-start.45 = (bf16[32,1536]{1,0:T(8,128)(2,1)S(1)}, bf16[32,1536]{1,0:T(8,128)(2,1)S(1)}, u32[]{:S(2)}, u32[]{:S(2)}) collective-permute-start(bf16[32,1536]{1,0:T(8,128)(2,1)S(1)} %get-tuple-element.531), channel_id=1, source_target_pairs={{0,8},{4,12},{8,16},{12,20},{16,24},{20,28},{24,0},{28,4},{1,9},{5... | collective-permute-start | bytes 294920 | tf_op jit(solution)/shard_map/ppermute | solution.py:678
  766.1 7.1 collective-permute-done.67
  774.7 6.9 collective-permute-done.66
  (428 shorter events, 252.3 us)
Async XLA Ops:
  7.1 62.4 %collective-permute-start.3 = (s32[6,1024]{1,0:T(8,128)S(1)}, s32[6,1024]{1,0:T(8,128)S(1)}, u32[]{:S(2)}, u32[]{:S(2)}) collective-permute-start(s32[6,1024]{1,0:T(8,128)S(1)} %pad_add_fusion.2), channel_id=1, source_target_pairs={{0,2},{1,3},{2,0},{3,1},{4,6},{5,7},{6,4},{7,5},{8,10},{9,11},{10,... | collective-permute-start | bytes 73736 | tf_op jit(solution)/shard_map/ppermute | solution.py:639
  10.2 59.4 %collective-permute-start.4 = (s32[6,1024]{1,0:T(8,128)S(1)}, s32[6,1024]{1,0:T(8,128)S(1)}, u32[]{:S(2)}, u32[]{:S(2)}) collective-permute-start(s32[6,1024]{1,0:T(8,128)S(1)} %pad_add_fusion.2), channel_id=1, source_target_pairs={{0,3},{1,2},{2,1},{3,0},{4,7},{5,6},{6,5},{7,4},{8,11},{9,10},{10,... | collective-permute-start | bytes 73736 | tf_op jit(solution)/shard_map/ppermute | solution.py:639
  10.2 59.4 %collective-permute-start.2 = (s32[6,1024]{1,0:T(8,128)S(1)}, s32[6,1024]{1,0:T(8,128)S(1)}, u32[]{:S(2)}, u32[]{:S(2)}) collective-permute-start(s32[6,1024]{1,0:T(8,128)S(1)} %pad_add_fusion.2), channel_id=1, source_target_pairs={{0,1},{1,0},{2,3},{3,2},{4,5},{5,4},{6,7},{7,6},{8,9},{9,8},{10,11... | collective-permute-start | bytes 73736 | tf_op jit(solution)/shard_map/ppermute | solution.py:634
  10.3 60.0 %collective-permute-start = (bf16[1024,1024]{1,0:T(8,128)(2,1)}, bf16[1024,1024]{1,0:T(8,128)(2,1)}, u32[]{:S(2)}, u32[]{:S(2)}) collective-permute-start(bf16[1024,1024]{1,0:T(8,128)(2,1)} %cot_a.1), channel_id=1, source_target_pairs={{0,1},{1,0},{2,3},{3,2},{4,5},{5,4},{6,7},{7,6},{8,9},{9,8},{10,11... | collective-permute-start | bytes 6291464 | tf_op jit(solution)/shard_map/ppermute | solution.py:634
  10.7 59.7 %collective-permute-start.1 = (bf16[1024,1024]{1,0:T(8,128)(2,1)}, bf16[1024,1024]{1,0:T(8,128)(2,1)}, u32[]{:S(2)}, u32[]{:S(2)}) collective-permute-start(bf16[1024,1024]{1,0:T(8,128)(2,1)} %cot_a.1), channel_id=1, source_target_pairs={{0,2},{1,3},{2,0},{3,1},{4,6},{5,7},{6,4},{7,5},{8,10},{9,11},{10,... | collective-permute-start | bytes 6291464 | tf_op jit(solution)/shard_map/ppermute | solution.py:639
  76.7 66.2 %collective-permute-start.6 = (bf16[1024,1024]{1,0:T(8,128)(2,1)S(1)}, bf16[1024,1024]{1,0:T(8,128)(2,1)}, u32[]{:S(2)}, u32[]{:S(2)}) collective-permute-start(bf16[1024,1024]{1,0:T(8,128)(2,1)S(1)} %multiply_convert_fusion.tok_a), channel_id=1, source_target_pairs={{0,2},{1,3},{2,0},{3,1},{4,6},{5,7},{6,4},{7,5},{8,10},{9,11},{10,... | collective-permute-start | bytes 6291464 | tf_op jit(solution)/shard_map/ppermute | solution.py:639
  77.0 65.9 %collective-permute-start.7 = (bf16[1024,1024]{1,0:T(8,128)(2,1)}, bf16[1024,1024]{1,0:T(8,128)(2,1)}, u32[]{:S(2)}, u32[]{:S(2)}) collective-permute-start(bf16[1024,1024]{1,0:T(8,128)(2,1)} %collective-permute-done.1.cot_a), channel_id=1, source_target_pairs={{0,1},{1,0},{2,3},{3,2},{4,5},{5,4},{6,7},{7,6},{8,9},{9,8},{10,11... | collective-permute-start | bytes 6291464 | tf_op jit(solution)/shard_map/ppermute | solution.py:634
  143.2 103.4 %collective-permute-start.11 = (bf16[1024,1024]{1,0:T(8,128)(2,1)}, bf16[1024,1024]{1,0:T(8,128)(2,1)S(1)}, u32[]{:S(2)}, u32[]{:S(2)}) collective-permute-start(bf16[1024,1024]{1,0:T(8,128)(2,1)} %get-tuple-element.256), channel_id=1, source_target_pairs={{0,1},{1,0},{2,3},{3,2},{4,5},{5,4},{6,7},{7,6},{8,9},{9,8},{10,11... | collective-permute-start | bytes 6291464 | tf_op jit(solution)/shard_map/ppermute | solution.py:634
  251.2 60.4 %collective-permute-start.13 = (bf16[1024,1024]{1,0:T(8,128)(2,1)}, bf16[1024,1024]{1,0:T(8,128)(2,1)}, u32[]{:S(2)}, u32[]{:S(2)}) collective-permute-start(bf16[1024,1024]{1,0:T(8,128)(2,1)} %add_convert_fusion.4), channel_id=1, source_target_pairs={{0,2},{1,3},{2,0},{3,1},{4,6},{5,7},{6,4},{7,5},{8,10},{9,11},{10,... | collective-permute-start | bytes 6291464 | tf_op jit(solution)/shard_map/ppermute | solution.py:639
  258.6 104.1 %collective-permute-start.15 = (bf16[4,352,1024]{2,1,0:T(8,128)(2,1)}, bf16[4,352,1024]{2,1,0:T(8,128)(2,1)}, u32[]{:S(2)}, u32[]{:S(2)}) collective-permute-start(bf16[4,352,1024]{2,1,0:T(8,128)(2,1)} %get-tuple-element.474), channel_id=1, source_target_pairs={{0,4},{4,0},{8,12},{12,8},{16,20},{20,16},{24,28},{28,24},{1,5},{5... | collective-permute-start | bytes 8650760 | tf_op jit(solution)/shard_map/ppermute | solution.py:678
  260.4 51.2 %collective-permute-start.14 = (f32[8,1024]{1,0:T(8,128)S(1)}, f32[8,1024]{1,0:T(8,128)S(1)}, u32[]{:S(2)}, u32[]{:S(2)}) collective-permute-start(f32[8,1024]{1,0:T(8,128)S(1)} %add.453), channel_id=1, source_target_pairs={{0,2},{1,3},{2,0},{3,1},{4,6},{5,7},{6,4},{7,5},{8,10},{9,11},{10,... | collective-permute-start | bytes 98312 | tf_op jit(solution)/shard_map/ppermute | solution.py:639
  310.7 99.1 %collective-permute-start.16 = (bf16[1024,1024]{1,0:T(8,128)(2,1)}, bf16[1024,1024]{1,0:T(8,128)(2,1)}, u32[]{:S(2)}, u32[]{:S(2)}) collective-permute-start(bf16[1024,1024]{1,0:T(8,128)(2,1)} %get-tuple-element.283), channel_id=1, source_target_pairs={{0,2},{1,3},{2,0},{3,1},{4,6},{5,7},{6,4},{7,5},{8,10},{9,11},{10,... | collective-permute-start | bytes 6291464 | tf_op jit(solution)/shard_map/ppermute | solution.py:639
  311.3 100.2 %collective-permute-start.17 = (bf16[1024,1024]{1,0:T(8,128)(2,1)}, bf16[1024,1024]{1,0:T(8,128)(2,1)}, u32[]{:S(2)}, u32[]{:S(2)}) collective-permute-start(bf16[1024,1024]{1,0:T(8,128)(2,1)} %get-tuple-element.284), channel_id=1, source_target_pairs={{0,3},{1,2},{2,1},{3,0},{4,7},{5,6},{6,5},{7,4},{8,11},{9,10},{10,... | collective-permute-start | bytes 6291464 | tf_op jit(solution)/shard_map/ppermute | solution.py:639
  358.4 53.1 %collective-permute-start.18 = (bf16[1024,1024]{1,0:T(8,128)(2,1)}, bf16[1024,1024]{1,0:T(8,128)(2,1)}, u32[]{:S(2)}, u32[]{:S(2)}) collective-permute-start(bf16[1024,1024]{1,0:T(8,128)(2,1)} %get-tuple-element.285), channel_id=1, source_target_pairs={{0,1},{1,0},{2,3},{3,2},{4,5},{5,4},{6,7},{7,6},{8,9},{9,8},{10,11... | collective-permute-start | bytes 6291464 | tf_op jit(solution)/shard_map/ppermute | solution.py:634
  367.6 115.5 %collective-permute-start.20 = (bf16[352,1024]{1,0:T(8,128)(2,1)}, bf16[352,1024]{1,0:T(8,128)(2,1)}, u32[]{:S(2)}, u32[]{:S(2)}) collective-permute-start(bf16[352,1024]{1,0:T(8,128)(2,1)} %get-tuple-element.495), channel_id=1, source_target_pairs={{0,8},{4,12},{8,16},{12,20},{16,24},{20,28},{24,0},{28,4},{1,9},{5... | collective-permute-start | bytes 2162696 | tf_op jit(solution)/shard_map/ppermute | solution.py:678
  369.2 113.9 %collective-permute-start.21 = (bf16[352,1024]{1,0:T(8,128)(2,1)}, bf16[352,1024]{1,0:T(8,128)(2,1)}, u32[]{:S(2)}, u32[]{:S(2)}) collective-permute-start(bf16[352,1024]{1,0:T(8,128)(2,1)} %get-tuple-element.494), channel_id=1, source_target_pairs={{0,16},{4,20},{8,24},{12,28},{16,0},{20,4},{24,8},{28,12},{1,17},{... | collective-permute-start | bytes 2162696 | tf_op jit(solution)/shard_map/ppermute | solution.py:678
  409.9 73.3 %collective-permute-start.22 = (bf16[352,1024]{1,0:T(8,128)(2,1)}, bf16[352,1024]{1,0:T(8,128)(2,1)}, u32[]{:S(2)}, u32[]{:S(2)}) collective-permute-start(bf16[352,1024]{1,0:T(8,128)(2,1)} %get-tuple-element.493), channel_id=1, source_target_pairs={{0,24},{4,28},{8,0},{12,4},{16,8},{20,12},{24,16},{28,20},{1,25},{... | collective-permute-start | bytes 2162696 | tf_op jit(solution)/shard_map/ppermute | solution.py:678
  417.6 65.5 %collective-permute-start.19 = (bf16[4,128,2816]{2,1,0:T(8,128)(2,1)}, bf16[4,128,2816]{2,1,0:T(8,128)(2,1)}, u32[]{:S(2)}, u32[]{:S(2)}) collective-permute-start(bf16[4,128,2816]{2,1,0:T(8,128)(2,1)} %get-tuple-element.472), channel_id=1, source_target_pairs={{0,4},{4,0},{8,12},{12,8},{16,20},{20,16},{24,28},{28,24},{1,5},{5... | collective-permute-start | bytes 8650760 | tf_op jit(solution)/shard_map/ppermute | solution.py:678
  482.6 63.9 %collective-permute-start.30 = (bf16[4,128,2816]{2,1,0:T(8,128)(2,1)}, bf16[4,128,2816]{2,1,0:T(8,128)(2,1)}, u32[]{:S(2)}, u32[]{:S(2)}) collective-permute-start(bf16[4,128,2816]{2,1,0:T(8,128)(2,1)} %get-tuple-element.470), channel_id=1, source_target_pairs={{0,4},{4,0},{8,12},{12,8},{16,20},{20,16},{24,28},{28,24},{1,5},{5... | collective-permute-start | bytes 8650760 | tf_op jit(solution)/shard_map/ppermute | solution.py:678
  526.8 51.0 %collective-permute-start.28 = (bf16[128,2816]{1,0:T(8,128)(2,1)}, bf16[128,2816]{1,0:T(8,128)(2,1)}, u32[]{:S(2)}, u32[]{:S(2)}) collective-permute-start(bf16[128,2816]{1,0:T(8,128)(2,1)} %get-tuple-element.490), channel_id=1, source_target_pairs={{0,16},{4,20},{8,24},{12,28},{16,0},{20,4},{24,8},{28,12},{1,17},{... | collective-permute-start | bytes 2162696 | tf_op jit(solution)/shard_map/ppermute | solution.py:678
  647.6 60.9 %collective-permute-start.53 = (bf16[128,2816]{1,0:T(8,128)(2,1)S(1)}, bf16[128,2816]{1,0:T(8,128)(2,1)S(1)}, u32[]{:S(2)}, u32[]{:S(2)}) collective-permute-start(bf16[128,2816]{1,0:T(8,128)(2,1)S(1)} %get-tuple-element.485), channel_id=1, source_target_pairs={{0,24},{4,28},{8,0},{12,4},{16,8},{20,12},{24,16},{28,20},{1,25},{... | collective-permute-start | bytes 2162696 | tf_op jit(solution)/shard_map/ppermute | solution.py:678
  651.3 57.3 %collective-permute-start.48 = (f32[32,128]{1,0:T(8,128)S(1)}, f32[32,128]{1,0:T(8,128)S(1)}, u32[]{:S(2)}, u32[]{:S(2)}) collective-permute-start(f32[32,128]{1,0:T(8,128)S(1)} %get-tuple-element.551), channel_id=1, source_target_pairs={{0,8},{4,12},{8,16},{12,20},{16,24},{20,28},{24,0},{28,4},{1,9},{5... | collective-permute-start | bytes 49160 | tf_op jit(solution)/shard_map/ppermute | solution.py:678
  657.7 54.4 %collective-permute-start.49 = (f32[32,128]{1,0:T(8,128)S(1)}, f32[32,128]{1,0:T(8,128)S(1)}, u32[]{:S(2)}, u32[]{:S(2)}) collective-permute-start(f32[32,128]{1,0:T(8,128)S(1)} %get-tuple-element.550), channel_id=1, source_target_pairs={{0,16},{4,20},{8,24},{12,28},{16,0},{20,4},{24,8},{28,12},{1,17},{... | collective-permute-start | bytes 49160 | tf_op jit(solution)/shard_map/ppermute | solution.py:678
  662.6 52.3 %collective-permute-start.50 = (f32[32,128]{1,0:T(8,128)S(1)}, f32[32,128]{1,0:T(8,128)S(1)}, u32[]{:S(2)}, u32[]{:S(2)}) collective-permute-start(f32[32,128]{1,0:T(8,128)S(1)} %get-tuple-element.549), channel_id=1, source_target_pairs={{0,24},{4,28},{8,0},{12,4},{16,8},{20,12},{24,16},{28,20},{1,25},{... | collective-permute-start | bytes 49160 | tf_op jit(solution)/shard_map/ppermute | solution.py:678
  (108 other events, 1530.4 us)

commit v3 on v2

--- a/solution.py
+++ b/solution.py
@@ -422,19 +422,18 @@
     return jax.ShapeDtypeStruct(shape, jnp.bfloat16)
 
 
-def expert_fwd(place, chips, rows, meta, router_rows, toks, cots, w_gate, w_up, w_down, buffers):
+def expert_fwd(place, rows, meta, router_rows, toks, cots, w_gate, w_up, w_down):
     count = toks[0].shape[0]
     width = w_gate.shape[2]
     wide = width // FT
     deep = D // FT
     once = pl.Buffered(1)
     whole = lambda *shape: pl.BlockSpec(shape, lambda j: (0,) * len(shape), pipeline_mode=once)
-    mine = pl.BlockSpec((2 * rows, D), lambda j: (place, 0), pipeline_mode=once)
+    mine = whole(2 * rows, D)
     one = lambda j: jnp.minimum(j, wide - 1)
     two = lambda j: jnp.maximum(j - wide, 0)
-    strip = pl.BlockSpec((2 * rows, FT), lambda j: (place, one(j)))
-    total = 2 * chips * rows
-    buffers = () if buffers is None else tuple(buffers)
+    strip = pl.BlockSpec((2 * rows, FT), lambda j: (0, one(j)))
+    total = 2 * rows
     return pl.pallas_call(
         expert_fwd_kernel,
         grid=(wide + deep,),
@@ -442,8 +441,7 @@
         + [whole(count, D)] * 2
         + [pl.BlockSpec((count, FT), lambda j: (0, two(j)))] * 2
         + [pl.BlockSpec((1, D, FT), lambda j: (0, 0, one(j)))] * 2
-        + [pl.BlockSpec((1, width, FT), lambda j: (0, 0, two(j)))]
-        + [pl.BlockSpec(memory_space=pl.ANY)] * len(buffers),
+        + [pl.BlockSpec((1, width, FT), lambda j: (0, 0, two(j)))],
         out_specs=[
             mine,
             mine,
@@ -464,11 +462,10 @@
             pltpu.VMEM((2 * rows, width), jnp.bfloat16),
             pltpu.VMEM((2 * rows, 128), jnp.float32),
         ],
-        input_output_aliases={9 + n: n for n in range(len(buffers))},
         compiler_params=pltpu.CompilerParams(vmem_limit_bytes=VMEM_MOST),
         cost_estimate=LIGHT,
         name=f"expert_fwd_{place}",
-    )(meta, router_rows, *toks, *cots, w_gate, w_up, w_down, *buffers)
+    )(meta, router_rows, *toks, *cots, w_gate, w_up, w_down)
 
 
 def expert_bwd(place, rows, meta, gc, slope, act, w_gate, w_up, w_down):
@@ -479,13 +476,13 @@
     once = pl.Buffered(1)
     one = lambda j: jnp.minimum(j, wide - 1)
     two = lambda j: jnp.maximum(j - wide, 0)
-    strip = pl.BlockSpec((2 * rows, FT), lambda j: (place, one(j)))
+    strip = pl.BlockSpec((2 * rows, FT), lambda j: (0, one(j)))
     return pl.pallas_call(
         expert_bwd_kernel,
         grid=(wide + deep,),
         in_specs=[
             pl.BlockSpec((2, 8, count), lambda j: (0, 0, 0), pipeline_mode=once),
-            pl.BlockSpec((2 * rows, D), lambda j: (place, 0), pipeline_mode=once),
+            pl.BlockSpec((2 * rows, D), lambda j: (0, 0), pipeline_mode=once),
             strip,
             strip,
             pl.BlockSpec((1, FT, D), lambda j: (0, one(j), 0)),
@@ -499,64 +496,89 @@
             pltpu.VMEM((2 * rows, width), jnp.bfloat16),
             pltpu.VMEM((2 * rows, width), jnp.bfloat16),
         ],
-        input_output_aliases={2: 0, 3: 1},
         compiler_params=pltpu.CompilerParams(vmem_limit_bytes=VMEM_MOST),
         cost_estimate=LIGHT,
         name=f"expert_bwd_{place}",
     )(meta, gc, slope, act, w_down, w_gate, w_up)
 
 
-def grad_down_kernel(left_ref, right_ref, out_ref, turned_s):
+def turn_into(turned_s, refs):
+    first = 0
+    for ref in refs:
+        turned_s[:, first : first + ref.shape[0]] = jnp.transpose(ref[...])
+        first += ref.shape[0]
+
+
+def row_sums(turned_s, refs):
+    first, out = 0, None
+    for ref in refs:
+        part = dot_nn(turned_s[:, first : first + ref.shape[0]], ref[...])
+        out = part if out is None else out + part
+        first += ref.shape[0]
+    return out
+
+
+def grad_down_kernel(*refs):
+    out_ref, turned_s = refs[-2:]
+    many = (len(refs) - 2) // 2
+
     @pl.when(pl.program_id(0) == 0)
     def _():
-        turned_s[...] = jnp.transpose(left_ref[...])
-
-    tile = dot_nn(turned_s[...], right_ref[...])
-    out_ref[...] = jnp.transpose(tile).astype(jnp.bfloat16)
-
-
-def grad_in_kernel(left_ref, gate_ref, up_ref, out_gate_ref, out_up_ref, turned_s):
+        turn_into(turned_s, refs[:many])
+
+    out_ref[...] = jnp.transpose(row_sums(turned_s, refs[many : 2 * many])).astype(jnp.bfloat16)
+
+
+def grad_in_kernel(*refs):
+    out_gate_ref, out_up_ref, turned_s = refs[-3:]
+    many = (len(refs) - 3) // 3
+
     @pl.when(pl.program_id(0) == 0)
     def _():
-        turned_s[...] = jnp.transpose(left_ref[...])
-
-    out_gate_ref[...] = dot_nn(turned_s[...], gate_ref[...]).astype(jnp.bfloat16)
-    out_up_ref[...] = dot_nn(turned_s[...], up_ref[...]).astype(jnp.bfloat16)
+        turn_into(turned_s, refs[:many])
+
+    out_gate_ref[...] = row_sums(turned_s, refs[many : 2 * many]).astype(jnp.bfloat16)
+    out_up_ref[...] = row_sums(turned_s, refs[2 * many : 3 * many]).astype(jnp.bfloat16)
 
 
 def grad_down(gc, hidden):
-    total, width = hidden.shape
+    rows, width = hidden[0].shape
+    once = pl.Buffered(1)
     return pl.pallas_call(
         grad_down_kernel,
         grid=(width // FT,),
-        in_specs=[pl.BlockSpec((total, D), lambda j: (0, 0)), pl.BlockSpec((total, FT), lambda j: (0, j))],
+        in_specs=[pl.BlockSpec((rows, D), lambda j: (0, 0), pipeline_mode=once)] * len(gc)
+        + [pl.BlockSpec((rows, FT), lambda j: (0, j))] * len(gc),
         out_specs=pl.BlockSpec((FT, D), lambda j: (j, 0)),
-        out_shape=jax.ShapeDtypeStruct((width, D), jnp.bfloat16),
-        scratch_shapes=[pltpu.VMEM((D, total), jnp.bfloat16)],
+        out_shape=low_shape(width, D),
+        scratch_shapes=[pltpu.VMEM((D, rows * len(gc)), jnp.bfloat16)],
         compiler_params=pltpu.CompilerParams(vmem_limit_bytes=VMEM_LIMIT),
         cost_estimate=LIGHT,
         name="grad_down",
-    )(gc, hidden)
-
-
-def grad_in(rows, dgate, dup):
-    total, width = dgate.shape
-    strip = pl.BlockSpec((total, FT), lambda j: (0, j))
+    )(*gc, *hidden)
+
+
+def grad_in(xs, dgate, dup):
+    rows, width = dgate[0].shape
+    once = pl.Buffered(1)
     out = pl.BlockSpec((D, FT), lambda j: (0, j))
     return pl.pallas_call(
         grad_in_kernel,
         grid=(width // FT,),
-        in_specs=[pl.BlockSpec((total, D), lambda j: (0, 0)), strip, strip],
+        in_specs=[pl.BlockSpec((rows, D), lambda j: (0, 0), pipeline_mode=once)] * len(xs)
+        + [pl.BlockSpec((rows, FT), lambda j: (0, j))] * (2 * len(xs)),
         out_specs=[out, out],
-        out_shape=[jax.ShapeDtypeStruct((D, width), jnp.bfloat16)] * 2,
-        scratch_shapes=[pltpu.VMEM((D, total), jnp.bfloat16)],
+        out_shape=[low_shape(D, width)] * 2,
+        scratch_shapes=[pltpu.VMEM((D, rows * len(xs)), jnp.bfloat16)],
         compiler_params=pltpu.CompilerParams(vmem_limit_bytes=VMEM_LIMIT),
         cost_estimate=LIGHT,
         name="grad_in",
-    )(rows, dgate, dup)
-
-
-def grad_half_kernel(left_ref, right_ref, out_ref, turned_s):
+    )(*xs, *dgate, *dup)
+
+
+def grad_half_kernel(left_ref, right_ref, *rest):
+    out_ref, turned_s = rest[-2:]
+
     @pl.when(pl.program_id(0) == 0)
     def _():
         turned_s[...] = jnp.transpose(left_ref[...])
@@ -564,19 +586,22 @@
     out_ref[...] = dot_nn(turned_s[...], right_ref[...]).astype(jnp.bfloat16)
 
 
-def grad_rows(left, right, name):
+def grad_rows(left, right, name, wide=None, first=0, buffer=None):
     count, width = right.shape
+    buffers = () if buffer is None else (buffer,)
     return pl.pallas_call(
         grad_half_kernel,
         grid=(width // 512,),
-        in_specs=[pl.BlockSpec((count, D), lambda j: (0, 0)), pl.BlockSpec((count, 512), lambda j: (0, j))],
-        out_specs=pl.BlockSpec((D, 512), lambda j: (0, j)),
-        out_shape=jax.ShapeDtypeStruct((D, width), jnp.bfloat16),
+        in_specs=[pl.BlockSpec((count, D), lambda j: (0, 0)), pl.BlockSpec((count, 512), lambda j: (0, j))]
+        + [pl.BlockSpec(memory_space=pl.ANY)] * len(buffers),
+        out_specs=pl.BlockSpec((D, 512), lambda j: (0, first // 512 + j)),
+        out_shape=jax.ShapeDtypeStruct((D, wide or width), jnp.bfloat16),
         scratch_shapes=[pltpu.VMEM((D, count), jnp.bfloat16)],
+        input_output_aliases={2: 0} if buffers else {},
         compiler_params=pltpu.CompilerParams(vmem_limit_bytes=VMEM_LIMIT),
         cost_estimate=LIGHT,
         name=name,
-    )(left, right)
+    )(left, right, *buffers)
 
 
 def grad_normed_kernel(first_ref, second_ref, w_ref, out_ref):
@@ -670,13 +695,18 @@
     )
 
 
-def swapped(x, level):
+def swapped(x, level, steps=None):
     axis, size, place, pairs = level
-    out = [lax.dynamic_index_in_dim(x, place, 0, keepdims=False)]
-    for step in range(1, size):
+    out = [] if steps else [lax.dynamic_index_in_dim(x, place, 0, keepdims=False)]
+    for step in steps or range(1, size):
         sent = lax.dynamic_index_in_dim(x, (place + step) % size, 0, keepdims=False)
         out.append(lax.ppermute(sent, axis, pairs(step)))
     return out
+
+
+def whole_swapped(x, level):
+    axis, size, place, pairs = level
+    return [x] + [lax.ppermute(x, axis, pairs(step)) for step in range(1, size)]
 
 
 def total(arrays):
@@ -779,19 +809,17 @@
     tok_far = [from_chip(routed_low, n) for n in range(1, chips)]
     cots = [(cotangent, cot_sib)] + [(far, to_sibling(far)) for far in cot_far]
     pair = (routed_low, to_sibling(routed_low))
-    made = expert_fwd(0, chips, capacity, metas[0], router_rows, pair, cots[0], *weights, None)
+    made = expert_fwd(0, capacity, metas[0], router_rows, pair, cots[0], *weights)
     made, tok_far, cots = tie(made, tok_far, cots)
     toks = [(far, to_sibling(far)) for far in tok_far]
     outs, dots = [made[5:7]], [(made[7][0], made[7][1])]
-    buffers = made[:5]
+    kept = [made[:5]]
     for away in range(1, chips):
-        made = expert_fwd(
-            away, chips, capacity, metas[away], router_rows, toks[away - 1], cots[away], *weights, buffers
-        )
-        buffers = made[:5]
+        made = expert_fwd(away, capacity, metas[away], router_rows, toks[away - 1], cots[away], *weights)
+        kept.append(made[:5])
         outs.append(made[5:7])
         dots.append((made[7][0], made[7][1]))
-    rows_in, rows_out, hidden, slope, act = buffers
+    rows_in, rows_out, hidden, slope, act = [list(x) for x in zip(*kept)]
 
     met = [[to_sibling(other) for mine, other in part] for part in (dots, outs)]
     down_low = grad_down(rows_out, hidden)
@@ -806,12 +834,14 @@
     down_near = near_swapped(down_low)
     grads = [None] * chips
     for away in reversed(range(1, chips)):
-        slope, act, *grads[away] = expert_bwd(away, capacity, metas[away], rows_out, slope, act, *weights)
+        slope[away], act[away], *grads[away] = expert_bwd(
+            away, capacity, metas[away], rows_out[away], slope[away], act[away], *weights
+        )
     slope, far_outs, far_dots = tie(slope, far_outs, far_dots)
     far_grads = []
     for away in range(1, chips):
         far_grads += [from_chip(grads[away][0], chips - away), from_chip(grads[away][1], chips - away, 1)]
-    slope, act, *here = expert_bwd(0, capacity, metas[0], rows_out, slope, act, *weights)
+    slope[0], act[0], *here = expert_bwd(0, capacity, metas[0], rows_out[0], slope[0], act[0], *weights)
     slope, down_near = tie(slope, down_near)
     down_near = low_total(down_near)
     slope, down_near = tie(slope, down_near)
@@ -842,26 +872,30 @@
 
     grad_attended, grad_branch, block_out = tie(grad_attended, grad_branch, block_out)
     first = attn_bwd(span_starts, qkv, grad_attended, attended_low, lse, diag, 0)
-    half_first = grad_rows(normed_low, first[0], "grad_qkv_0")
-    grad_w_out = grad_rows(attended_low, grad_branch, "grad_out")
-    half_first, grad_w_out, grad_attended, gate_near, down_far = tie(
-        half_first, grad_w_out, grad_attended, gate_near, down_far
-    )
+    early = grad_rows(attended_low, grad_branch, "grad_out", 5 * D // 2, 3 * D // 2)
+    early = grad_rows(normed_low, first[0], "grad_qkv_0", 5 * D // 2, 0, early)
+    early, grad_attended, gate_near, down_far = tie(early, grad_attended, gate_near, down_far)
     gate_near = low_total(gate_near)
     sum_down = total(down_far)
-    gate_near, grad_attended, sum_down = tie(gate_near, grad_attended, sum_down)
+    gate_near, grad_attended, sum_down, up_low = tie(gate_near, grad_attended, sum_down, up_low)
     gate_far = swapped(gate_near, outer)
     up_near = near_swapped(up_low)
-    early = [rows_swapped(x, core) for x in (half_first, grad_w_out)]
+    early = rows_swapped(early, core)
     second = attn_bwd(span_starts, qkv, grad_attended, attended_low, lse, diag, 1)
-    second, early = tie(second, early)
-    early = tie(*[low_total(x) for x in early])
-    early = [rows_swapped(x, chip) for x in early]
+    second, early, gate_far, up_near = tie(second, early, gate_far, up_near)
+    second = list(second)
+    up_near, early = tie(low_total(up_near), low_total(early))
+    early = rows_swapped(early, chip)
+    own = lax.dynamic_index_in_dim(up_near, levels()[3][2], 0, keepdims=False)
+    up_far = swapped(up_near, outer, (1, OUTER - 1))
     half_second = grad_rows(normed_low, second[0], "grad_qkv_1")
+    late = rows_swapped(half_second, core)
+    half_second, *second[:1] = tie(half_second, second[0])
     grad_normed = grad_normed_of(first[0], second[0], w_qkv)
-    half_second, grad_normed, early, gate_far, up_near = tie(half_second, grad_normed, early, gate_far, up_near)
-    up_near = low_total(up_near)
-    early = [low_total(x) for x in early]
+    late, grad_normed, early, up_far = tie(late, grad_normed, early, up_far)
+    early, late = tie(low_total(early), low_total(late))
+    late = rows_swapped(late, inner)
+    last = swapped(up_near, outer, tuple(range(2, OUTER - 1)))
     grad_norm_attn, grad_gain_attn = rms_backward(token_float, scale_attn, gain_attn, grad_normed)
     grad_tokens = grad_mixed + grad_norm_attn
     grad_rel_table = rel_grad(jnp.concatenate([first[1], second[1]]), jnp.concatenate([first[2], second[2]]))
@@ -873,27 +907,27 @@
             grad_gain_moe[None],
         ]
     )
-    small = jnp.pad(jnp.transpose(small), ((0, 0), (0, 128 - small.shape[0])))
-    up_near, half_second, small, early, grad_tokens = tie(up_near, half_second, small, early, grad_tokens)
-    up_far = swapped(up_near, outer)
-    late = tie(*[rows_swapped(x, core) for x in (half_second, small)])
-    late = [low_total(x) for x in late]
-    late = tie(*[rows_swapped(x, inner) for x in late])
-    late, early = tie([low_total(x) for x in late], early)
-    late, early = tie([rows_swapped(x, chip) for x in late], [rows_swapped(x, inner) for x in early])
-    both = tie(*[low_total(x) for x in (*early, *late)])
-    both, up_far = tie([rows_swapped(x, outer) for x in both], up_far)
-    both = tie(*[low_total(x) for x in both])
-    both = tie(*[collected(x, outer) for x in both])
-    both = tie(*[collected(x, level) for x, level in zip(both, (inner, inner, chip, chip))])
-    both = tie(*[collected(x, level) for x, level in zip(both, (chip, chip, inner, inner))])
-    both = tie(*[collected(x, core) for x in both])
-    sum_first, sum_w_out, sum_second, small = [x.astype(jnp.float32) for x in both]
+    late, small, grad_tokens = tie(late, small, grad_tokens)
+    late, early = tie(low_total(late), early)
+    small = whole_swapped(small, core)
+    late, early, last, small = tie(rows_swapped(late, chip), rows_swapped(early, inner), last, small)
+    wide = early[0].shape[1]
+    both, small = tie(jnp.concatenate([low_total(early), low_total(late)], axis=1), total(small))
+    both, small = tie(rows_swapped(both, outer), whole_swapped(small, chip))
+    both, small = tie(low_total(both), total(small))
+    both, small = tie(collected(both, outer), whole_swapped(small, inner))
+    early, late, small = tie(both[:, :wide], both[:, wide:], total(small))
+    early, late, small = tie(collected(early, inner), collected(late, chip), whole_swapped(small, outer))
+    small = total(small)
+    early, late = tie(collected(early, chip), collected(late, inner))
+    early, late = tie(collected(early, core), collected(late, core))
+    sum_first, sum_second = early[:, : 3 * D // 2].astype(jnp.float32), late.astype(jnp.float32)
+    sum_w_out = early[:, 3 * D // 2 :].astype(jnp.float32)
+    up_far = [own] + up_far + last
     sum_gate, sum_up = total(gate_far), total(up_far)
     sum_w_qkv = jnp.concatenate(
         [x[:, n * D // 2 : (n + 1) * D // 2] for n in range(3) for x in (sum_first, sum_second)], axis=1
     )
-    small = jnp.transpose(small)
     small = (
         small[experts, : BUCKETS * H].reshape(BUCKETS, H),
         jnp.transpose(small[:experts]),

time: 833 us -> 794 us (0.953)
  starting transfers between devices: 118 us -> 72.8 us
  waiting for transfers between devices: 132 us -> 141 us
    ppermute x36 -> x21, starting transfers between devices: 79.6 us -> 31.3 us  [swapped(): out.append(lax.ppermute(sent, axis, pairs(step)))]
    ppermute x0 -> x6, starting transfers between devices: none -> 10.8 us  [whole_swapped(): return [x] + [lax.ppermute(x, axis, pairs(step)) for step in range(1, size)]]
    ppermute x12 -> x6, waiting for transfers between devices: 31.3 us -> 41.4 us  [collected(): other = lax.ppermute(x, axis, pairs(1))]
    ppermute x36 -> x21, waiting for transfers between devices: 80.8 us -> 73.9 us  [swapped(): out.append(lax.ppermute(sent, axis, pairs(step)))]
    convert_element_type x15 -> x10, other arithmetic: 18.6 us -> 16.2 us  [low_total(): return total(arrays).astype(arrays[0].dtype)]
    squeeze x20 -> x13, local copies, waits for them, and re-layouts: 26.5 us -> 27 us  [swapped(): sent = lax.dynamic_index_in_dim(x, (place + step) % size, 0, keepdims=False)]
  transfers between devices with their start and end apart: 78 -> 54, of which waited for: 26 -> 19; matrix products, arithmetic and copies ran while one was open for 10% -> 10% of each run, Pallas kernels for 52% -> 54%
where the time goes in v3:
time: 794 us; the launch traced here: 784 us
  Pallas kernels  431 us (54%)
  waiting for transfers between devices  141 us (18%)
  starting transfers between devices  72.8 us (9%)
  other arithmetic  71.4 us (9%)
  local copies, waits for them, and re-layouts  42.5 us (5%)
  matrix products  24.4 us (3%)
    pallas_call x2, Pallas kernels, expert_fwd(): pl.pallas_call(expert_fwd_kernel, grid=(wide + deep,), in_specs=[whole(2,...  136 us
    pallas_call x2, Pallas kernels, expert_bwd(): pl.pallas_call(expert_bwd_kernel, grid=(wide + deep,), in_specs=[pl.Block...  93.3 us
    ppermute x21, waiting for transfers between devices, swapped(): out.append(lax.ppermute(sent, axis, pairs(step)))  73.9 us
    pallas_call x2, Pallas kernels, attn_bwd(): pl.pallas_call(attn_bwd_kernel, grid=(pairs, 3), in_specs=[pl.BlockSpec(m...  64.3 us
    ppermute x6, waiting for transfers between devices, collected(): other = lax.ppermute(x, axis, pairs(1))  41.4 us
    pallas_call x1, Pallas kernels, attn_fwd(): pl.pallas_call(attn_fwd_kernel, grid=(H // 2,), in_specs=[pl.BlockSpec(me...  40 us
    pallas_call x1, Pallas kernels, grad_in(): pl.pallas_call(grad_in_kernel, grid=(width // FT,), in_specs=[pl.BlockSpe...  38.2 us
    ppermute x21, starting transfers between devices, swapped(): out.append(lax.ppermute(sent, axis, pairs(step)))  31.3 us
  transfers between devices with their start and end apart: 54, of which 19 were waited for; matrix products, arithmetic and copies ran while one was open for 10% of the time, Pallas kernels for 54%

profile of v3, /device:TPU:0, one launch (start us, length us, event | category | flops | bytes accessed | tf_op | source)
XLA Modules:
  0.0 784.4 jit_solution(15270305559771098894)
XLA Ops:
  16.2 12.1 %convolution_convert_fusion.q_ref.k_ref.v_ref = bf16[1024,3072]{1,0:T(8,128)(2,1)} fusion(bf16[1024,1024]{1,0:T(8,128)(2,1)S(1)} %fusion.2.left_ref, bf16[1024,3072]{1,0:T(8,128)(2,1)} %w_ref.1), kind=kOutput, calls=%fused_computation.10 | convolution fusion | flops 6445596672 | bytes 14680064 | tf_op jit(solution)/shard_map/dot_general | solution.py:794
  29.4 40.0 %attn_fwd.1 = (bf16[1024,1024]{1,0:T(8,128)(2,1)}, f32[8,2,1024]{2,1,0:T(2,128)}) custom-call(s32[1,2]{1,0:T(1,128)} %span_ref.5, bf16[1024,3072]{1,0:T(8,128)(2,1)} %convolution_convert_fusion.q_ref.k_ref.v_ref, bf16[1024,3072]{1,0:T(8,128)(2,1)} %convolution_convert_fusion.q_ref.k_ref.v_ref, bf16[1024,3072]{1,0:T(8,128)(2,1)} %convolution_convert_fusion.q_ref.k_ref.v_ref, ...), custom_call_target="tpu_custom_call" | custom-call | flops 1000 | bytes 1000 | tf_op jit(solution)/shard_map/attn_fwd/pallas_call | solution.py:144
  80.7 62.1 %expert_fwd_0.1 = (bf16[1280,1024]{1,0:T(8,128)(2,1)}, bf16[1280,1024]{1,0:T(8,128)(2,1)}, bf16[1280,2816]{1,0:T(8,128)(2,1)}, bf16[1280,2816]{1,0:T(8,128)(2,1)...) custom-call(s32[2,8,1024]{2,1,0:T(8,128)} %get-tuple-element.207.met, ...), custom_call_target="tpu_custom_call" | custom-call | flops 1000 | bytes 1000 | tf_op jit(solution)/shard_map/expert_fwd_0/pallas_call | solution.py:437
  148.1 73.8 %expert_fwd_1.1 = (bf16[1280,1024]{1,0:T(8,128)(2,1)}, bf16[1280,1024]{1,0:T(8,128)(2,1)}, bf16[1280,2816]{1,0:T(8,128)(2,1)}, bf16[1280,2816]{1,0:T(8,128)(2,1)...) custom-call(s32[2,8,1024]{2,1,0:T(8,128)} %get-tuple-element.219.met, ...), custom_call_target="tpu_custom_call" | custom-call | flops 1000 | bytes 1000 | tf_op jit(solution)/shard_map/expert_fwd_1/pallas_call | solution.py:437
  223.5 23.1 %grad_down.1 = bf16[2816,1024]{1,0:T(8,128)(2,1)} custom-call(bf16[1280,1024]{1,0:T(8,128)(2,1)} %get-tuple-element.218.refs_0_.gc_ref, bf16[1280,1024]{1,0:T(8,128)(2,1)} %get-tuple-element.223.refs_1_.gc_ref, bf16[1280,2816]{1,0:T(8,128)(2,1)} %get-tuple-element.224.refs_2_, bf16[1280,2816]{1,0:T(8,128)(2,1)} %get-tuple-element.225.refs_3_), custom_call_target="tpu_custom_call" | custom-call | flops 1000 | bytes 1000 | tf_op jit(solution)/shard_map/grad_down/pallas_call | solution.py:547
  260.7 46.5 %expert_bwd_1.1 = (bf16[1280,2816]{1,0:T(8,128)(2,1)}, bf16[1280,2816]{1,0:T(8,128)(2,1)}, bf16[1024,1024]{1,0:T(8,128)(2,1)}, bf16[1024,1024]{1,0:T(8,128)(2,1)}) custom-call(s32[2,8,1024]{2,1,0:T(8,128)} %get-tuple-element.219.meta_ref, bf16[1280,1024]{1,0:T(8,128)(2,1)} %get-tuple-element.223.refs_1_.gc_ref, ...), custom_call_target="tpu_custom_call" | custom-call | flops 1000 | bytes 1000 | tf_op jit(solution)/shard_map/expert_bwd_1/pallas_call | solution.py:480
  308.1 46.8 %expert_bwd_0.1 = (bf16[1280,2816]{1,0:T(8,128)(2,1)}, bf16[1280,2816]{1,0:T(8,128)(2,1)}, bf16[1024,1024]{1,0:T(8,128)(2,1)}, bf16[1024,1024]{1,0:T(8,128)(2,1)}) custom-call(s32[2,8,1024]{2,1,0:T(8,128)} %get-tuple-element.207.meta_ref, bf16[1280,1024]{1,0:T(8,128)(2,1)} %get-tuple-element.218.refs_0_.gc_ref, ...), custom_call_target="tpu_custom_call" | custom-call | flops 1000 | bytes 1000 | tf_op jit(solution)/shard_map/expert_bwd_0/pallas_call | solution.py:480
  362.7 38.2 %grad_in.1 = (bf16[1024,2816]{1,0:T(8,128)(2,1)}, bf16[1024,2816]{1,0:T(8,128)(2,1)}) custom-call(bf16[1280,1024]{1,0:T(8,128)(2,1)} %get-tuple-element.249.refs_0_, bf16[1280,1024]{1,0:T(8,128)(2,1)} %get-tuple-element.250.refs_1_, bf16[1280,2816]{1,0:T(8,128)(2,1)} %get-tuple-element.258.refs_2_, bf16[1280,2816]{1,0:T(8,128)(2,1)} %get-tuple-element.259.refs_3_, ...), custom_call_target="tpu_custom_call" | custom-call | flops 1000 | bytes 1000 | tf_op jit(solution)/shard_map/grad_in/pallas_call | solution.py:565
  414.1 8.0 %multiply_reduce_fusion = (f32[1024]{0:T(1024)S(1)}, f32[1024]{0:T(1024)S(1)}, f32[1024,1024]{1,0:T(8,128)S(1)}, bf16[1024,1024]{1,0:T(8,128)(2,1)}) fusion(f32[1024,1024]{1,0:T(8,128)S(1)} %copy-done.3, f32[1024]{0:T(1024)S(1)} %get-tuple-element.487, f32[1024]{0:T(1024)S(1)} %copy-done.38, f32[1024,1024]{1,0:T(8,128)S(1)} %fusion.38, ...), kind=kLoop, calls=%fused_computation.22 | loop fusion | flops 22018048 | bytes 29376512 | tf_op jit(solution)/shard_map/reduce_sum | solution.py:648
  434.5 32.4 %attn_bwd_0.1 = (bf16[1024,1536]{1,0:T(8,128)(2,1)}, f32[4,2,768]{2,1,0:T(2,128)}, f32[4,2,2,8,256]{4,3,2,1,0:T(8,128)}) custom-call(s32[1,2]{1,0:T(1,128)} %span_ref.5, bf16[1024,3072]{1,0:T(8,128)(2,1)} %convolution_convert_fusion.q_ref.k_ref.v_ref, bf16[1024,3072]{1,0:T(8,128)(2,1)} %convolution_convert_fusion.q_ref.k_ref.v_ref, ...), custom_call_target="tpu_custom_call" | custom-call | flops 1000 | bytes 1000 | tf_op jit(solution)/shard_map/attn_bwd_0/pallas_call | solution.py:248
  466.9 7.7 grad_qkv_0.1
  495.1 31.9 %attn_bwd_1.1 = (bf16[1024,1536]{1,0:T(8,128)(2,1)}, f32[4,2,768]{2,1,0:T(2,128)}, f32[4,2,2,8,256]{4,3,2,1,0:T(8,128)}) custom-call(s32[1,2]{1,0:T(1,128)} %span_ref.5, bf16[1024,3072]{1,0:T(8,128)(2,1)} %convolution_convert_fusion.q_ref.k_ref.v_ref, bf16[1024,3072]{1,0:T(8,128)(2,1)} %convolution_convert_fusion.q_ref.k_ref.v_ref, ...), custom_call_target="tpu_custom_call" | custom-call | flops 1000 | bytes 1000 | tf_op jit(solution)/shard_map/attn_bwd_1/pallas_call | solution.py:248
  527.1 14.1 %collective-permute-done.25 = bf16[128,2816]{1,0:T(8,128)(2,1)} collective-permute-done((bf16[128,2816]{1,0:T(8,128)(2,1)}, bf16[128,2816]{1,0:T(8,128)(2,1)}, u32[]{:S(2)}, u32[]{:S(2)}) %collective-permute-start.25) | collective-permute-done | bytes 720928 | tf_op jit(solution)/shard_map/ppermute | solution.py:703
  552.6 8.7 %grad_qkv_1.1 = bf16[1024,1536]{1,0:T(8,128)(2,1)} custom-call(bf16[1024,1024]{1,0:T(8,128)(2,1)} %copy-done.10, bf16[1024,1536]{1,0:T(8,128)(2,1)} %get-tuple-element.299.right_ref.second_ref), custom_call_target="tpu_custom_call" | custom-call | flops 1000 | bytes 1000 | tf_op jit(solution)/shard_map/grad_qkv_1/pallas_call | solution.py:592
  568.7 9.6 %collective-permute-start.30 = (bf16[128,2816]{1,0:T(8,128)(2,1)}, bf16[128,2816]{1,0:T(8,128)(2,1)}, u32[]{:S(2)}, u32[]{:S(2)}) collective-permute-start(bf16[128,2816]{1,0:T(8,128)(2,1)} %get-tuple-element.437), channel_id=1, source_target_pairs={{0,8},{4,12},{8,16},{12,20},{16,24},{20,28},{24,0},{28,4},{1,9},{5... | collective-permute-start | bytes 2162696 | tf_op jit(solution)/shard_map/ppermute | solution.py:703
  578.6 13.5 %grad_normed.1 = f32[1024,1024]{1,0:T(8,128)} custom-call(bf16[1024,1536]{1,0:T(8,128)(2,1)} %get-tuple-element.279.right_ref.first_ref, bf16[1024,1536]{1,0:T(8,128)(2,1)} %get-tuple-element.299.right_ref.second_ref, bf16[1024,3072]{1,0:T(8,128)(2,1)} %w_ref.1), custom_call_target="tpu_custom_call" | custom-call | flops 1000 | bytes 1000 | tf_op jit(solution)/shard_map/grad_normed/pallas_call | solution.py:626
  596.2 14.4 %collective-permute-done.31 = bf16[128,2816]{1,0:T(8,128)(2,1)} collective-permute-done((bf16[128,2816]{1,0:T(8,128)(2,1)}, bf16[128,2816]{1,0:T(8,128)(2,1)}, u32[]{:S(2)}, u32[]{:S(2)}) %collective-permute-start.31) | collective-permute-done | bytes 720928 | tf_op jit(solution)/shard_map/ppermute | solution.py:703
  622.2 15.2 %collective-permute-done.32 = bf16[256,1536]{1,0:T(8,128)(2,1)S(1)} collective-permute-done((bf16[256,1536]{1,0:T(8,128)(2,1)S(1)}, bf16[256,1536]{1,0:T(8,128)(2,1)S(1)}, u32[]{:S(2)}, u32[]{:S(2)}) %collective-permute-start.32) | collective-permute-done | bytes 786464 | tf_op jit(solution)/shard_map/ppermute | solution.py:703
  664.9 8.2 %collective-permute-done.38 = bf16[32,4096]{1,0:T(8,128)(2,1)S(1)} collective-permute-done((bf16[32,4096]{1,0:T(8,128)(2,1)S(1)}, bf16[32,4096]{1,0:T(8,128)(2,1)S(1)}, u32[]{:S(2)}, u32[]{:S(2)}) %collective-permute-start.38) | collective-permute-done | bytes 262176 | tf_op jit(solution)/shard_map/ppermute | solution.py:703
  673.2 11.7 %collective-permute-start.41 = (bf16[32,4096]{1,0:T(8,128)(2,1)S(1)}, bf16[32,4096]{1,0:T(8,128)(2,1)S(1)}, u32[]{:S(2)}, u32[]{:S(2)}) collective-permute-start(bf16[32,4096]{1,0:T(8,128)(2,1)S(1)} %add_convert_fusion.11), channel_id=1, source_target_pairs={{0,8},{4,12},{8,16},{12,20},{16,24},{20,28},{24,0},{28,4},{1,9},{5... | collective-permute-start | bytes 786440 | tf_op jit(solution)/shard_map/ppermute | solution.py:727
  691.6 7.6 collective-permute-done.42
  713.7 13.9 %collective-permute-done.45 = bf16[128,2560]{1,0:T(8,128)(2,1)S(1)} collective-permute-done((bf16[128,2560]{1,0:T(8,128)(2,1)S(1)}, bf16[128,2560]{1,0:T(8,128)(2,1)S(1)}, u32[]{:S(2)}, u32[]{:S(2)}) %collective-permute-start.45) | collective-permute-done | bytes 655392 | tf_op jit(solution)/shard_map/ppermute | solution.py:723
  729.7 15.4 %collective-permute-done.51 = bf16[256,1536]{1,0:T(8,128)(2,1)S(1)} collective-permute-done((bf16[256,1536]{1,0:T(8,128)(2,1)S(1)}, bf16[256,1536]{1,0:T(8,128)(2,1)S(1)}, u32[]{:S(2)}, u32[]{:S(2)}) %collective-permute-start.51) | collective-permute-done | bytes 786464 | tf_op jit(solution)/shard_map/ppermute | solution.py:723
  745.3 12.1 %collective-permute-done.50 = bf16[256,2560]{1,0:T(8,128)(2,1)} collective-permute-done((bf16[256,2560]{1,0:T(8,128)(2,1)S(1)}, bf16[256,2560]{1,0:T(8,128)(2,1)}, u32[]{:S(2)}, u32[]{:S(2)}) %collective-permute-start.50) | collective-permute-done | bytes 1310752 | tf_op jit(solution)/shard_map/ppermute | solution.py:723
  (325 shorter events, 215.4 us)
Async XLA Ops:
  7.2 62.3 %collective-permute-start.3 = (s32[6,1024]{1,0:T(8,128)S(1)}, s32[6,1024]{1,0:T(8,128)S(1)}, u32[]{:S(2)}, u32[]{:S(2)}) collective-permute-start(s32[6,1024]{1,0:T(8,128)S(1)} %pad_add_fusion.2), channel_id=1, source_target_pairs={{0,2},{1,3},{2,0},{3,1},{4,6},{5,7},{6,4},{7,5},{8,10},{9,11},{10,... | collective-permute-start | bytes 73736 | tf_op jit(solution)/shard_map/ppermute | solution.py:664
  10.2 59.3 %collective-permute-start.4 = (s32[6,1024]{1,0:T(8,128)S(1)}, s32[6,1024]{1,0:T(8,128)S(1)}, u32[]{:S(2)}, u32[]{:S(2)}) collective-permute-start(s32[6,1024]{1,0:T(8,128)S(1)} %pad_add_fusion.2), channel_id=1, source_target_pairs={{0,3},{1,2},{2,1},{3,0},{4,7},{5,6},{6,5},{7,4},{8,11},{9,10},{10,... | collective-permute-start | bytes 73736 | tf_op jit(solution)/shard_map/ppermute | solution.py:664
  10.2 59.4 %collective-permute-start.2 = (s32[6,1024]{1,0:T(8,128)S(1)}, s32[6,1024]{1,0:T(8,128)S(1)}, u32[]{:S(2)}, u32[]{:S(2)}) collective-permute-start(s32[6,1024]{1,0:T(8,128)S(1)} %pad_add_fusion.2), channel_id=1, source_target_pairs={{0,1},{1,0},{2,3},{3,2},{4,5},{5,4},{6,7},{7,6},{8,9},{9,8},{10,11... | collective-permute-start | bytes 73736 | tf_op jit(solution)/shard_map/ppermute | solution.py:659
  10.3 60.0 %collective-permute-start = (bf16[1024,1024]{1,0:T(8,128)(2,1)}, bf16[1024,1024]{1,0:T(8,128)(2,1)}, u32[]{:S(2)}, u32[]{:S(2)}) collective-permute-start(bf16[1024,1024]{1,0:T(8,128)(2,1)} %cot_a.1), channel_id=1, source_target_pairs={{0,1},{1,0},{2,3},{3,2},{4,5},{5,4},{6,7},{7,6},{8,9},{9,8},{10,11... | collective-permute-start | bytes 6291464 | tf_op jit(solution)/shard_map/ppermute | solution.py:659
  10.7 59.7 %collective-permute-start.1 = (bf16[1024,1024]{1,0:T(8,128)(2,1)}, bf16[1024,1024]{1,0:T(8,128)(2,1)}, u32[]{:S(2)}, u32[]{:S(2)}) collective-permute-start(bf16[1024,1024]{1,0:T(8,128)(2,1)} %cot_a.1), channel_id=1, source_target_pairs={{0,2},{1,3},{2,0},{3,1},{4,6},{5,7},{6,4},{7,5},{8,10},{9,11},{10,... | collective-permute-start | bytes 6291464 | tf_op jit(solution)/shard_map/ppermute | solution.py:664
  76.7 66.2 %collective-permute-start.6 = (bf16[1024,1024]{1,0:T(8,128)(2,1)S(1)}, bf16[1024,1024]{1,0:T(8,128)(2,1)}, u32[]{:S(2)}, u32[]{:S(2)}) collective-permute-start(bf16[1024,1024]{1,0:T(8,128)(2,1)S(1)} %multiply_convert_fusion.tok_a), channel_id=1, source_target_pairs={{0,2},{1,3},{2,0},{3,1},{4,6},{5,7},{6,4},{7,5},{8,10},{9,11},{10,... | collective-permute-start | bytes 6291464 | tf_op jit(solution)/shard_map/ppermute | solution.py:664
  76.9 65.9 %collective-permute-start.7 = (bf16[1024,1024]{1,0:T(8,128)(2,1)}, bf16[1024,1024]{1,0:T(8,128)(2,1)}, u32[]{:S(2)}, u32[]{:S(2)}) collective-permute-start(bf16[1024,1024]{1,0:T(8,128)(2,1)} %collective-permute-done.1.cot_a), channel_id=1, source_target_pairs={{0,1},{1,0},{2,3},{3,2},{4,5},{5,4},{6,7},{7,6},{8,9},{9,8},{10,11... | collective-permute-start | bytes 6291464 | tf_op jit(solution)/shard_map/ppermute | solution.py:659
  143.2 103.4 %collective-permute-start.11 = (bf16[1024,1024]{1,0:T(8,128)(2,1)}, bf16[1024,1024]{1,0:T(8,128)(2,1)S(1)}, u32[]{:S(2)}, u32[]{:S(2)}) collective-permute-start(bf16[1024,1024]{1,0:T(8,128)(2,1)} %get-tuple-element.230), channel_id=1, source_target_pairs={{0,1},{1,0},{2,3},{3,2},{4,5},{5,4},{6,7},{7,6},{8,9},{9,8},{10,11... | collective-permute-start | bytes 6291464 | tf_op jit(solution)/shard_map/ppermute | solution.py:659
  251.3 56.8 %collective-permute-start.13 = (bf16[1024,1024]{1,0:T(8,128)(2,1)}, bf16[1024,1024]{1,0:T(8,128)(2,1)}, u32[]{:S(2)}, u32[]{:S(2)}) collective-permute-start(bf16[1024,1024]{1,0:T(8,128)(2,1)} %add_convert_fusion.5), channel_id=1, source_target_pairs={{0,2},{1,3},{2,0},{3,1},{4,6},{5,7},{6,4},{7,5},{8,10},{9,11},{10,... | collective-permute-start | bytes 6291464 | tf_op jit(solution)/shard_map/ppermute | solution.py:664
  258.7 99.9 %collective-permute-start.15 = (bf16[4,352,1024]{2,1,0:T(8,128)(2,1)}, bf16[4,352,1024]{2,1,0:T(8,128)(2,1)}, u32[]{:S(2)}, u32[]{:S(2)}) collective-permute-start(bf16[4,352,1024]{2,1,0:T(8,128)(2,1)} %get-tuple-element.424), channel_id=1, source_target_pairs={{0,4},{4,0},{8,12},{12,8},{16,20},{20,16},{24,28},{28,24},{1,5},{5... | collective-permute-start | bytes 8650760 | tf_op jit(solution)/shard_map/ppermute | solution.py:703
  259.3 48.8 %collective-permute-start.14 = (f32[8,1024]{1,0:T(8,128)S(1)}, f32[8,1024]{1,0:T(8,128)S(1)}, u32[]{:S(2)}, u32[]{:S(2)}) collective-permute-start(f32[8,1024]{1,0:T(8,128)S(1)} %add.342), channel_id=1, source_target_pairs={{0,2},{1,3},{2,0},{3,1},{4,6},{5,7},{6,4},{7,5},{8,10},{9,11},{10,... | collective-permute-start | bytes 98312 | tf_op jit(solution)/shard_map/ppermute | solution.py:664
  307.2 93.7 %collective-permute-start.16 = (bf16[1024,1024]{1,0:T(8,128)(2,1)}, bf16[1024,1024]{1,0:T(8,128)(2,1)}, u32[]{:S(2)}, u32[]{:S(2)}) collective-permute-start(bf16[1024,1024]{1,0:T(8,128)(2,1)} %get-tuple-element.264), channel_id=1, source_target_pairs={{0,2},{1,3},{2,0},{3,1},{4,6},{5,7},{6,4},{7,5},{8,10},{9,11},{10,... | collective-permute-start | bytes 6291464 | tf_op jit(solution)/shard_map/ppermute | solution.py:664
  307.8 93.1 %collective-permute-start.17 = (bf16[1024,1024]{1,0:T(8,128)(2,1)}, bf16[1024,1024]{1,0:T(8,128)(2,1)}, u32[]{:S(2)}, u32[]{:S(2)}) collective-permute-start(bf16[1024,1024]{1,0:T(8,128)(2,1)} %get-tuple-element.265), channel_id=1, source_target_pairs={{0,3},{1,2},{2,1},{3,0},{4,7},{5,6},{6,5},{7,4},{8,11},{9,10},{10,... | collective-permute-start | bytes 6291464 | tf_op jit(solution)/shard_map/ppermute | solution.py:664
  354.8 46.1 %collective-permute-start.18 = (bf16[1024,1024]{1,0:T(8,128)(2,1)}, bf16[1024,1024]{1,0:T(8,128)(2,1)}, u32[]{:S(2)}, u32[]{:S(2)}) collective-permute-start(bf16[1024,1024]{1,0:T(8,128)(2,1)} %get-tuple-element.266), channel_id=1, source_target_pairs={{0,1},{1,0},{2,3},{3,2},{4,5},{5,4},{6,7},{7,6},{8,9},{9,8},{10,11... | collective-permute-start | bytes 6291464 | tf_op jit(solution)/shard_map/ppermute | solution.py:659
  405.5 69.1 %collective-permute-start.19 = (bf16[4,128,2816]{2,1,0:T(8,128)(2,1)}, bf16[4,128,2816]{2,1,0:T(8,128)(2,1)}, u32[]{:S(2)}, u32[]{:S(2)}) collective-permute-start(bf16[4,128,2816]{2,1,0:T(8,128)(2,1)} %get-tuple-element.422), channel_id=1, source_target_pairs={{0,4},{4,0},{8,12},{12,8},{16,20},{20,16},{24,28},{28,24},{1,5},{5... | collective-permute-start | bytes 8650760 | tf_op jit(solution)/shard_map/ppermute | solution.py:703
  408.5 66.1 %collective-permute-start.20 = (bf16[352,1024]{1,0:T(8,128)(2,1)}, bf16[352,1024]{1,0:T(8,128)(2,1)S(1)}, u32[]{:S(2)}, u32[]{:S(2)}) collective-permute-start(bf16[352,1024]{1,0:T(8,128)(2,1)} %get-tuple-element.444), channel_id=1, source_target_pairs={{0,8},{4,12},{8,16},{12,20},{16,24},{20,28},{24,0},{28,4},{1,9},{5... | collective-permute-start | bytes 2162696 | tf_op jit(solution)/shard_map/ppermute | solution.py:703
  410.1 64.5 %collective-permute-start.21 = (bf16[352,1024]{1,0:T(8,128)(2,1)}, bf16[352,1024]{1,0:T(8,128)(2,1)}, u32[]{:S(2)}, u32[]{:S(2)}) collective-permute-start(bf16[352,1024]{1,0:T(8,128)(2,1)} %get-tuple-element.443), channel_id=1, source_target_pairs={{0,16},{4,20},{8,24},{12,28},{16,0},{20,4},{24,8},{28,12},{1,17},{... | collective-permute-start | bytes 2162696 | tf_op jit(solution)/shard_map/ppermute | solution.py:703
  412.7 61.9 %collective-permute-start.22 = (bf16[352,1024]{1,0:T(8,128)(2,1)}, bf16[352,1024]{1,0:T(8,128)(2,1)}, u32[]{:S(2)}, u32[]{:S(2)}) collective-permute-start(bf16[352,1024]{1,0:T(8,128)(2,1)} %get-tuple-element.442), channel_id=1, source_target_pairs={{0,24},{4,28},{8,0},{12,4},{16,8},{20,12},{24,16},{28,20},{1,25},{... | collective-permute-start | bytes 2162696 | tf_op jit(solution)/shard_map/ppermute | solution.py:703
  483.7 63.7 %collective-permute-start.27 = (bf16[4,128,2816]{2,1,0:T(8,128)(2,1)}, bf16[4,128,2816]{2,1,0:T(8,128)(2,1)}, u32[]{:S(2)}, u32[]{:S(2)}) collective-permute-start(bf16[4,128,2816]{2,1,0:T(8,128)(2,1)} %get-tuple-element.420), channel_id=1, source_target_pairs={{0,4},{4,0},{8,12},{12,8},{16,20},{20,16},{24,28},{28,24},{1,5},{5... | collective-permute-start | bytes 8650760 | tf_op jit(solution)/shard_map/ppermute | solution.py:703
  487.9 53.4 %collective-permute-start.23 = (bf16[512,2560]{1,0:T(8,128)(2,1)}, bf16[512,2560]{1,0:T(8,128)(2,1)}, u32[]{:S(2)}, u32[]{:S(2)}) collective-permute-start(bf16[512,2560]{1,0:T(8,128)(2,1)} %get-tuple-element.428), channel_id=1, source_target_pairs={{0,1},{1,0},{2,3},{3,2},{4,5},{5,4},{6,7},{7,6},{8,9},{9,8},{10,11... | collective-permute-start | bytes 7864328 | tf_op jit(solution)/shard_map/ppermute | solution.py:703
  490.5 50.7 %collective-permute-start.25 = (bf16[128,2816]{1,0:T(8,128)(2,1)}, bf16[128,2816]{1,0:T(8,128)(2,1)}, u32[]{:S(2)}, u32[]{:S(2)}) collective-permute-start(bf16[128,2816]{1,0:T(8,128)(2,1)} %get-tuple-element.439), channel_id=1, source_target_pairs={{0,16},{4,20},{8,24},{12,28},{16,0},{20,4},{24,8},{28,12},{1,17},{... | collective-permute-start | bytes 2162696 | tf_op jit(solution)/shard_map/ppermute | solution.py:703
  492.1 49.2 %collective-permute-start.26 = (bf16[128,2816]{1,0:T(8,128)(2,1)}, bf16[128,2816]{1,0:T(8,128)(2,1)}, u32[]{:S(2)}, u32[]{:S(2)}) collective-permute-start(bf16[128,2816]{1,0:T(8,128)(2,1)} %get-tuple-element.438), channel_id=1, source_target_pairs={{0,24},{4,28},{8,0},{12,4},{16,8},{20,12},{24,16},{28,20},{1,25},{... | collective-permute-start | bytes 2162696 | tf_op jit(solution)/shard_map/ppermute | solution.py:703
  565.0 45.6 %collective-permute-start.28 = (bf16[512,1536]{1,0:T(8,128)(2,1)}, bf16[512,1536]{1,0:T(8,128)(2,1)}, u32[]{:S(2)}, u32[]{:S(2)}) collective-permute-start(bf16[512,1536]{1,0:T(8,128)(2,1)} %get-tuple-element.433), channel_id=1, source_target_pairs={{0,1},{1,0},{2,3},{3,2},{4,5},{5,4},{6,7},{7,6},{8,9},{9,8},{10,11... | collective-permute-start | bytes 4718600 | tf_op jit(solution)/shard_map/ppermute | solution.py:703
  594.7 46.4 %collective-permute-start.35 = (bf16[128,2816]{1,0:T(8,128)(2,1)}, bf16[128,2816]{1,0:T(8,128)(2,1)S(1)}, u32[]{:S(2)}, u32[]{:S(2)}) collective-permute-start(bf16[128,2816]{1,0:T(8,128)(2,1)} %get-tuple-element.435), channel_id=1, source_target_pairs={{0,16},{4,20},{8,24},{12,28},{16,0},{20,4},{24,8},{28,12},{1,17},{... | collective-permute-start | bytes 2162696 | tf_op jit(solution)/shard_map/ppermute | solution.py:703
  (79 other events, 1190.0 us)

commit v4 on v3

--- a/solution.py
+++ b/solution.py
@@ -104,38 +104,55 @@
     return jnp.where((lane < HD) if h == 0 else (lane >= HD), x, jnp.zeros_like(x))
 
 
+def both_halves(ref, i):
+    rows = ref[i * QB : (i + 1) * QB, :]
+    return jnp.concatenate([half_lanes(rows, h) for h in range(2)], axis=0)
+
+
 def attn_fwd_kernel(span_ref, q_ref, k_ref, v_ref, diag_ref, out_ref, lse_ref, mask_s, bias_s, vt_s, s_s, p_s):
     @pl.when(pl.program_id(0) == 0)
     def _():
         fill_mask(span_ref, mask_s)
 
-    vt = jnp.transpose(v_ref[...])
+    vt_s[:128] = jnp.transpose(v_ref[...])
+    vt_s[128:] = jnp.ones((16, SEQ), jnp.bfloat16)
     for h in range(2):
         spread_bias(diag_ref, h, bias_s)
-        vt_s[h, :HD] = vt[h * HD : (h + 1) * HD]
-        vt_s[h, HD:] = jnp.ones((16, SEQ), jnp.bfloat16)
     scale = LOG2E * HD ** (-0.5)
-    for i in range(SEQ // QB):
+    blocks = SEQ // QB
+
+    def products(i):
+        s_s[i % 2, : key_count(i)] = dot_nt(k_ref[: key_count(i), :], both_halves(q_ref, i))
+
+    products(0)
+    for i in range(blocks):
         nk = key_count(i)
-        outs = []
+        if i + 1 < blocks:
+            products(i + 1)
+        tops = []
         for h in range(2):
             low = diag_ref[0, h : h + 1, 600:601]
             high = diag_ref[0, h : h + 1, 0:1]
-            qs = half_lanes(q_ref[i * QB : (i + 1) * QB, :], h)
-            s_s[h, :nk] = dot_nt(k_ref[:nk, :], qs)
+            cols = slice(h * QB, (h + 1) * QB)
             top = None
             for kt in range(nk // KB):
-                s = shifted(s_s[h, kt * KB : (kt + 1) * KB] * scale, i, kt, h, bias_s, mask_s, low, high, None)
-                s_s[h, kt * KB : (kt + 1) * KB] = s
+                tile = slice(kt * KB, (kt + 1) * KB)
+                s = shifted(s_s[i % 2, tile, cols] * scale, i, kt, h, bias_s, mask_s, low, high, None)
+                s_s[i % 2, tile, cols] = s
                 t = jnp.max(s.reshape(KB // 8, 8, QB), axis=0)
                 top = t if top is None else jnp.maximum(top, t)
             m = jnp.max(top, axis=0, keepdims=True)
+            tops.append(m)
             for kt in range(nk // KB):
-                p_s[h, kt * KB : (kt + 1) * KB] = jnp.exp2(s_s[h, kt * KB : (kt + 1) * KB] - m).astype(jnp.bfloat16)
-            ot = dot_nn(vt_s[h, :, :nk], p_s[h, :nk])
-            total = ot[HD : HD + 1]
-            outs.append(ot[:HD] / total)
-            lse_ref[0, h : h + 1, i * QB : (i + 1) * QB] = m + jnp.log2(total)
+                tile = slice(kt * KB, (kt + 1) * KB)
+                p_s[i % 2, tile, cols] = jnp.exp2(s_s[i % 2, tile, cols] - m).astype(jnp.bfloat16)
+        ot = dot_nn(vt_s[:, :nk], p_s[i % 2, :nk])
+        outs = []
+        for h in range(2):
+            cols = slice(h * QB, (h + 1) * QB)
+            total = ot[128:129, cols]
+            outs.append(ot[h * HD : (h + 1) * HD, cols] / total)
+            lse_ref[0, h : h + 1, i * QB : (i + 1) * QB] = tops[h] + jnp.log2(total)
         out_ref[i * QB : (i + 1) * QB, :] = jnp.transpose(jnp.concatenate(outs, axis=0)).astype(jnp.bfloat16)
 
 
@@ -159,9 +176,9 @@
         scratch_shapes=[
             pltpu.VMEM((16, KB, QB), jnp.float32),
             pltpu.VMEM((2, KB, WIDE), jnp.float32),
-            pltpu.VMEM((2, HD + 16, SEQ), jnp.bfloat16),
-            pltpu.VMEM((2, SEQ, QB), jnp.float32),
-            pltpu.VMEM((2, SEQ, QB), jnp.bfloat16),
+            pltpu.VMEM((128 + 16, SEQ), jnp.bfloat16),
+            pltpu.VMEM((2, SEQ, 2 * QB), jnp.float32),
+            pltpu.VMEM((2, SEQ, 2 * QB), jnp.bfloat16),
         ],
         compiler_params=pltpu.CompilerParams(vmem_limit_bytes=VMEM_LIMIT),
         cost_estimate=LIGHT,
@@ -170,10 +187,12 @@
 
 
 def attn_bwd_kernel(
-    span_ref, q_ref, k_ref, v_ref, g_ref, o_ref, lse_ref, diag_ref,
-    out_ref, drel_ref, far_ref,
-    mask_s, bias_s, acc_s, kt_s, s_s, dp_s, p_s, ds_s, dk_s, dv_s, delta_s,
+    span_ref, q_ref, k_ref, v_ref, g_ref, o_ref, lse_ref, diag_ref, *rest
 ):
+    (
+        out_ref, drel_ref, far_ref,
+        mask_s, bias_s, acc_s, kt_s, s_s, dp_s, p_s, ds_s, dk_s, dv_s, delta_s,
+    ) = rest[-14:]
     part = pl.program_id(1)
 
     @pl.when((pl.program_id(0) == 0) & (part == 0))
@@ -198,38 +217,44 @@
         acc_s[...] = jnp.zeros_like(acc_s)
         far_ref[...] = jnp.zeros_like(far_ref)
         scale = LOG2E * HD ** (-0.5)
-        for i in reversed(range(SEQ // QB)):
+        blocks = SEQ // QB
+
+        def products(i):
+            nk = key_count(i)
+            s_s[i % 2, :nk] = dot_nt(k_ref[:nk, :], both_halves(q_ref, i))
+            dp_s[i % 2, :nk] = dot_nt(v_ref[:nk, :], both_halves(g_ref, i))
+
+        products(blocks - 1)
+        for i in reversed(range(blocks)):
             nk = key_count(i)
             rows = slice(i * QB, (i + 1) * QB)
-            dqs = []
+            if i > 0:
+                products(i - 1)
             for h in range(2):
                 low = diag_ref[0, h : h + 1, 600:601]
                 high = diag_ref[0, h : h + 1, 0:1]
-                qs = half_lanes(q_ref[rows, :], h)
-                gs = half_lanes(g_ref[rows, :], h)
-                s_s[h, :nk] = dot_nt(k_ref[:nk, :], qs)
-                dp_s[h, :nk] = dot_nt(v_ref[:nk, :], gs)
                 nlse = -lse_ref[0, h : h + 1, rows]
                 delta = delta_s[h : h + 1, rows]
+                cols = slice(h * QB, (h + 1) * QB)
                 for kt in range(nk // KB):
                     tile = slice(kt * KB, (kt + 1) * KB)
                     d = kt - 2 * i
-                    p = jnp.exp2(shifted(s_s[h, tile] * scale, i, kt, h, bias_s, mask_s, low, high, nlse))
-                    ds = p * (dp_s[h, tile] - delta)
-                    p_s[tile, h * QB : (h + 1) * QB] = p.astype(jnp.bfloat16)
-                    ds_s[tile, h * QB : (h + 1) * QB] = ds.astype(jnp.bfloat16)
+                    s = s_s[i % 2, tile, cols] * scale
+                    p = jnp.exp2(shifted(s, i, kt, h, bias_s, mask_s, low, high, nlse))
+                    ds = p * (dp_s[i % 2, tile, cols] - delta)
+                    p_s[i % 2, tile, cols] = p.astype(jnp.bfloat16)
+                    ds_s[i % 2, tile, cols] = ds.astype(jnp.bfloat16)
                     if -1 <= d <= 2:
-                        cols = slice((2 - d) * 128, (2 - d) * 128 + 256)
-                        acc_s[h, :, cols] += ds
+                        near = slice((2 - d) * 128, (2 - d) * 128 + 256)
+                        acc_s[h, :, near] += ds
                     else:
                         far_ref[0, h, 0 if d < 0 else 1] += jnp.sum(ds.reshape(KB // 8, 8, QB), axis=0)
-                dqs.append(dot_nn(kt_s[h * HD : (h + 1) * HD, :nk], ds_s[:nk, h * QB : (h + 1) * QB]))
-            out_ref[rows, :] = (jnp.transpose(jnp.concatenate(dqs, axis=0)) * HD ** (-0.5)).astype(jnp.bfloat16)
-            gg = jnp.concatenate([half_lanes(g_ref[rows, :], h) for h in range(2)], axis=0)
-            qq = jnp.concatenate([half_lanes(q_ref[rows, :], h) for h in range(2)], axis=0)
-            dv = dot_nn(p_s[:nk, :], gg)
-            dk = dot_nn(ds_s[:nk, :], qq)
-            if i == SEQ // QB - 1:
+            dq = dot_nn(kt_s[:, :nk], ds_s[i % 2, :nk])
+            dq = jnp.concatenate([dq[h * HD : (h + 1) * HD, h * QB : (h + 1) * QB] for h in range(2)], axis=0)
+            out_ref[rows, :] = (jnp.transpose(dq) * HD ** (-0.5)).astype(jnp.bfloat16)
+            dv = dot_nn(p_s[i % 2, :nk], both_halves(g_ref, i))
+            dk = dot_nn(ds_s[i % 2, :nk], both_halves(q_ref, i))
+            if i == blocks - 1:
                 dv_s[...] = dv
                 dk_s[...] = dk
             else:
@@ -239,9 +264,10 @@
             drel_ref[0, h : h + 1, :] = diagonal_sums(acc_s[h])
 
 
-def attn_bwd(spans, qkv, grad_att, att, lse, diag, half):
-    pairs = H // 4
-    base = half * pairs
+def attn_bwd(spans, qkv, grad_att, att, lse, diag, part, buffer):
+    buffers = () if buffer is None else (buffer,)
+    pairs = H // 8
+    base = part * pairs
     col = lambda off: pl.BlockSpec((SEQ, 128), lambda g, p: (0, base + g + off))
     one = lambda *dims: pl.BlockSpec((1, *dims), lambda g, p: (base + g,) + (0,) * len(dims))
     new = lambda *dims: pl.BlockSpec((1, *dims), lambda g, p: (g,) + (0,) * len(dims))
@@ -257,14 +283,15 @@
             col(0),
             one(2, SEQ),
             one(2, WIDE),
-        ],
+        ]
+        + [pl.BlockSpec(memory_space=pl.ANY)] * len(buffers),
         out_specs=[
-            pl.BlockSpec((SEQ, 128), lambda g, p: (0, p * pairs + g)),
+            pl.BlockSpec((SEQ, 128), lambda g, p: (0, p * (H // 2) + base + g)),
             new(2, WIDE),
             new(2, 2, 8, QB),
         ],
         out_shape=[
-            jax.ShapeDtypeStruct((SEQ, 3 * D // 2), jnp.bfloat16),
+            jax.ShapeDtypeStruct((SEQ, 3 * D), jnp.bfloat16),
             jax.ShapeDtypeStruct((pairs, 2, WIDE), jnp.float32),
             jax.ShapeDtypeStruct((pairs, 2, 2, 8, QB), jnp.float32),
         ],
@@ -273,18 +300,19 @@
             pltpu.VMEM((2, KB, WIDE), jnp.float32),
             pltpu.VMEM((2, KB, WIDE), jnp.float32),
             pltpu.VMEM((128, SEQ), jnp.bfloat16),
-            pltpu.VMEM((2, SEQ, QB), jnp.float32),
-            pltpu.VMEM((2, SEQ, QB), jnp.float32),
-            pltpu.VMEM((SEQ, 2 * QB), jnp.bfloat16),
-            pltpu.VMEM((SEQ, 2 * QB), jnp.bfloat16),
+            pltpu.VMEM((2, SEQ, 2 * QB), jnp.float32),
+            pltpu.VMEM((2, SEQ, 2 * QB), jnp.float32),
+            pltpu.VMEM((2, SEQ, 2 * QB), jnp.bfloat16),
+            pltpu.VMEM((2, SEQ, 2 * QB), jnp.bfloat16),
             pltpu.VMEM((SEQ, 128), jnp.float32),
             pltpu.VMEM((SEQ, 128), jnp.float32),
             pltpu.VMEM((2, SEQ), jnp.float32),
         ],
+        input_output_aliases={8: 0} if buffers else {},
         compiler_params=pltpu.CompilerParams(vmem_limit_bytes=VMEM_LIMIT),
         cost_estimate=LIGHT,
-        name=f"attn_bwd_{half}",
-    )(spans, qkv, qkv, qkv, grad_att, att, lse, diag)
+        name=f"attn_bwd_{part}",
+    )(spans, qkv, qkv, qkv, grad_att, att, lse, diag, *buffers)
 
 
 def wide_diag(rel_table):
@@ -308,7 +336,7 @@
 
 
 VMEM_MOST = 58 * 1024 * 1024
-PARTS = 2
+PARTS = 1
 
 
 def slot_onehot(meta_ref, n, rows):
@@ -363,21 +391,19 @@
             hid_s[here, cols] = hidden
             hid_ref[here] = hidden
 
-    for n in range(deep):
-
-        @pl.when(step == wide + n)
-        def _():
-            cols = slice(n * FT, (n + 1) * FT)
-            outs = dot_nn(hid_s[...], down_ref[0])
-            for s, tok_ref, cot_ref, here in pair:
-                gates = gate_s[here, 0:1]
-                out = outs[here].astype(jnp.bfloat16).astype(jnp.float32)
-                cot = dot_nn(hot_s[s], cot_ref[...])
-                lane = lax.broadcasted_iota(jnp.int32, (rows, 128), 1)
-                gate_s[here] += jnp.where(lane < 64, 0.0, jnp.sum(out * cot, axis=1, keepdims=True))
-                gc_ref[here, cols] = (gates * cot).astype(jnp.bfloat16)
-                p_ref = (p_a, p_b)[s]
-                p_ref[...] = dot_nn(turned_s[s], (gates * out).astype(jnp.bfloat16)).astype(jnp.bfloat16)
+    @pl.when(step >= wide)
+    def _():
+        cols = pl.ds(pl.multiple_of((step - wide) * FT, FT), FT)
+        outs = dot_nn(hid_s[...], down_ref[0])
+        for s, tok_ref, cot_ref, here in pair:
+            gates = gate_s[here, 0:1]
+            out = outs[here].astype(jnp.bfloat16).astype(jnp.float32)
+            cot = dot_nn(hot_s[s], cot_ref[...])
+            lane = lax.broadcasted_iota(jnp.int32, (rows, 128), 1)
+            gate_s[here] += jnp.where(lane < 64, 0.0, jnp.sum(out * cot, axis=1, keepdims=True))
+            gc_ref[here, cols] = (gates * cot).astype(jnp.bfloat16)
+            p_ref = (p_a, p_b)[s]
+            p_ref[...] = dot_nn(turned_s[s], (gates * out).astype(jnp.bfloat16)).astype(jnp.bfloat16)
 
     @pl.when(step == wide + deep - 1)
     def _():
@@ -529,16 +555,22 @@
     out_ref[...] = jnp.transpose(row_sums(turned_s, refs[many : 2 * many])).astype(jnp.bfloat16)
 
 
-def grad_in_kernel(*refs):
-    out_gate_ref, out_up_ref, turned_s = refs[-3:]
-    many = (len(refs) - 3) // 3
+def grad_in_kernel(many, inner, place_ref, *refs):
+    sides = refs[3 * many : 3 * many + 2 * inner]
+    turned_s, tile_s = refs[-2:]
+    blocks, rows, wide = tile_s.shape
 
     @pl.when(pl.program_id(0) == 0)
     def _():
         turn_into(turned_s, refs[:many])
 
-    out_gate_ref[...] = row_sums(turned_s, refs[many : 2 * many]).astype(jnp.bfloat16)
-    out_up_ref[...] = row_sums(turned_s, refs[2 * many : 3 * many]).astype(jnp.bfloat16)
+    for kind in range(2):
+        tile = row_sums(turned_s, refs[(kind + 1) * many : (kind + 2) * many]).astype(jnp.bfloat16)
+        tile_s[...] = tile.reshape(blocks, rows, wide)
+        for away in range(inner):
+            side = lax.rem(place_ref[0] + away, inner)
+            for block in range(blocks // inner):
+                sides[kind * inner + away][block] = tile_s[block * inner + side]
 
 
 def grad_down(gc, hidden):
@@ -558,81 +590,180 @@
     )(*gc, *hidden)
 
 
-def grad_in(xs, dgate, dup):
+def grad_in(place, inner, blocks, xs, dgate, dup):
     rows, width = dgate[0].shape
+    many = len(xs)
     once = pl.Buffered(1)
-    out = pl.BlockSpec((D, FT), lambda j: (0, j))
-    return pl.pallas_call(
-        grad_in_kernel,
+    out = pl.BlockSpec((blocks // inner, D // blocks, FT), lambda j: (0, 0, j))
+    made = pl.pallas_call(
+        partial(grad_in_kernel, many, inner),
         grid=(width // FT,),
-        in_specs=[pl.BlockSpec((rows, D), lambda j: (0, 0), pipeline_mode=once)] * len(xs)
-        + [pl.BlockSpec((rows, FT), lambda j: (0, j))] * (2 * len(xs)),
-        out_specs=[out, out],
-        out_shape=[low_shape(D, width)] * 2,
-        scratch_shapes=[pltpu.VMEM((D, rows * len(xs)), jnp.bfloat16)],
+        in_specs=[pl.BlockSpec(memory_space=pltpu.SMEM)]
+        + [pl.BlockSpec((rows, D), lambda j: (0, 0), pipeline_mode=once)] * many
+        + [pl.BlockSpec((rows, FT), lambda j: (0, j))] * (2 * many),
+        out_specs=[out] * (2 * inner),
+        out_shape=[low_shape(blocks // inner, D // blocks, width)] * (2 * inner),
+        scratch_shapes=[
+            pltpu.VMEM((D, rows * many), jnp.bfloat16),
+            pltpu.VMEM((blocks, D // blocks, FT), jnp.bfloat16),
+        ],
         compiler_params=pltpu.CompilerParams(vmem_limit_bytes=VMEM_LIMIT),
         cost_estimate=LIGHT,
         name="grad_in",
-    )(*xs, *dgate, *dup)
-
-
-def grad_half_kernel(left_ref, right_ref, *rest):
-    out_ref, turned_s = rest[-2:]
-
-    @pl.when(pl.program_id(0) == 0)
-    def _():
-        turned_s[...] = jnp.transpose(left_ref[...])
-
-    out_ref[...] = dot_nn(turned_s[...], right_ref[...]).astype(jnp.bfloat16)
-
-
-def grad_rows(left, right, name, wide=None, first=0, buffer=None):
-    count, width = right.shape
-    buffers = () if buffer is None else (buffer,)
+    )(place, *xs, *dgate, *dup)
+    return made[:inner], made[inner:]
+
+
+def grad_attn_kernel(place_ref, normed_ref, attended_ref, right_ref, branch_ref, own_ref, other_ref, turned_s):
+    step = pl.program_id(0)
+    first = pl.num_programs(0) - 2
+
+    @pl.when(step == 0)
+    def _():
+        turned_s[...] = jnp.transpose(normed_ref[...])
+
+    @pl.when(step == first)
+    def _():
+        turned_s[...] = jnp.transpose(attended_ref[...])
+
+    def hand(right):
+        made = dot_nn(turned_s[...], right).astype(jnp.bfloat16)
+        upper, lower = made[: D // 2], made[D // 2 :]
+        swap = place_ref[0] == 1
+        own_ref[...] = jnp.where(swap, lower, upper)
+        other_ref[...] = jnp.where(swap, upper, lower)
+
+    @pl.when(step < first)
+    def _():
+        hand(right_ref[...])
+
+    @pl.when(step >= first)
+    def _():
+        hand(branch_ref[...])
+
+
+def grad_attn(place, normed, attended, grad_qkv, branch):
+    count = normed.shape[0]
+    whole = pl.BlockSpec((count, D), lambda j: (0, 0), pipeline_mode=pl.Buffered(1))
+    half = pl.BlockSpec((D // 2, 512), lambda j: (0, j))
     return pl.pallas_call(
-        grad_half_kernel,
-        grid=(width // 512,),
-        in_specs=[pl.BlockSpec((count, D), lambda j: (0, 0)), pl.BlockSpec((count, 512), lambda j: (0, j))]
-        + [pl.BlockSpec(memory_space=pl.ANY)] * len(buffers),
-        out_specs=pl.BlockSpec((D, 512), lambda j: (0, first // 512 + j)),
-        out_shape=jax.ShapeDtypeStruct((D, wide or width), jnp.bfloat16),
+        grad_attn_kernel,
+        grid=(8,),
+        in_specs=[
+            pl.BlockSpec(memory_space=pltpu.SMEM),
+            whole,
+            whole,
+            pl.BlockSpec((count, 512), lambda j: (0, jnp.minimum(j, 5))),
+            pl.BlockSpec((count, 512), lambda j: (0, jnp.maximum(j - 6, 0))),
+        ],
+        out_specs=[half, half],
+        out_shape=[low_shape(D // 2, 4 * D)] * 2,
         scratch_shapes=[pltpu.VMEM((D, count), jnp.bfloat16)],
-        input_output_aliases={2: 0} if buffers else {},
         compiler_params=pltpu.CompilerParams(vmem_limit_bytes=VMEM_LIMIT),
         cost_estimate=LIGHT,
-        name=name,
-    )(left, right, *buffers)
-
-
-def grad_normed_kernel(first_ref, second_ref, w_ref, out_ref):
-    step = pl.program_id(0)
-
-    @pl.when(step == 0)
-    def _():
-        out_ref[...] = jnp.zeros_like(out_ref)
-
-    @pl.when(step % 2 == 0)
-    def _():
-        out_ref[...] += dot_nt(first_ref[...], w_ref[...])
-
-    @pl.when(step % 2 == 1)
-    def _():
-        out_ref[...] += dot_nt(second_ref[...], w_ref[...])
-
-
-def grad_normed_of(first, second, w_qkv):
-    count = first.shape[0]
-    part = pl.BlockSpec((count, D // 2), lambda j: (0, j // 2))
+        name="grad_attn",
+    )(place, normed, attended, grad_qkv, branch)
+
+
+def grad_normed_kernel(grad_ref, w_ref, out_ref):
+    @pl.when(pl.program_id(0) == 0)
+    def _():
+        out_ref[...] = dot_nt(grad_ref[...], w_ref[...])
+
+    @pl.when(pl.program_id(0) > 0)
+    def _():
+        out_ref[...] += dot_nt(grad_ref[...], w_ref[...])
+
+
+def grad_normed_of(grad_qkv, w_qkv):
+    count = grad_qkv.shape[0]
     return pl.pallas_call(
         grad_normed_kernel,
-        grid=(6,),
-        in_specs=[part, part, pl.BlockSpec((D, D // 2), lambda j: (0, j))],
-        out_specs=pl.BlockSpec((count, D), lambda j: (0, 0)),
+        grid=(3,),
+        in_specs=[pl.BlockSpec((count, D), lambda p: (0, p)), pl.BlockSpec((D, D), lambda p: (0, p))],
+        out_specs=pl.BlockSpec((count, D), lambda p: (0, 0)),
         out_shape=jax.ShapeDtypeStruct((count, D), jnp.float32),
         compiler_params=pltpu.CompilerParams(vmem_limit_bytes=VMEM_LIMIT),
         cost_estimate=LIGHT,
         name="grad_normed",
-    )(first, second, w_qkv)
+    )(grad_qkv, w_qkv)
+
+
+def gather_kernel(place_ref, one_own, one_other, two_own, two_other, qkv_ref, out_ref):
+    step = pl.program_id(0)
+    swap = place_ref[0] == 1
+    rows = one_own.shape[0]
+
+    def whole(own_ref, other_ref, target):
+        own, other = own_ref[...], other_ref[...]
+        target[:rows] = jnp.where(swap, other, own).astype(jnp.float32)
+        target[rows:] = jnp.where(swap, own, other).astype(jnp.float32)
+
+    @pl.when(step < 4)
+    def _():
+        whole(one_own, one_other, qkv_ref)
+
+    @pl.when((step >= 4) & (step < 6))
+    def _():
+        whole(two_own, two_other, qkv_ref)
+
+    @pl.when(step >= 6)
+    def _():
+        whole(two_own, two_other, out_ref)
+
+
+def gather_halves(place, one, two):
+    rows = one[0].shape[0]
+    left = pl.BlockSpec((rows, 512), lambda j: (0, jnp.minimum(j, 3)))
+    right = pl.BlockSpec((rows, 512), lambda j: (0, jnp.maximum(j - 4, 0)))
+    return pl.pallas_call(
+        gather_kernel,
+        grid=(8,),
+        in_specs=[pl.BlockSpec(memory_space=pltpu.SMEM), left, left, right, right],
+        out_specs=[
+            pl.BlockSpec((2 * rows, 512), lambda j: (0, jnp.minimum(j, 5))),
+            pl.BlockSpec((2 * rows, 512), lambda j: (0, jnp.maximum(j - 6, 0))),
+        ],
+        out_shape=[
+            jax.ShapeDtypeStruct((2 * rows, 3 * D), jnp.float32),
+            jax.ShapeDtypeStruct((2 * rows, D), jnp.float32),
+        ],
+        compiler_params=pltpu.CompilerParams(vmem_limit_bytes=VMEM_LIMIT),
+        cost_estimate=LIGHT,
+        name="gather_halves",
+    )(place, *one, *two)
+
+
+def project_kernel(tok_ref, gain_ref, w_ref, normed_ref, qkv_ref):
+    @pl.when(pl.program_id(0) == 0)
+    def _():
+        values = tok_ref[...].astype(jnp.float32)
+        scale = lax.rsqrt(jnp.mean(values * values, axis=-1, keepdims=True) + EPSILON)
+        normed_ref[...] = (values * scale * gain_ref[...]).astype(jnp.bfloat16)
+
+    qkv_ref[...] = dot_nn(normed_ref[...], w_ref[...]).astype(jnp.bfloat16)
+
+
+def project(tokens, gain, w_qkv):
+    count, width = tokens.shape[0], w_qkv.shape[1]
+    once = pl.Buffered(1)
+    return pl.pallas_call(
+        project_kernel,
+        grid=(width // 512,),
+        in_specs=[
+            pl.BlockSpec((count, D), lambda j: (0, 0), pipeline_mode=once),
+            pl.BlockSpec((1, D), lambda j: (0, 0), pipeline_mode=once),
+            pl.BlockSpec((D, 512), lambda j: (0, j)),
+        ],
+        out_specs=[
+            pl.BlockSpec((count, D), lambda j: (0, 0), pipeline_mode=once),
+            pl.BlockSpec((count, 512), lambda j: (0, j)),
+        ],
+        out_shape=[low_shape(count, D), low_shape(count, width)],
+        compiler_params=pltpu.CompilerParams(vmem_limit_bytes=VMEM_LIMIT),
+        cost_estimate=LIGHT,
+        name="project",
+    )(tokens, gain[None], w_qkv)
 
 
 OUTER = 4
@@ -702,6 +833,11 @@
         sent = lax.dynamic_index_in_dim(x, (place + step) % size, 0, keepdims=False)
         out.append(lax.ppermute(sent, axis, pairs(step)))
     return out
+
+
+def sides_swapped(sides, level):
+    axis, size, place, pairs = level
+    return [sides[0]] + [lax.ppermute(sides[step], axis, pairs(step)) for step in range(1, size)]
 
 
 def whole_swapped(x, level):
@@ -789,9 +925,7 @@
 
     diag = wide_diag(rel_table)
     token_float = tokens.astype(jnp.float32)
-    normed, scale_attn = rms_forward(token_float, gain_attn)
-    normed_low = normed.astype(jnp.bfloat16)
-    qkv = jnp.dot(normed_low, w_qkv, preferred_element_type=jnp.float32).astype(jnp.bfloat16)
+    normed_low, qkv = project(tokens, gain_attn, w_qkv)
     attended_low, lse = attn_fwd(span_starts, qkv, diag)
     attended_low, cot_sib, cot_far, metas = tie(attended_low, cot_sib, cot_far, metas)
     mixed = token_float + jnp.dot(attended_low, w_out, preferred_element_type=jnp.float32)
@@ -847,19 +981,20 @@
     slope, down_near = tie(slope, down_near)
     near_grads = to_sibling(here[1])
     down_far = swapped(down_near, outer)
-    gate_low, up_low = grad_in(rows_in, slope, act)
+    gate_low, up_low = grad_in(
+        jnp.reshape(inner[2], (1,)), inner[1], lax.axis_size("rep"), rows_in, slope, act
+    )
     gate_low, up_low, far_grads, near_grads = tie(gate_low, up_low, far_grads, near_grads)
     grad_pairs = total([here[0], near_grads] + far_grads)
     grad_gates_all = total([dots[0]] + far_dots)
     block_out = (mixed + total([outs[0]] + far_outs)).astype(jnp.bfloat16)
-    gate_near = near_swapped(gate_low)
+    gate_near = sides_swapped(gate_low, inner)
 
     grad_out = cotangent.astype(jnp.float32)
     by_token = jnp.transpose(grad_gates_all[:experts])
     grad_gates = jnp.sum(jnp.where(choose, by_token[:, None, :], 0.0), axis=-1)
     grad_chosen = gates * (grad_gates - jnp.sum(gates * grad_gates, axis=-1, keepdims=True))
     grad_logits = jnp.sum(jnp.where(choose, grad_chosen[:, :, None], 0.0), axis=1).astype(jnp.bfloat16)
-    grad_w_router = jnp.einsum("td,te->de", routed_low, grad_logits, preferred_element_type=jnp.float32)
     grad_routed = grad_pairs + jnp.einsum(
         "te,de->td", grad_logits, w_router, preferred_element_type=jnp.float32
     )
@@ -870,35 +1005,41 @@
         "te,de->td", grad_branch, w_out, preferred_element_type=jnp.float32
     ).astype(jnp.bfloat16)
 
-    grad_attended, grad_branch, block_out = tie(grad_attended, grad_branch, block_out)
-    first = attn_bwd(span_starts, qkv, grad_attended, attended_low, lse, diag, 0)
-    early = grad_rows(attended_low, grad_branch, "grad_out", 5 * D // 2, 3 * D // 2)
-    early = grad_rows(normed_low, first[0], "grad_qkv_0", 5 * D // 2, 0, early)
-    early, grad_attended, gate_near, down_far = tie(early, grad_attended, gate_near, down_far)
+    grad_attended, grad_branch = tie(grad_attended, grad_branch)
+    quarters = [None] * 4
+    made = None
+
+    def backward(part, grad, made):
+        return attn_bwd(span_starts, qkv, grad, attended_low, lse, diag, part, made)
+
+    for part in (0, 1):
+        made, *quarters[part] = backward(part, grad_attended, made)
+    made, grad_attended, gate_near, down_far, up_low = tie(
+        made, grad_attended, gate_near, down_far, up_low
+    )
     gate_near = low_total(gate_near)
-    sum_down = total(down_far)
-    gate_near, grad_attended, sum_down, up_low = tie(gate_near, grad_attended, sum_down, up_low)
+    gate_near, grad_attended, up_low = tie(gate_near, grad_attended, up_low)
     gate_far = swapped(gate_near, outer)
-    up_near = near_swapped(up_low)
-    early = rows_swapped(early, core)
-    second = attn_bwd(span_starts, qkv, grad_attended, attended_low, lse, diag, 1)
-    second, early, gate_far, up_near = tie(second, early, gate_far, up_near)
-    second = list(second)
-    up_near, early = tie(low_total(up_near), low_total(early))
-    early = rows_swapped(early, chip)
-    own = lax.dynamic_index_in_dim(up_near, levels()[3][2], 0, keepdims=False)
-    up_far = swapped(up_near, outer, (1, OUTER - 1))
-    half_second = grad_rows(normed_low, second[0], "grad_qkv_1")
-    late = rows_swapped(half_second, core)
-    half_second, *second[:1] = tie(half_second, second[0])
-    grad_normed = grad_normed_of(first[0], second[0], w_qkv)
-    late, grad_normed, early, up_far = tie(late, grad_normed, early, up_far)
-    early, late = tie(low_total(early), low_total(late))
-    late = rows_swapped(late, inner)
-    last = swapped(up_near, outer, tuple(range(2, OUTER - 1)))
+    up_near = sides_swapped(up_low, inner)
+    for part in (2, 3):
+        made, *quarters[part] = backward(part, grad_attended, made)
+    mine, other = grad_attn(jnp.reshape(core[2], (1,)), normed_low, attended_low, made, grad_branch)
+    grad_normed = grad_normed_of(made, w_qkv)
+    mine, other, grad_normed, gate_far, up_near = tie(mine, other, grad_normed, gate_far, up_near)
+    up_near, other = tie(low_total(up_near), other)
+    other = to_sibling(other)
+    up_far = swapped(up_near, outer)
+    both = low_total([mine, other])
+    cut = both.shape[1] // 2
+    one, two, quarters, late = tie(both[:, :cut], both[:, cut:], quarters, (routed_low, grad_logits))
+    grad_w_router = jnp.einsum("td,te->de", *late, preferred_element_type=jnp.float32)
+    one, two = rows_swapped(one, chip), rows_swapped(two, inner)
+    scale_attn = lax.rsqrt(jnp.mean(token_float * token_float, axis=-1, keepdims=True) + EPSILON)
     grad_norm_attn, grad_gain_attn = rms_backward(token_float, scale_attn, gain_attn, grad_normed)
     grad_tokens = grad_mixed + grad_norm_attn
-    grad_rel_table = rel_grad(jnp.concatenate([first[1], second[1]]), jnp.concatenate([first[2], second[2]]))
+    grad_rel_table = rel_grad(
+        jnp.concatenate([x[0] for x in quarters]), jnp.concatenate([x[1] for x in quarters])
+    )
     small = jnp.concatenate(
         [
             jnp.transpose(grad_w_router),
@@ -907,27 +1048,22 @@
             grad_gain_moe[None],
         ]
     )
-    late, small, grad_tokens = tie(late, small, grad_tokens)
-    late, early = tie(low_total(late), early)
-    small = whole_swapped(small, core)
-    late, early, last, small = tie(rows_swapped(late, chip), rows_swapped(early, inner), last, small)
-    wide = early[0].shape[1]
-    both, small = tie(jnp.concatenate([low_total(early), low_total(late)], axis=1), total(small))
-    both, small = tie(rows_swapped(both, outer), whole_swapped(small, chip))
+    one, two, small, grad_tokens = tie(one, two, small, grad_tokens)
+    one, two = tie(low_total(one), low_total(two))
+    one, two, up_far = tie(rows_swapped(one, inner), rows_swapped(two, chip), up_far)
+    both = jnp.concatenate([low_total(one), low_total(two)], axis=1)
+    both, small = tie(rows_swapped(both, outer), whole_swapped(small, core))
     both, small = tie(low_total(both), total(small))
-    both, small = tie(collected(both, outer), whole_swapped(small, inner))
-    early, late, small = tie(both[:, :wide], both[:, wide:], total(small))
-    early, late, small = tie(collected(early, inner), collected(late, chip), whole_swapped(small, outer))
+    both, small = tie(collected(both, outer), whole_swapped(small, chip))
+    one, two, small = tie(both[:, :cut], both[:, cut:], total(small))
+    one, two, small = tie(collected(one, inner), collected(two, chip), whole_swapped(small, inner))
+    small = whole_swapped(total(small), outer)
+    one, two, small = tie(collected(one, chip), collected(two, inner), small)
+    one, two = (one, to_sibling(one)), (two, to_sibling(two))
+    sum_w_qkv, sum_w_out = gather_halves(jnp.reshape(core[2], (1,)), one, two)
     small = total(small)
-    early, late = tie(collected(early, chip), collected(late, inner))
-    early, late = tie(collected(early, core), collected(late, core))
-    sum_first, sum_second = early[:, : 3 * D // 2].astype(jnp.float32), late.astype(jnp.float32)
-    sum_w_out = early[:, 3 * D // 2 :].astype(jnp.float32)
-    up_far = [own] + up_far + last
+    sum_down = total(down_far)
     sum_gate, sum_up = total(gate_far), total(up_far)
-    sum_w_qkv = jnp.concatenate(
-        [x[:, n * D // 2 : (n + 1) * D // 2] for n in range(3) for x in (sum_first, sum_second)], axis=1
-    )
     small = (
         small[experts, : BUCKETS * H].reshape(BUCKETS, H),
         jnp.transpose(small[:experts]),

time: 794 us -> 703 us (0.89)
  waiting for transfers between devices: 141 us -> 97.7 us
  other arithmetic: 71.4 us -> 56.4 us
  Pallas kernels: 431 us -> 418 us
  matrix products: 24.4 us -> 15 us
  local copies, waits for them, and re-layouts: 42.5 us -> 33.6 us
    ppermute x21 -> x17, waiting for transfers between devices: 73.9 us -> 42 us  [swapped(): out.append(lax.ppermute(sent, axis, pairs(step)))]
    ppermute x6 -> x4, waiting for transfers between devices: 41.4 us -> 21.6 us  [collected(): other = lax.ppermute(x, axis, pairs(1))]
    pallas_call x5, Pallas kernels: 74.1 us -> 90.8 us  [the longest x1 39.4 us: grad_in(): pl.pallas_call(partial(grad_in_kernel, many, inner), grid=(width // FT,),...]
    pallas_call x2, Pallas kernels: 136 us -> 119 us  [expert_fwd(): pl.pallas_call(expert_fwd_kernel, grid=(wide + deep,), in_specs=[whole(2,...]
    pallas_call x1, Pallas kernels: 40 us -> 24.9 us  [attn_fwd(): pl.pallas_call(attn_fwd_kernel, grid=(H // 2,), in_specs=[pl.BlockSpec(me...]
    dot_general x2 -> x1, matrix products: 12.5 us -> 0.38 us  [per_device(): jnp.einsum('td,te->de', *late, preferred_element_type=jnp.float32)]
    squeeze x13 -> x9, local copies, waits for them, and re-layouts: 27 us -> 15.3 us  [swapped(): sent = lax.dynamic_index_in_dim(x, (place + step) % size, 0, keepdims=False)]
    ppermute x0 -> x2, waiting for transfers between devices: none -> 8.06 us  [sides_swapped(): lax.ppermute(sides[step], axis, pairs(step))]
  transfers between devices with their start and end apart: 54 -> 53, of which waited for: 19 -> 18; matrix products, arithmetic and copies ran while one was open for 10% -> 13% of each run, Pallas kernels for 54% -> 59%
where the time goes in v4:
time: 703 us; the launch traced here: 689 us
  Pallas kernels  418 us (59%)
  waiting for transfers between devices  97.7 us (14%)
  starting transfers between devices  66.6 us (9%)
  other arithmetic  56.4 us (8%)
  local copies, waits for them, and re-layouts  33.6 us (5%)
  matrix products  15 us (2%)
    pallas_call x2, Pallas kernels, expert_fwd(): pl.pallas_call(expert_fwd_kernel, grid=(wide + deep,), in_specs=[whole(2,...  119 us
    pallas_call x2, Pallas kernels, expert_bwd(): pl.pallas_call(expert_bwd_kernel, grid=(wide + deep,), in_specs=[pl.Block...  93.2 us
    pallas_call x4, Pallas kernels, attn_bwd(): pl.pallas_call(attn_bwd_kernel, grid=(pairs, 3), in_specs=[pl.BlockSpec(m...  66.5 us
    ppermute x17, waiting for transfers between devices, swapped(): out.append(lax.ppermute(sent, axis, pairs(step)))  42 us
    pallas_call x1, Pallas kernels, grad_in(): pl.pallas_call(partial(grad_in_kernel, many, inner), grid=(width // FT,),...  39.4 us
    ppermute x17, starting transfers between devices, swapped(): out.append(lax.ppermute(sent, axis, pairs(step)))  30 us
    pallas_call x1, Pallas kernels, attn_fwd(): pl.pallas_call(attn_fwd_kernel, grid=(H // 2,), in_specs=[pl.BlockSpec(me...  24.9 us
    pallas_call x1, Pallas kernels, grad_down(): pl.pallas_call(grad_down_kernel, grid=(width // FT,), in_specs=[pl.BlockS...  23.5 us
  transfers between devices with their start and end apart: 53, of which 18 were waited for; matrix products, arithmetic and copies ran while one was open for 13% of the time, Pallas kernels for 59%

profile of v4, /device:TPU:0, one launch (start us, length us, event | category | flops | bytes accessed | tf_op | source)
XLA Modules:
  0.0 689.4 jit_solution(9984142312087356988)
XLA Ops:
  14.6 12.2 %project.1 = (bf16[1024,1024]{1,0:T(8,128)(2,1)}, bf16[1024,3072]{1,0:T(8,128)(2,1)}) custom-call(bf16[1024,1024]{1,0:T(8,128)(2,1)} %tok_ref.1, f32[1,1024]{1,0:T(1,128)} %bitcast.129, bf16[1024,3072]{1,0:T(8,128)(2,1)} %w_ref.3), custom_call_target="tpu_custom_call" | custom-call | flops 1000 | bytes 1000 | tf_op jit(solution)/shard_map/project/pallas_call | solution.py:750
  27.5 24.9 %attn_fwd.1 = (bf16[1024,1024]{1,0:T(8,128)(2,1)}, f32[8,2,1024]{2,1,0:T(2,128)}) custom-call(s32[1,2]{1,0:T(1,128)} %span_ref.9, bf16[1024,3072]{1,0:T(8,128)(2,1)} %get-tuple-element.223.q_ref.k_ref.v_ref, bf16[1024,3072]{1,0:T(8,128)(2,1)} %get-tuple-element.223.q_ref.k_ref.v_ref, bf16[1024,3072]{1,0:T(8,128)(2,1)} %get-tuple-element.223.q_ref.k_ref.v_ref, ...), custom_call_target="tpu_custom_call" | custom-call | flops 1000 | bytes 1000 | tf_op jit(solution)/shard_map/attn_fwd/pallas_call | solution.py:161
  63.7 59.7 %expert_fwd_0.1 = (bf16[1280,1024]{1,0:T(8,128)(2,1)}, bf16[1280,1024]{1,0:T(8,128)(2,1)}, bf16[1280,2816]{1,0:T(8,128)(2,1)}, bf16[1280,2816]{1,0:T(8,128)(2,1)...) custom-call(s32[2,8,1024]{2,1,0:T(8,128)} %get-tuple-element.226.met, ...), custom_call_target="tpu_custom_call" | custom-call | flops 1000 | bytes 1000 | tf_op jit(solution)/shard_map/expert_fwd_0/pallas_call | solution.py:463
  130.7 59.8 %expert_fwd_1.1 = (bf16[1280,1024]{1,0:T(8,128)(2,1)}, bf16[1280,1024]{1,0:T(8,128)(2,1)}, bf16[1280,2816]{1,0:T(8,128)(2,1)}, bf16[1280,2816]{1,0:T(8,128)(2,1)...) custom-call(s32[2,8,1024]{2,1,0:T(8,128)} %get-tuple-element.238.met, ...), custom_call_target="tpu_custom_call" | custom-call | flops 1000 | bytes 1000 | tf_op jit(solution)/shard_map/expert_fwd_1/pallas_call | solution.py:463
  192.1 23.5 %grad_down.1 = bf16[2816,1024]{1,0:T(8,128)(2,1)} custom-call(bf16[1280,1024]{1,0:T(8,128)(2,1)} %get-tuple-element.237.refs_0_.gc_ref, bf16[1280,1024]{1,0:T(8,128)(2,1)} %get-tuple-element.242.refs_1_.gc_ref, bf16[1280,2816]{1,0:T(8,128)(2,1)} %get-tuple-element.243.refs_2_, bf16[1280,2816]{1,0:T(8,128)(2,1)} %get-tuple-element.244.refs_3_), custom_call_target="tpu_custom_call" | custom-call | flops 1000 | bytes 1000 | tf_op jit(solution)/shard_map/grad_down/pallas_call | solution.py:579
  227.3 46.5 %expert_bwd_1.1 = (bf16[1280,2816]{1,0:T(8,128)(2,1)}, bf16[1280,2816]{1,0:T(8,128)(2,1)}, bf16[1024,1024]{1,0:T(8,128)(2,1)}, bf16[1024,1024]{1,0:T(8,128)(2,1)}) custom-call(s32[2,8,1024]{2,1,0:T(8,128)} %get-tuple-element.238.meta_ref, bf16[1280,1024]{1,0:T(8,128)(2,1)} %get-tuple-element.242.refs_1_.gc_ref, ...), custom_call_target="tpu_custom_call" | custom-call | flops 1000 | bytes 1000 | tf_op jit(solution)/shard_map/expert_bwd_1/pallas_call | solution.py:506
  274.8 46.7 %expert_bwd_0.1 = (bf16[1280,2816]{1,0:T(8,128)(2,1)}, bf16[1280,2816]{1,0:T(8,128)(2,1)}, bf16[1024,1024]{1,0:T(8,128)(2,1)}, bf16[1024,1024]{1,0:T(8,128)(2,1)}) custom-call(s32[2,8,1024]{2,1,0:T(8,128)} %get-tuple-element.226.meta_ref, bf16[1280,1024]{1,0:T(8,128)(2,1)} %get-tuple-element.237.refs_0_.gc_ref, ...), custom_call_target="tpu_custom_call" | custom-call | flops 1000 | bytes 1000 | tf_op jit(solution)/shard_map/expert_bwd_0/pallas_call | solution.py:506
  329.3 39.4 %grad_in.1 = (bf16[4,128,2816]{2,1,0:T(8,128)(2,1)}, bf16[4,128,2816]{2,1,0:T(8,128)(2,1)}, bf16[4,128,2816]{2,1,0:T(8,128)(2,1)}, bf16[4,128,2816]{2,1,0:T(8,128)(2,1)}) custom-call(s32[1]{0:T(128)} %bitcast.14.place_ref, bf16[1280,1024]{1,0:T(8,128)(2,1)} %get-tuple-element.272.refs_0_, bf16[1280,1024]{1,0:T(8,128)(2,1)} %get-tuple-element.273.refs_1_, ...), custom_call_target="tpu_custom_call" | custom-call | flops 1000 | bytes 1000 | tf_op jit(solution)/shard_map/grad_in/pallas_call | solution.py:598
  392.1 16.5 %attn_bwd_0.1 = (bf16[1024,3072]{1,0:T(8,128)(2,1)}, f32[2,2,768]{2,1,0:T(2,128)}, f32[2,2,2,8,256]{4,3,2,1,0:T(8,128)}) custom-call(s32[1,2]{1,0:T(1,128)} %span_ref.9, bf16[1024,3072]{1,0:T(8,128)(2,1)} %get-tuple-element.223.q_ref.k_ref.v_ref, bf16[1024,3072]{1,0:T(8,128)(2,1)} %get-tuple-element.223.q_ref.k_ref.v_ref, ...), custom_call_target="tpu_custom_call" | custom-call | flops 1000 | bytes 1000 | tf_op jit(solution)/shard_map/attn_bwd_0/pallas_call | solution.py:274
  408.6 16.8 %attn_bwd_1.1 = (bf16[1024,3072]{1,0:T(8,128)(2,1)}, f32[2,2,768]{2,1,0:T(2,128)}, f32[2,2,2,8,256]{4,3,2,1,0:T(8,128)}) custom-call(s32[1,2]{1,0:T(1,128)} %span_ref.9, bf16[1024,3072]{1,0:T(8,128)(2,1)} %get-tuple-element.223.q_ref.k_ref.v_ref, bf16[1024,3072]{1,0:T(8,128)(2,1)} %get-tuple-element.223.q_ref.k_ref.v_ref, ...), custom_call_target="tpu_custom_call", output_to_operand_aliasing={{0}: (8, {})} | custom-call | flops 1000 | bytes 1000 | tf_op jit(solution)/shard_map/attn_bwd_1/pallas_call | solution.py:274
  425.5 8.1 %collective-permute-done.19 = bf16[4,128,2816]{2,1,0:T(8,128)(2,1)S(1)} collective-permute-done((bf16[4,128,2816]{2,1,0:T(8,128)(2,1)}, bf16[4,128,2816]{2,1,0:T(8,128)(2,1)S(1)}, u32[]{:S(2)}, u32[]{:S(2)}) %collective-permute-start.19) | collective-permute-done | bytes 2883616 | tf_op jit(solution)/shard_map/ppermute | solution.py:840
  444.8 16.5 %attn_bwd_2.1 = (bf16[1024,3072]{1,0:T(8,128)(2,1)}, f32[2,2,768]{2,1,0:T(2,128)}, f32[2,2,2,8,256]{4,3,2,1,0:T(8,128)}) custom-call(s32[1,2]{1,0:T(1,128)} %span_ref.9, bf16[1024,3072]{1,0:T(8,128)(2,1)} %get-tuple-element.223.q_ref.k_ref.v_ref, bf16[1024,3072]{1,0:T(8,128)(2,1)} %get-tuple-element.223.q_ref.k_ref.v_ref, ...), custom_call_target="tpu_custom_call", output_to_operand_aliasing={{0}: (8, {})} | custom-call | flops 1000 | bytes 1000 | tf_op jit(solution)/shard_map/attn_bwd_2/pallas_call | solution.py:274
  461.3 16.7 %attn_bwd_3.1 = (bf16[1024,3072]{1,0:T(8,128)(2,1)}, f32[2,2,768]{2,1,0:T(2,128)}, f32[2,2,2,8,256]{4,3,2,1,0:T(8,128)}) custom-call(s32[1,2]{1,0:T(1,128)} %span_ref.9, bf16[1024,3072]{1,0:T(8,128)(2,1)} %get-tuple-element.223.q_ref.k_ref.v_ref, bf16[1024,3072]{1,0:T(8,128)(2,1)} %get-tuple-element.223.q_ref.k_ref.v_ref, ...), custom_call_target="tpu_custom_call", output_to_operand_aliasing={{0}: (8, {})} | custom-call | flops 1000 | bytes 1000 | tf_op jit(solution)/shard_map/attn_bwd_3/pallas_call | solution.py:274
  477.9 11.4 %grad_normed.1 = f32[1024,1024]{1,0:T(8,128)} custom-call(bf16[1024,3072]{1,0:T(8,128)(2,1)} %get-tuple-element.315.right_ref.grad_ref, bf16[1024,3072]{1,0:T(8,128)(2,1)} %w_ref.3), custom_call_target="tpu_custom_call" | custom-call | flops 1000 | bytes 1000 | tf_op jit(solution)/shard_map/grad_normed/pallas_call | solution.py:680
  489.4 16.9 %grad_attn.1 = (bf16[512,4096]{1,0:T(8,128)(2,1)}, bf16[512,4096]{1,0:T(8,128)(2,1)}) custom-call(s32[1]{0:T(128)} %bitcast.13.place_ref, bf16[1024,1024]{1,0:T(8,128)(2,1)} %get-tuple-element.268.normed_ref, bf16[1024,1024]{1,0:T(8,128)(2,1)} %get-tuple-element.225.o_ref.attended_ref, bf16[1024,3072]{1,0:T(8,128)(2,1)} %get-tuple-element.315.right_ref.grad_ref, ...), custom_call_target="tpu_custom_call" | custom-call | flops 1000 | bytes 1000 | tf_op jit(solution)/shard_map/grad_attn/pallas_call | solution.py:649
  545.7 14.6 %collective-permute-done.29 = bf16[256,2048]{1,0:T(8,128)(2,1)} collective-permute-done((bf16[256,2048]{1,0:T(8,128)(2,1)}, bf16[256,2048]{1,0:T(8,128)(2,1)}, u32[]{:S(2)}, u32[]{:S(2)}) %collective-permute-start.29) | collective-permute-done | bytes 1048608 | tf_op jit(solution)/shard_map/ppermute | solution.py:834
  568.6 10.2 %collective-permute-done.31 = bf16[128,2048]{1,0:T(8,128)(2,1)S(1)} collective-permute-done((bf16[128,2048]{1,0:T(8,128)(2,1)S(1)}, bf16[128,2048]{1,0:T(8,128)(2,1)S(1)}, u32[]{:S(2)}, u32[]{:S(2)}) %collective-permute-start.31) | collective-permute-done | bytes 524320 | tf_op jit(solution)/shard_map/ppermute | solution.py:834
  591.8 10.5 %collective-permute-done.36 = bf16[32,4096]{1,0:T(8,128)(2,1)S(1)} collective-permute-done((bf16[32,4096]{1,0:T(8,128)(2,1)S(1)}, bf16[32,4096]{1,0:T(8,128)(2,1)S(1)}, u32[]{:S(2)}, u32[]{:S(2)}) %collective-permute-start.36) | collective-permute-done | bytes 262176 | tf_op jit(solution)/shard_map/ppermute | solution.py:834
  602.5 6.1 collective-permute-start.39
  618.4 10.0 %collective-permute-done.40 = bf16[32,4096]{1,0:T(8,128)(2,1)S(1)} collective-permute-done((bf16[32,4096]{1,0:T(8,128)(2,1)S(1)}, bf16[32,4096]{1,0:T(8,128)(2,1)S(1)}, u32[]{:S(2)}, u32[]{:S(2)}) %collective-permute-start.40) | collective-permute-done | bytes 262176 | tf_op jit(solution)/shard_map/ppermute | solution.py:863
  631.2 11.2 %collective-permute-done.44 = bf16[128,2048]{1,0:T(8,128)(2,1)S(1)} collective-permute-done((bf16[128,2048]{1,0:T(8,128)(2,1)S(1)}, bf16[128,2048]{1,0:T(8,128)(2,1)S(1)}, u32[]{:S(2)}, u32[]{:S(2)}) %collective-permute-start.44) | collective-permute-done | bytes 524320 | tf_op jit(solution)/shard_map/ppermute | solution.py:859
  648.6 6.1 collective-permute-start.48
  657.2 10.0 %collective-permute-done.47 = bf16[256,2048]{1,0:T(8,128)(2,1)S(1)} collective-permute-done((bf16[256,2048]{1,0:T(8,128)(2,1)S(1)}, bf16[256,2048]{1,0:T(8,128)(2,1)S(1)}, u32[]{:S(2)}, u32[]{:S(2)}) %collective-permute-start.47) | collective-permute-done | bytes 1048608 | tf_op jit(solution)/shard_map/ppermute | solution.py:859
  678.4 10.9 %gather_halves.1 = (f32[1024,3072]{1,0:T(8,128)}, f32[1024,1024]{1,0:T(8,128)}) custom-call(s32[1]{0:T(128)} %bitcast.13.place_ref, bf16[512,2048]{1,0:T(8,128)(2,1)} %pad_maximum_fusion.one_own, bf16[512,2048]{1,0:T(8,128)(2,1)} %collective-permute-done.51.one_other, bf16[512,2048]{1,0:T(8,128)(2,1)} %pad_maximum_fusion.1.two_own, ...), custom_call_target="tpu_custom_call" | custom-call | flops 1000 | bytes 1000 | tf_op jit(solution)/shard_map/gather_halves/pallas_call | solution.py:719
  (293 shorter events, 182.4 us)
Async XLA Ops:
  0.7 52.7 %collective-permute-start = (bf16[1024,1024]{1,0:T(8,128)(2,1)}, bf16[1024,1024]{1,0:T(8,128)(2,1)}, u32[]{:S(2)}, u32[]{:S(2)}) collective-permute-start(bf16[1024,1024]{1,0:T(8,128)(2,1)} %cot_a.1), channel_id=1, source_target_pairs={{0,1},{1,0},{2,3},{3,2},{4,5},{5,4},{6,7},{7,6},{8,9},{9,8},{10,11... | collective-permute-start | bytes 6291464 | tf_op jit(solution)/shard_map/ppermute | solution.py:790
  1.2 52.1 %collective-permute-start.1 = (bf16[1024,1024]{1,0:T(8,128)(2,1)}, bf16[1024,1024]{1,0:T(8,128)(2,1)}, u32[]{:S(2)}, u32[]{:S(2)}) collective-permute-start(bf16[1024,1024]{1,0:T(8,128)(2,1)} %cot_a.1), channel_id=1, source_target_pairs={{0,2},{1,3},{2,0},{3,1},{4,6},{5,7},{6,4},{7,5},{8,10},{9,11},{10,... | collective-permute-start | bytes 6291464 | tf_op jit(solution)/shard_map/ppermute | solution.py:795
  10.1 42.4 %collective-permute-start.3 = (s32[6,1024]{1,0:T(8,128)S(1)}, s32[6,1024]{1,0:T(8,128)S(1)}, u32[]{:S(2)}, u32[]{:S(2)}) collective-permute-start(s32[6,1024]{1,0:T(8,128)S(1)} %pad_add_fusion.2), channel_id=1, source_target_pairs={{0,2},{1,3},{2,0},{3,1},{4,6},{5,7},{6,4},{7,5},{8,10},{9,11},{10,... | collective-permute-start | bytes 73736 | tf_op jit(solution)/shard_map/ppermute | solution.py:795
  10.3 42.2 %collective-permute-start.4 = (s32[6,1024]{1,0:T(8,128)S(1)}, s32[6,1024]{1,0:T(8,128)S(1)}, u32[]{:S(2)}, u32[]{:S(2)}) collective-permute-start(s32[6,1024]{1,0:T(8,128)S(1)} %pad_add_fusion.2), channel_id=1, source_target_pairs={{0,3},{1,2},{2,1},{3,0},{4,7},{5,6},{6,5},{7,4},{8,11},{9,10},{10,... | collective-permute-start | bytes 73736 | tf_op jit(solution)/shard_map/ppermute | solution.py:795
  59.4 64.0 %collective-permute-start.6 = (bf16[1024,1024]{1,0:T(8,128)(2,1)S(1)}, bf16[1024,1024]{1,0:T(8,128)(2,1)}, u32[]{:S(2)}, u32[]{:S(2)}) collective-permute-start(bf16[1024,1024]{1,0:T(8,128)(2,1)S(1)} %multiply_convert_fusion.tok_a), channel_id=1, source_target_pairs={{0,2},{1,3},{2,0},{3,1},{4,6},{5,7},{6,4},{7,5},{8,10},{9,11},{10,... | collective-permute-start | bytes 6291464 | tf_op jit(solution)/shard_map/ppermute | solution.py:795
  60.1 63.3 %collective-permute-start.7 = (bf16[1024,1024]{1,0:T(8,128)(2,1)}, bf16[1024,1024]{1,0:T(8,128)(2,1)}, u32[]{:S(2)}, u32[]{:S(2)}) collective-permute-start(bf16[1024,1024]{1,0:T(8,128)(2,1)} %collective-permute-done.1.cot_a), channel_id=1, source_target_pairs={{0,1},{1,0},{2,3},{3,2},{4,5},{5,4},{6,7},{7,6},{8,9},{9,8},{10,11... | collective-permute-start | bytes 6291464 | tf_op jit(solution)/shard_map/ppermute | solution.py:790
  123.7 91.9 %collective-permute-start.11 = (bf16[1024,1024]{1,0:T(8,128)(2,1)}, bf16[1024,1024]{1,0:T(8,128)(2,1)}, u32[]{:S(2)}, u32[]{:S(2)}) collective-permute-start(bf16[1024,1024]{1,0:T(8,128)(2,1)} %get-tuple-element.249), channel_id=1, source_target_pairs={{0,1},{1,0},{2,3},{3,2},{4,5},{5,4},{6,7},{7,6},{8,9},{9,8},{10,11... | collective-permute-start | bytes 6291464 | tf_op jit(solution)/shard_map/ppermute | solution.py:790
  217.9 56.8 %collective-permute-start.13 = (bf16[1024,1024]{1,0:T(8,128)(2,1)}, bf16[1024,1024]{1,0:T(8,128)(2,1)}, u32[]{:S(2)}, u32[]{:S(2)}) collective-permute-start(bf16[1024,1024]{1,0:T(8,128)(2,1)} %add_convert_fusion.5), channel_id=1, source_target_pairs={{0,2},{1,3},{2,0},{3,1},{4,6},{5,7},{6,4},{7,5},{8,10},{9,11},{10,... | collective-permute-start | bytes 6291464 | tf_op jit(solution)/shard_map/ppermute | solution.py:795
  224.4 100.8 %collective-permute-start.15 = (bf16[4,352,1024]{2,1,0:T(8,128)(2,1)}, bf16[4,352,1024]{2,1,0:T(8,128)(2,1)}, u32[]{:S(2)}, u32[]{:S(2)}) collective-permute-start(bf16[4,352,1024]{2,1,0:T(8,128)(2,1)} %get-tuple-element.456), channel_id=1, source_target_pairs={{0,4},{4,0},{8,12},{12,8},{16,20},{20,16},{24,28},{28,24},{1,5},{5... | collective-permute-start | bytes 8650760 | tf_op jit(solution)/shard_map/ppermute | solution.py:834
  225.8 48.9 %collective-permute-start.14 = (f32[8,1024]{1,0:T(8,128)S(1)}, f32[8,1024]{1,0:T(8,128)S(1)}, u32[]{:S(2)}, u32[]{:S(2)}) collective-permute-start(f32[8,1024]{1,0:T(8,128)S(1)} %add.308), channel_id=1, source_target_pairs={{0,2},{1,3},{2,0},{3,1},{4,6},{5,7},{6,4},{7,5},{8,10},{9,11},{10,... | collective-permute-start | bytes 98312 | tf_op jit(solution)/shard_map/ppermute | solution.py:795
  273.9 94.8 %collective-permute-start.16 = (bf16[1024,1024]{1,0:T(8,128)(2,1)}, bf16[1024,1024]{1,0:T(8,128)(2,1)}, u32[]{:S(2)}, u32[]{:S(2)}) collective-permute-start(bf16[1024,1024]{1,0:T(8,128)(2,1)} %get-tuple-element.289), channel_id=1, source_target_pairs={{0,2},{1,3},{2,0},{3,1},{4,6},{5,7},{6,4},{7,5},{8,10},{9,11},{10,... | collective-permute-start | bytes 6291464 | tf_op jit(solution)/shard_map/ppermute | solution.py:795
  274.4 94.3 %collective-permute-start.17 = (bf16[1024,1024]{1,0:T(8,128)(2,1)}, bf16[1024,1024]{1,0:T(8,128)(2,1)}, u32[]{:S(2)}, u32[]{:S(2)}) collective-permute-start(bf16[1024,1024]{1,0:T(8,128)(2,1)} %get-tuple-element.290), channel_id=1, source_target_pairs={{0,3},{1,2},{2,1},{3,0},{4,7},{5,6},{6,5},{7,4},{8,11},{9,10},{10,... | collective-permute-start | bytes 6291464 | tf_op jit(solution)/shard_map/ppermute | solution.py:795
  321.5 47.2 %collective-permute-start.18 = (bf16[1024,1024]{1,0:T(8,128)(2,1)}, bf16[1024,1024]{1,0:T(8,128)(2,1)}, u32[]{:S(2)}, u32[]{:S(2)}) collective-permute-start(bf16[1024,1024]{1,0:T(8,128)(2,1)} %get-tuple-element.291), channel_id=1, source_target_pairs={{0,1},{1,0},{2,3},{3,2},{4,5},{5,4},{6,7},{7,6},{8,9},{9,8},{10,11... | collective-permute-start | bytes 6291464 | tf_op jit(solution)/shard_map/ppermute | solution.py:790
  368.7 64.8 %collective-permute-start.19 = (bf16[4,128,2816]{2,1,0:T(8,128)(2,1)}, bf16[4,128,2816]{2,1,0:T(8,128)(2,1)S(1)}, u32[]{:S(2)}, u32[]{:S(2)}) collective-permute-start(bf16[4,128,2816]{2,1,0:T(8,128)(2,1)} %get-tuple-element.303), channel_id=1, source_target_pairs={{0,4},{4,0},{8,12},{12,8},{16,20},{20,16},{24,28},{28,24},{1,5},{5... | collective-permute-start | bytes 8650760 | tf_op jit(solution)/shard_map/ppermute | solution.py:840
  371.9 53.5 %collective-permute-start.20 = (bf16[352,1024]{1,0:T(8,128)(2,1)}, bf16[352,1024]{1,0:T(8,128)(2,1)}, u32[]{:S(2)}, u32[]{:S(2)}) collective-permute-start(bf16[352,1024]{1,0:T(8,128)(2,1)} %get-tuple-element.471), channel_id=1, source_target_pairs={{0,8},{4,12},{8,16},{12,20},{16,24},{20,28},{24,0},{28,4},{1,9},{5... | collective-permute-start | bytes 2162696 | tf_op jit(solution)/shard_map/ppermute | solution.py:834
  373.5 52.0 %collective-permute-start.21 = (bf16[352,1024]{1,0:T(8,128)(2,1)}, bf16[352,1024]{1,0:T(8,128)(2,1)}, u32[]{:S(2)}, u32[]{:S(2)}) collective-permute-start(bf16[352,1024]{1,0:T(8,128)(2,1)} %get-tuple-element.470), channel_id=1, source_target_pairs={{0,16},{4,20},{8,24},{12,28},{16,0},{20,4},{24,8},{28,12},{1,17},{... | collective-permute-start | bytes 2162696 | tf_op jit(solution)/shard_map/ppermute | solution.py:834
  376.0 49.4 %collective-permute-start.22 = (bf16[352,1024]{1,0:T(8,128)(2,1)}, bf16[352,1024]{1,0:T(8,128)(2,1)}, u32[]{:S(2)}, u32[]{:S(2)}) collective-permute-start(bf16[352,1024]{1,0:T(8,128)(2,1)} %get-tuple-element.469), channel_id=1, source_target_pairs={{0,24},{4,28},{8,0},{12,4},{16,8},{20,12},{24,16},{28,20},{1,25},{... | collective-permute-start | bytes 2162696 | tf_op jit(solution)/shard_map/ppermute | solution.py:834
  434.2 72.1 %collective-permute-start.26 = (bf16[4,128,2816]{2,1,0:T(8,128)(2,1)}, bf16[4,128,2816]{2,1,0:T(8,128)(2,1)}, u32[]{:S(2)}, u32[]{:S(2)}) collective-permute-start(bf16[4,128,2816]{2,1,0:T(8,128)(2,1)} %get-tuple-element.321), channel_id=1, source_target_pairs={{0,4},{4,0},{8,12},{12,8},{16,20},{20,16},{24,28},{28,24},{1,5},{5... | collective-permute-start | bytes 8650760 | tf_op jit(solution)/shard_map/ppermute | solution.py:840
  436.3 70.0 %collective-permute-start.23 = (bf16[128,2816]{1,0:T(8,128)(2,1)}, bf16[128,2816]{1,0:T(8,128)(2,1)S(1)}, u32[]{:S(2)}, u32[]{:S(2)}) collective-permute-start(bf16[128,2816]{1,0:T(8,128)(2,1)} %get-tuple-element.467), channel_id=1, source_target_pairs={{0,8},{4,12},{8,16},{12,20},{16,24},{20,28},{24,0},{28,4},{1,9},{5... | collective-permute-start | bytes 2162696 | tf_op jit(solution)/shard_map/ppermute | solution.py:834
  442.4 63.9 %collective-permute-start.24 = (bf16[128,2816]{1,0:T(8,128)(2,1)}, bf16[128,2816]{1,0:T(8,128)(2,1)S(1)}, u32[]{:S(2)}, u32[]{:S(2)}) collective-permute-start(bf16[128,2816]{1,0:T(8,128)(2,1)} %get-tuple-element.466), channel_id=1, source_target_pairs={{0,16},{4,20},{8,24},{12,28},{16,0},{20,4},{24,8},{28,12},{1,17},{... | collective-permute-start | bytes 2162696 | tf_op jit(solution)/shard_map/ppermute | solution.py:834
  444.0 62.3 %collective-permute-start.25 = (bf16[128,2816]{1,0:T(8,128)(2,1)S(1)}, bf16[128,2816]{1,0:T(8,128)(2,1)S(1)}, u32[]{:S(2)}, u32[]{:S(2)}) collective-permute-start(bf16[128,2816]{1,0:T(8,128)(2,1)S(1)} %get-tuple-element.465), channel_id=1, source_target_pairs={{0,24},{4,28},{8,0},{12,4},{16,8},{20,12},{24,16},{28,20},{1,25},{... | collective-permute-start | bytes 2162696 | tf_op jit(solution)/shard_map/ppermute | solution.py:834
  517.0 50.6 %collective-permute-start.32 = (bf16[128,2816]{1,0:T(8,128)(2,1)}, bf16[128,2816]{1,0:T(8,128)(2,1)}, u32[]{:S(2)}, u32[]{:S(2)}) collective-permute-start(bf16[128,2816]{1,0:T(8,128)(2,1)} %get-tuple-element.463), channel_id=1, source_target_pairs={{0,8},{4,12},{8,16},{12,20},{16,24},{20,28},{24,0},{28,4},{1,9},{5... | collective-permute-start | bytes 2162696 | tf_op jit(solution)/shard_map/ppermute | solution.py:834
  518.2 50.4 %collective-permute-start.33 = (bf16[128,2816]{1,0:T(8,128)(2,1)}, bf16[128,2816]{1,0:T(8,128)(2,1)}, u32[]{:S(2)}, u32[]{:S(2)}) collective-permute-start(bf16[128,2816]{1,0:T(8,128)(2,1)} %get-tuple-element.462), channel_id=1, source_target_pairs={{0,16},{4,20},{8,24},{12,28},{16,0},{20,4},{24,8},{28,12},{1,17},{... | collective-permute-start | bytes 2162696 | tf_op jit(solution)/shard_map/ppermute | solution.py:834
  519.5 49.1 %collective-permute-start.34 = (bf16[128,2816]{1,0:T(8,128)(2,1)}, bf16[128,2816]{1,0:T(8,128)(2,1)}, u32[]{:S(2)}, u32[]{:S(2)}) collective-permute-start(bf16[128,2816]{1,0:T(8,128)(2,1)} %get-tuple-element.461), channel_id=1, source_target_pairs={{0,24},{4,28},{8,0},{12,4},{16,8},{20,12},{24,16},{28,20},{1,25},{... | collective-permute-start | bytes 2162696 | tf_op jit(solution)/shard_map/ppermute | solution.py:834
  (73 other events, 908.2 us)

commit v5 on v4

--- a/solution.py
+++ b/solution.py
@@ -1031,7 +1031,10 @@
     up_far = swapped(up_near, outer)
     both = low_total([mine, other])
     cut = both.shape[1] // 2
-    one, two, quarters, late = tie(both[:, :cut], both[:, cut:], quarters, (routed_low, grad_logits))
+    one, two, quarters, late, tokens_late = tie(
+        both[:, :cut], both[:, cut:], quarters, (routed_low, grad_logits), tokens
+    )
+    token_float = tokens_late.astype(jnp.float32)
     grad_w_router = jnp.einsum("td,te->de", *late, preferred_element_type=jnp.float32)
     one, two = rows_swapped(one, chip), rows_swapped(two, inner)
     scale_attn = lax.rsqrt(jnp.mean(token_float * token_float, axis=-1, keepdims=True) + EPSILON)

time: 703 us -> 702 us (level)
  no operation moved by 1% of the time
where the time goes in v5:
time: 702 us; the launch traced here: 688 us
  Pallas kernels  418 us (60%)
  waiting for transfers between devices  92.7 us (13%)
  starting transfers between devices  70 us (10%)
  other arithmetic  61.3 us (9%)
  local copies, waits for them, and re-layouts  30.2 us (4%)
  matrix products  14 us (2%)
    pallas_call x2, Pallas kernels, expert_fwd(): pl.pallas_call(expert_fwd_kernel, grid=(wide + deep,), in_specs=[whole(2,...  119 us
    pallas_call x2, Pallas kernels, expert_bwd(): pl.pallas_call(expert_bwd_kernel, grid=(wide + deep,), in_specs=[pl.Block...  93.2 us
    pallas_call x4, Pallas kernels, attn_bwd(): pl.pallas_call(attn_bwd_kernel, grid=(pairs, 3), in_specs=[pl.BlockSpec(m...  66.5 us
    pallas_call x1, Pallas kernels, grad_in(): pl.pallas_call(partial(grad_in_kernel, many, inner), grid=(width // FT,),...  39.4 us
    ppermute x17, waiting for transfers between devices, swapped(): out.append(lax.ppermute(sent, axis, pairs(step)))  37.7 us
    ppermute x17, starting transfers between devices, swapped(): out.append(lax.ppermute(sent, axis, pairs(step)))  33.3 us
    pallas_call x1, Pallas kernels, attn_fwd(): pl.pallas_call(attn_fwd_kernel, grid=(H // 2,), in_specs=[pl.BlockSpec(me...  24.9 us
    pallas_call x1, Pallas kernels, grad_down(): pl.pallas_call(grad_down_kernel, grid=(width // FT,), in_specs=[pl.BlockS...  23.5 us
  transfers between devices with their start and end apart: 53, of which 18 were waited for; matrix products, arithmetic and copies ran while one was open for 13% of the time, Pallas kernels for 59%

profile of v5, /device:TPU:0, one launch (start us, length us, event | category | flops | bytes accessed | tf_op | source)
XLA Modules:
  0.0 688.5 jit_solution(13081599827563673997)
XLA Ops:
  14.6 12.2 %project.1 = (bf16[1024,1024]{1,0:T(8,128)(2,1)}, bf16[1024,3072]{1,0:T(8,128)(2,1)}) custom-call(bf16[1024,1024]{1,0:T(8,128)(2,1)} %tok_ref.1, f32[1,1024]{1,0:T(1,128)} %bitcast.129, bf16[1024,3072]{1,0:T(8,128)(2,1)} %w_ref.3), custom_call_target="tpu_custom_call" | custom-call | flops 1000 | bytes 1000 | tf_op jit(solution)/shard_map/project/pallas_call | solution.py:750
  27.5 24.9 %attn_fwd.1 = (bf16[1024,1024]{1,0:T(8,128)(2,1)}, f32[8,2,1024]{2,1,0:T(2,128)}) custom-call(s32[1,2]{1,0:T(1,128)} %span_ref.9, bf16[1024,3072]{1,0:T(8,128)(2,1)} %get-tuple-element.224.q_ref.k_ref.v_ref, bf16[1024,3072]{1,0:T(8,128)(2,1)} %get-tuple-element.224.q_ref.k_ref.v_ref, bf16[1024,3072]{1,0:T(8,128)(2,1)} %get-tuple-element.224.q_ref.k_ref.v_ref, ...), custom_call_target="tpu_custom_call" | custom-call | flops 1000 | bytes 1000 | tf_op jit(solution)/shard_map/attn_fwd/pallas_call | solution.py:161
  63.7 59.7 %expert_fwd_0.1 = (bf16[1280,1024]{1,0:T(8,128)(2,1)}, bf16[1280,1024]{1,0:T(8,128)(2,1)}, bf16[1280,2816]{1,0:T(8,128)(2,1)}, bf16[1280,2816]{1,0:T(8,128)(2,1)...) custom-call(s32[2,8,1024]{2,1,0:T(8,128)} %get-tuple-element.227.met, ...), custom_call_target="tpu_custom_call" | custom-call | flops 1000 | bytes 1000 | tf_op jit(solution)/shard_map/expert_fwd_0/pallas_call | solution.py:463
  130.7 59.8 %expert_fwd_1.1 = (bf16[1280,1024]{1,0:T(8,128)(2,1)}, bf16[1280,1024]{1,0:T(8,128)(2,1)}, bf16[1280,2816]{1,0:T(8,128)(2,1)}, bf16[1280,2816]{1,0:T(8,128)(2,1)...) custom-call(s32[2,8,1024]{2,1,0:T(8,128)} %get-tuple-element.239.met, ...), custom_call_target="tpu_custom_call" | custom-call | flops 1000 | bytes 1000 | tf_op jit(solution)/shard_map/expert_fwd_1/pallas_call | solution.py:463
  192.1 23.5 %grad_down.1 = bf16[2816,1024]{1,0:T(8,128)(2,1)} custom-call(bf16[1280,1024]{1,0:T(8,128)(2,1)} %get-tuple-element.238.refs_0_.gc_ref, bf16[1280,1024]{1,0:T(8,128)(2,1)} %get-tuple-element.243.refs_1_.gc_ref, bf16[1280,2816]{1,0:T(8,128)(2,1)} %get-tuple-element.244.refs_2_, bf16[1280,2816]{1,0:T(8,128)(2,1)} %get-tuple-element.245.refs_3_), custom_call_target="tpu_custom_call" | custom-call | flops 1000 | bytes 1000 | tf_op jit(solution)/shard_map/grad_down/pallas_call | solution.py:579
  227.3 46.5 %expert_bwd_1.1 = (bf16[1280,2816]{1,0:T(8,128)(2,1)}, bf16[1280,2816]{1,0:T(8,128)(2,1)}, bf16[1024,1024]{1,0:T(8,128)(2,1)}, bf16[1024,1024]{1,0:T(8,128)(2,1)}) custom-call(s32[2,8,1024]{2,1,0:T(8,128)} %get-tuple-element.239.meta_ref, bf16[1280,1024]{1,0:T(8,128)(2,1)} %get-tuple-element.243.refs_1_.gc_ref, ...), custom_call_target="tpu_custom_call" | custom-call | flops 1000 | bytes 1000 | tf_op jit(solution)/shard_map/expert_bwd_1/pallas_call | solution.py:506
  274.8 46.7 %expert_bwd_0.1 = (bf16[1280,2816]{1,0:T(8,128)(2,1)}, bf16[1280,2816]{1,0:T(8,128)(2,1)}, bf16[1024,1024]{1,0:T(8,128)(2,1)}, bf16[1024,1024]{1,0:T(8,128)(2,1)}) custom-call(s32[2,8,1024]{2,1,0:T(8,128)} %get-tuple-element.227.meta_ref, bf16[1280,1024]{1,0:T(8,128)(2,1)} %get-tuple-element.238.refs_0_.gc_ref, ...), custom_call_target="tpu_custom_call" | custom-call | flops 1000 | bytes 1000 | tf_op jit(solution)/shard_map/expert_bwd_0/pallas_call | solution.py:506
  329.3 39.4 %grad_in.1 = (bf16[4,128,2816]{2,1,0:T(8,128)(2,1)}, bf16[4,128,2816]{2,1,0:T(8,128)(2,1)}, bf16[4,128,2816]{2,1,0:T(8,128)(2,1)}, bf16[4,128,2816]{2,1,0:T(8,128)(2,1)}) custom-call(s32[1]{0:T(128)} %bitcast.14.place_ref, bf16[1280,1024]{1,0:T(8,128)(2,1)} %get-tuple-element.273.refs_0_, bf16[1280,1024]{1,0:T(8,128)(2,1)} %get-tuple-element.274.refs_1_, ...), custom_call_target="tpu_custom_call" | custom-call | flops 1000 | bytes 1000 | tf_op jit(solution)/shard_map/grad_in/pallas_call | solution.py:598
  392.7 16.5 %attn_bwd_0.1 = (bf16[1024,3072]{1,0:T(8,128)(2,1)}, f32[2,2,768]{2,1,0:T(2,128)}, f32[2,2,2,8,256]{4,3,2,1,0:T(8,128)}) custom-call(s32[1,2]{1,0:T(1,128)} %span_ref.9, bf16[1024,3072]{1,0:T(8,128)(2,1)} %get-tuple-element.224.q_ref.k_ref.v_ref, bf16[1024,3072]{1,0:T(8,128)(2,1)} %get-tuple-element.224.q_ref.k_ref.v_ref, ...), custom_call_target="tpu_custom_call" | custom-call | flops 1000 | bytes 1000 | tf_op jit(solution)/shard_map/attn_bwd_0/pallas_call | solution.py:274
  409.2 16.8 %attn_bwd_1.1 = (bf16[1024,3072]{1,0:T(8,128)(2,1)}, f32[2,2,768]{2,1,0:T(2,128)}, f32[2,2,2,8,256]{4,3,2,1,0:T(8,128)}) custom-call(s32[1,2]{1,0:T(1,128)} %span_ref.9, bf16[1024,3072]{1,0:T(8,128)(2,1)} %get-tuple-element.224.q_ref.k_ref.v_ref, bf16[1024,3072]{1,0:T(8,128)(2,1)} %get-tuple-element.224.q_ref.k_ref.v_ref, ...), custom_call_target="tpu_custom_call", output_to_operand_aliasing={{0}: (8, {})} | custom-call | flops 1000 | bytes 1000 | tf_op jit(solution)/shard_map/attn_bwd_1/pallas_call | solution.py:274
  426.1 7.5 %collective-permute-done.19 = bf16[4,128,2816]{2,1,0:T(8,128)(2,1)S(1)} collective-permute-done((bf16[4,128,2816]{2,1,0:T(8,128)(2,1)}, bf16[4,128,2816]{2,1,0:T(8,128)(2,1)S(1)}, u32[]{:S(2)}, u32[]{:S(2)}) %collective-permute-start.19) | collective-permute-done | bytes 2883616 | tf_op jit(solution)/shard_map/ppermute | solution.py:840
  444.8 16.5 %attn_bwd_2.1 = (bf16[1024,3072]{1,0:T(8,128)(2,1)}, f32[2,2,768]{2,1,0:T(2,128)}, f32[2,2,2,8,256]{4,3,2,1,0:T(8,128)}) custom-call(s32[1,2]{1,0:T(1,128)} %span_ref.9, bf16[1024,3072]{1,0:T(8,128)(2,1)} %get-tuple-element.224.q_ref.k_ref.v_ref, bf16[1024,3072]{1,0:T(8,128)(2,1)} %get-tuple-element.224.q_ref.k_ref.v_ref, ...), custom_call_target="tpu_custom_call", output_to_operand_aliasing={{0}: (8, {})} | custom-call | flops 1000 | bytes 1000 | tf_op jit(solution)/shard_map/attn_bwd_2/pallas_call | solution.py:274
  461.3 16.7 %attn_bwd_3.1 = (bf16[1024,3072]{1,0:T(8,128)(2,1)}, f32[2,2,768]{2,1,0:T(2,128)}, f32[2,2,2,8,256]{4,3,2,1,0:T(8,128)}) custom-call(s32[1,2]{1,0:T(1,128)} %span_ref.9, bf16[1024,3072]{1,0:T(8,128)(2,1)} %get-tuple-element.224.q_ref.k_ref.v_ref, bf16[1024,3072]{1,0:T(8,128)(2,1)} %get-tuple-element.224.q_ref.k_ref.v_ref, ...), custom_call_target="tpu_custom_call", output_to_operand_aliasing={{0}: (8, {})} | custom-call | flops 1000 | bytes 1000 | tf_op jit(solution)/shard_map/attn_bwd_3/pallas_call | solution.py:274
  477.9 11.4 %grad_normed.1 = f32[1024,1024]{1,0:T(8,128)} custom-call(bf16[1024,3072]{1,0:T(8,128)(2,1)} %get-tuple-element.316.right_ref.grad_ref, bf16[1024,3072]{1,0:T(8,128)(2,1)} %w_ref.3), custom_call_target="tpu_custom_call" | custom-call | flops 1000 | bytes 1000 | tf_op jit(solution)/shard_map/grad_normed/pallas_call | solution.py:680
  489.4 16.9 %grad_attn.1 = (bf16[512,4096]{1,0:T(8,128)(2,1)}, bf16[512,4096]{1,0:T(8,128)(2,1)}) custom-call(s32[1]{0:T(128)} %bitcast.13.place_ref, bf16[1024,1024]{1,0:T(8,128)(2,1)} %get-tuple-element.269.normed_ref, bf16[1024,1024]{1,0:T(8,128)(2,1)} %get-tuple-element.226.o_ref.attended_ref, bf16[1024,3072]{1,0:T(8,128)(2,1)} %get-tuple-element.316.right_ref.grad_ref, ...), custom_call_target="tpu_custom_call" | custom-call | flops 1000 | bytes 1000 | tf_op jit(solution)/shard_map/grad_attn/pallas_call | solution.py:649
  545.7 11.6 %collective-permute-done.29 = bf16[256,2048]{1,0:T(8,128)(2,1)} collective-permute-done((bf16[256,2048]{1,0:T(8,128)(2,1)}, bf16[256,2048]{1,0:T(8,128)(2,1)}, u32[]{:S(2)}, u32[]{:S(2)}) %collective-permute-start.29) | collective-permute-done | bytes 1048608 | tf_op jit(solution)/shard_map/ppermute | solution.py:834
  567.7 7.4 %collective-permute-done.31 = bf16[128,2048]{1,0:T(8,128)(2,1)S(1)} collective-permute-done((bf16[128,2048]{1,0:T(8,128)(2,1)S(1)}, bf16[128,2048]{1,0:T(8,128)(2,1)S(1)}, u32[]{:S(2)}, u32[]{:S(2)}) %collective-permute-start.31) | collective-permute-done | bytes 524320 | tf_op jit(solution)/shard_map/ppermute | solution.py:834
  576.0 8.2 %collective-permute-start.35 = (bf16[32,4096]{1,0:T(8,128)(2,1)S(1)}, bf16[32,4096]{1,0:T(8,128)(2,1)S(1)}, u32[]{:S(2)}, u32[]{:S(2)}) collective-permute-start(bf16[32,4096]{1,0:T(8,128)(2,1)S(1)} %get-tuple-element.491), channel_id=1, source_target_pairs={{0,8},{4,12},{8,16},{12,20},{16,24},{20,28},{24,0},{28,4},{1,9},{5... | collective-permute-start | bytes 786440 | tf_op jit(solution)/shard_map/ppermute | solution.py:834
  590.9 10.4 %collective-permute-done.36 = bf16[32,4096]{1,0:T(8,128)(2,1)S(1)} collective-permute-done((bf16[32,4096]{1,0:T(8,128)(2,1)S(1)}, bf16[32,4096]{1,0:T(8,128)(2,1)S(1)}, u32[]{:S(2)}, u32[]{:S(2)}) %collective-permute-start.36) | collective-permute-done | bytes 262176 | tf_op jit(solution)/shard_map/ppermute | solution.py:834
  617.4 10.0 %collective-permute-done.40 = bf16[32,4096]{1,0:T(8,128)(2,1)S(1)} collective-permute-done((bf16[32,4096]{1,0:T(8,128)(2,1)S(1)}, bf16[32,4096]{1,0:T(8,128)(2,1)S(1)}, u32[]{:S(2)}, u32[]{:S(2)}) %collective-permute-start.40) | collective-permute-done | bytes 262176 | tf_op jit(solution)/shard_map/ppermute | solution.py:863
  630.3 11.2 %collective-permute-done.44 = bf16[128,2048]{1,0:T(8,128)(2,1)S(1)} collective-permute-done((bf16[128,2048]{1,0:T(8,128)(2,1)S(1)}, bf16[128,2048]{1,0:T(8,128)(2,1)S(1)}, u32[]{:S(2)}, u32[]{:S(2)}) %collective-permute-start.44) | collective-permute-done | bytes 524320 | tf_op jit(solution)/shard_map/ppermute | solution.py:859
  647.7 6.1 collective-permute-start.48
  656.3 10.0 %collective-permute-done.47 = bf16[256,2048]{1,0:T(8,128)(2,1)S(1)} collective-permute-done((bf16[256,2048]{1,0:T(8,128)(2,1)S(1)}, bf16[256,2048]{1,0:T(8,128)(2,1)S(1)}, u32[]{:S(2)}, u32[]{:S(2)}) %collective-permute-start.47) | collective-permute-done | bytes 1048608 | tf_op jit(solution)/shard_map/ppermute | solution.py:859
  677.4 10.9 %gather_halves.1 = (f32[1024,3072]{1,0:T(8,128)}, f32[1024,1024]{1,0:T(8,128)}) custom-call(s32[1]{0:T(128)} %bitcast.13.place_ref, bf16[512,2048]{1,0:T(8,128)(2,1)} %pad_maximum_fusion.one_own, bf16[512,2048]{1,0:T(8,128)(2,1)} %collective-permute-done.51.one_other, bf16[512,2048]{1,0:T(8,128)(2,1)} %pad_maximum_fusion.1.two_own, ...), custom_call_target="tpu_custom_call" | custom-call | flops 1000 | bytes 1000 | tf_op jit(solution)/shard_map/gather_halves/pallas_call | solution.py:719
  (293 shorter events, 185.8 us)
Async XLA Ops:
  0.7 52.7 %collective-permute-start = (bf16[1024,1024]{1,0:T(8,128)(2,1)}, bf16[1024,1024]{1,0:T(8,128)(2,1)}, u32[]{:S(2)}, u32[]{:S(2)}) collective-permute-start(bf16[1024,1024]{1,0:T(8,128)(2,1)} %cot_a.1), channel_id=1, source_target_pairs={{0,1},{1,0},{2,3},{3,2},{4,5},{5,4},{6,7},{7,6},{8,9},{9,8},{10,11... | collective-permute-start | bytes 6291464 | tf_op jit(solution)/shard_map/ppermute | solution.py:790
  1.2 52.1 %collective-permute-start.1 = (bf16[1024,1024]{1,0:T(8,128)(2,1)}, bf16[1024,1024]{1,0:T(8,128)(2,1)}, u32[]{:S(2)}, u32[]{:S(2)}) collective-permute-start(bf16[1024,1024]{1,0:T(8,128)(2,1)} %cot_a.1), channel_id=1, source_target_pairs={{0,2},{1,3},{2,0},{3,1},{4,6},{5,7},{6,4},{7,5},{8,10},{9,11},{10,... | collective-permute-start | bytes 6291464 | tf_op jit(solution)/shard_map/ppermute | solution.py:795
  10.1 42.4 %collective-permute-start.3 = (s32[6,1024]{1,0:T(8,128)S(1)}, s32[6,1024]{1,0:T(8,128)S(1)}, u32[]{:S(2)}, u32[]{:S(2)}) collective-permute-start(s32[6,1024]{1,0:T(8,128)S(1)} %pad_add_fusion.2), channel_id=1, source_target_pairs={{0,2},{1,3},{2,0},{3,1},{4,6},{5,7},{6,4},{7,5},{8,10},{9,11},{10,... | collective-permute-start | bytes 73736 | tf_op jit(solution)/shard_map/ppermute | solution.py:795
  10.3 42.2 %collective-permute-start.4 = (s32[6,1024]{1,0:T(8,128)S(1)}, s32[6,1024]{1,0:T(8,128)S(1)}, u32[]{:S(2)}, u32[]{:S(2)}) collective-permute-start(s32[6,1024]{1,0:T(8,128)S(1)} %pad_add_fusion.2), channel_id=1, source_target_pairs={{0,3},{1,2},{2,1},{3,0},{4,7},{5,6},{6,5},{7,4},{8,11},{9,10},{10,... | collective-permute-start | bytes 73736 | tf_op jit(solution)/shard_map/ppermute | solution.py:795
  59.4 64.0 %collective-permute-start.6 = (bf16[1024,1024]{1,0:T(8,128)(2,1)S(1)}, bf16[1024,1024]{1,0:T(8,128)(2,1)}, u32[]{:S(2)}, u32[]{:S(2)}) collective-permute-start(bf16[1024,1024]{1,0:T(8,128)(2,1)S(1)} %multiply_convert_fusion.tok_a), channel_id=1, source_target_pairs={{0,2},{1,3},{2,0},{3,1},{4,6},{5,7},{6,4},{7,5},{8,10},{9,11},{10,... | collective-permute-start | bytes 6291464 | tf_op jit(solution)/shard_map/ppermute | solution.py:795
  60.1 63.3 %collective-permute-start.7 = (bf16[1024,1024]{1,0:T(8,128)(2,1)}, bf16[1024,1024]{1,0:T(8,128)(2,1)}, u32[]{:S(2)}, u32[]{:S(2)}) collective-permute-start(bf16[1024,1024]{1,0:T(8,128)(2,1)} %collective-permute-done.1.cot_a), channel_id=1, source_target_pairs={{0,1},{1,0},{2,3},{3,2},{4,5},{5,4},{6,7},{7,6},{8,9},{9,8},{10,11... | collective-permute-start | bytes 6291464 | tf_op jit(solution)/shard_map/ppermute | solution.py:790
  123.7 91.9 %collective-permute-start.11 = (bf16[1024,1024]{1,0:T(8,128)(2,1)}, bf16[1024,1024]{1,0:T(8,128)(2,1)}, u32[]{:S(2)}, u32[]{:S(2)}) collective-permute-start(bf16[1024,1024]{1,0:T(8,128)(2,1)} %get-tuple-element.250), channel_id=1, source_target_pairs={{0,1},{1,0},{2,3},{3,2},{4,5},{5,4},{6,7},{7,6},{8,9},{9,8},{10,11... | collective-permute-start | bytes 6291464 | tf_op jit(solution)/shard_map/ppermute | solution.py:790
  217.9 56.8 %collective-permute-start.13 = (bf16[1024,1024]{1,0:T(8,128)(2,1)}, bf16[1024,1024]{1,0:T(8,128)(2,1)}, u32[]{:S(2)}, u32[]{:S(2)}) collective-permute-start(bf16[1024,1024]{1,0:T(8,128)(2,1)} %add_convert_fusion.5), channel_id=1, source_target_pairs={{0,2},{1,3},{2,0},{3,1},{4,6},{5,7},{6,4},{7,5},{8,10},{9,11},{10,... | collective-permute-start | bytes 6291464 | tf_op jit(solution)/shard_map/ppermute | solution.py:795
  224.4 100.8 %collective-permute-start.15 = (bf16[4,352,1024]{2,1,0:T(8,128)(2,1)}, bf16[4,352,1024]{2,1,0:T(8,128)(2,1)}, u32[]{:S(2)}, u32[]{:S(2)}) collective-permute-start(bf16[4,352,1024]{2,1,0:T(8,128)(2,1)} %get-tuple-element.458), channel_id=1, source_target_pairs={{0,4},{4,0},{8,12},{12,8},{16,20},{20,16},{24,28},{28,24},{1,5},{5... | collective-permute-start | bytes 8650760 | tf_op jit(solution)/shard_map/ppermute | solution.py:834
  225.8 48.9 %collective-permute-start.14 = (f32[8,1024]{1,0:T(8,128)S(1)}, f32[8,1024]{1,0:T(8,128)S(1)}, u32[]{:S(2)}, u32[]{:S(2)}) collective-permute-start(f32[8,1024]{1,0:T(8,128)S(1)} %add.308), channel_id=1, source_target_pairs={{0,2},{1,3},{2,0},{3,1},{4,6},{5,7},{6,4},{7,5},{8,10},{9,11},{10,... | collective-permute-start | bytes 98312 | tf_op jit(solution)/shard_map/ppermute | solution.py:795
  273.9 94.8 %collective-permute-start.16 = (bf16[1024,1024]{1,0:T(8,128)(2,1)}, bf16[1024,1024]{1,0:T(8,128)(2,1)}, u32[]{:S(2)}, u32[]{:S(2)}) collective-permute-start(bf16[1024,1024]{1,0:T(8,128)(2,1)} %get-tuple-element.290), channel_id=1, source_target_pairs={{0,2},{1,3},{2,0},{3,1},{4,6},{5,7},{6,4},{7,5},{8,10},{9,11},{10,... | collective-permute-start | bytes 6291464 | tf_op jit(solution)/shard_map/ppermute | solution.py:795
  274.4 94.3 %collective-permute-start.17 = (bf16[1024,1024]{1,0:T(8,128)(2,1)}, bf16[1024,1024]{1,0:T(8,128)(2,1)}, u32[]{:S(2)}, u32[]{:S(2)}) collective-permute-start(bf16[1024,1024]{1,0:T(8,128)(2,1)} %get-tuple-element.291), channel_id=1, source_target_pairs={{0,3},{1,2},{2,1},{3,0},{4,7},{5,6},{6,5},{7,4},{8,11},{9,10},{10,... | collective-permute-start | bytes 6291464 | tf_op jit(solution)/shard_map/ppermute | solution.py:795
  321.5 47.2 %collective-permute-start.18 = (bf16[1024,1024]{1,0:T(8,128)(2,1)}, bf16[1024,1024]{1,0:T(8,128)(2,1)}, u32[]{:S(2)}, u32[]{:S(2)}) collective-permute-start(bf16[1024,1024]{1,0:T(8,128)(2,1)} %get-tuple-element.292), channel_id=1, source_target_pairs={{0,1},{1,0},{2,3},{3,2},{4,5},{5,4},{6,7},{7,6},{8,9},{9,8},{10,11... | collective-permute-start | bytes 6291464 | tf_op jit(solution)/shard_map/ppermute | solution.py:790
  368.7 64.8 %collective-permute-start.19 = (bf16[4,128,2816]{2,1,0:T(8,128)(2,1)}, bf16[4,128,2816]{2,1,0:T(8,128)(2,1)S(1)}, u32[]{:S(2)}, u32[]{:S(2)}) collective-permute-start(bf16[4,128,2816]{2,1,0:T(8,128)(2,1)} %get-tuple-element.304), channel_id=1, source_target_pairs={{0,4},{4,0},{8,12},{12,8},{16,20},{20,16},{24,28},{28,24},{1,5},{5... | collective-permute-start | bytes 8650760 | tf_op jit(solution)/shard_map/ppermute | solution.py:840
  371.9 54.1 %collective-permute-start.20 = (bf16[352,1024]{1,0:T(8,128)(2,1)}, bf16[352,1024]{1,0:T(8,128)(2,1)}, u32[]{:S(2)}, u32[]{:S(2)}) collective-permute-start(bf16[352,1024]{1,0:T(8,128)(2,1)} %get-tuple-element.473), channel_id=1, source_target_pairs={{0,8},{4,12},{8,16},{12,20},{16,24},{20,28},{24,0},{28,4},{1,9},{5... | collective-permute-start | bytes 2162696 | tf_op jit(solution)/shard_map/ppermute | solution.py:834
  373.5 52.6 %collective-permute-start.21 = (bf16[352,1024]{1,0:T(8,128)(2,1)}, bf16[352,1024]{1,0:T(8,128)(2,1)}, u32[]{:S(2)}, u32[]{:S(2)}) collective-permute-start(bf16[352,1024]{1,0:T(8,128)(2,1)} %get-tuple-element.472), channel_id=1, source_target_pairs={{0,16},{4,20},{8,24},{12,28},{16,0},{20,4},{24,8},{28,12},{1,17},{... | collective-permute-start | bytes 2162696 | tf_op jit(solution)/shard_map/ppermute | solution.py:834
  376.0 50.0 %collective-permute-start.22 = (bf16[352,1024]{1,0:T(8,128)(2,1)}, bf16[352,1024]{1,0:T(8,128)(2,1)}, u32[]{:S(2)}, u32[]{:S(2)}) collective-permute-start(bf16[352,1024]{1,0:T(8,128)(2,1)} %get-tuple-element.471), channel_id=1, source_target_pairs={{0,24},{4,28},{8,0},{12,4},{16,8},{20,12},{24,16},{28,20},{1,25},{... | collective-permute-start | bytes 2162696 | tf_op jit(solution)/shard_map/ppermute | solution.py:834
  434.2 72.1 %collective-permute-start.26 = (bf16[4,128,2816]{2,1,0:T(8,128)(2,1)}, bf16[4,128,2816]{2,1,0:T(8,128)(2,1)}, u32[]{:S(2)}, u32[]{:S(2)}) collective-permute-start(bf16[4,128,2816]{2,1,0:T(8,128)(2,1)} %get-tuple-element.322), channel_id=1, source_target_pairs={{0,4},{4,0},{8,12},{12,8},{16,20},{20,16},{24,28},{28,24},{1,5},{5... | collective-permute-start | bytes 8650760 | tf_op jit(solution)/shard_map/ppermute | solution.py:840
  436.3 70.0 %collective-permute-start.23 = (bf16[128,2816]{1,0:T(8,128)(2,1)}, bf16[128,2816]{1,0:T(8,128)(2,1)S(1)}, u32[]{:S(2)}, u32[]{:S(2)}) collective-permute-start(bf16[128,2816]{1,0:T(8,128)(2,1)} %get-tuple-element.469), channel_id=1, source_target_pairs={{0,8},{4,12},{8,16},{12,20},{16,24},{20,28},{24,0},{28,4},{1,9},{5... | collective-permute-start | bytes 2162696 | tf_op jit(solution)/shard_map/ppermute | solution.py:834
  442.4 63.9 %collective-permute-start.24 = (bf16[128,2816]{1,0:T(8,128)(2,1)}, bf16[128,2816]{1,0:T(8,128)(2,1)S(1)}, u32[]{:S(2)}, u32[]{:S(2)}) collective-permute-start(bf16[128,2816]{1,0:T(8,128)(2,1)} %get-tuple-element.468), channel_id=1, source_target_pairs={{0,16},{4,20},{8,24},{12,28},{16,0},{20,4},{24,8},{28,12},{1,17},{... | collective-permute-start | bytes 2162696 | tf_op jit(solution)/shard_map/ppermute | solution.py:834
  444.0 62.3 %collective-permute-start.25 = (bf16[128,2816]{1,0:T(8,128)(2,1)S(1)}, bf16[128,2816]{1,0:T(8,128)(2,1)S(1)}, u32[]{:S(2)}, u32[]{:S(2)}) collective-permute-start(bf16[128,2816]{1,0:T(8,128)(2,1)S(1)} %get-tuple-element.467), channel_id=1, source_target_pairs={{0,24},{4,28},{8,0},{12,4},{16,8},{20,12},{24,16},{28,20},{1,25},{... | collective-permute-start | bytes 2162696 | tf_op jit(solution)/shard_map/ppermute | solution.py:834
  516.1 48.6 %collective-permute-start.32 = (bf16[128,2816]{1,0:T(8,128)(2,1)}, bf16[128,2816]{1,0:T(8,128)(2,1)}, u32[]{:S(2)}, u32[]{:S(2)}) collective-permute-start(bf16[128,2816]{1,0:T(8,128)(2,1)} %get-tuple-element.465), channel_id=1, source_target_pairs={{0,8},{4,12},{8,16},{12,20},{16,24},{20,28},{24,0},{28,4},{1,9},{5... | collective-permute-start | bytes 2162696 | tf_op jit(solution)/shard_map/ppermute | solution.py:834
  517.3 50.4 %collective-permute-start.33 = (bf16[128,2816]{1,0:T(8,128)(2,1)}, bf16[128,2816]{1,0:T(8,128)(2,1)}, u32[]{:S(2)}, u32[]{:S(2)}) collective-permute-start(bf16[128,2816]{1,0:T(8,128)(2,1)} %get-tuple-element.464), channel_id=1, source_target_pairs={{0,16},{4,20},{8,24},{12,28},{16,0},{20,4},{24,8},{28,12},{1,17},{... | collective-permute-start | bytes 2162696 | tf_op jit(solution)/shard_map/ppermute | solution.py:834
  518.7 49.0 %collective-permute-start.34 = (bf16[128,2816]{1,0:T(8,128)(2,1)}, bf16[128,2816]{1,0:T(8,128)(2,1)}, u32[]{:S(2)}, u32[]{:S(2)}) collective-permute-start(bf16[128,2816]{1,0:T(8,128)(2,1)} %get-tuple-element.463), channel_id=1, source_target_pairs={{0,24},{4,28},{8,0},{12,4},{16,8},{20,12},{24,16},{28,20},{1,25},{... | collective-permute-start | bytes 2162696 | tf_op jit(solution)/shard_map/ppermute | solution.py:834
  (73 other events, 910.0 us)
